TPU v7x, 32 devices: a whole 2x2x4 slice. The times are simulated.
32 devices in a mesh: row: 4 (over x, core), col: 8 (over z, y).
Axes of the slice: x: 2, y: 2, z: 4, core: 2. Of those that a mesh axis runs over, the one named last changes fastest.
Arguments:
- tokens: bfloat16 [24576, 768], P(('row', 'col')), may hold values from -6 to 6
- w_qkv: bfloat16 [3, 768, 768], replicated, may hold values from -0.21875 to 0.21875
- w_attn_out: bfloat16 [768, 768], replicated, may hold values from -0.875 to 0.875
- w_in: bfloat16 [768, 3072], replicated, may hold values from -0.21875 to 0.21875
- w_out: bfloat16 [3072, 768], replicated, may hold values from -0.109375 to 0.109375
- vectors: float32 [9216], replicated
- out_grad: bfloat16 [24576, 768], P(('row', 'col')), may hold values from -6 to 6
- span_count: int32 [32], replicated, may hold values from 1 to 6, as said below
- pair_index: int32 [192], replicated, may hold values from 0 to 191, as said below
- owner_list: int32 [48], replicated, may hold values from 0 to 47, each once
- master: float32 [48, 768, 192], P('col'), may hold values from -0.21875 to 0.21875
- first_moment: float32 [48, 768, 192], P('col'), may hold values from -56 to 56
- second_moment: float32 [48, 768, 192], P('col'), may hold values from 6.144 to 24.576
- left_basis: float32 [48, 768, 768], P('col'), as said below
- right_basis: float32 [48, 192, 192], P('col'), as said below
- vec_first: float32 [9216], replicated, may hold values from -112 to 112
- vec_second: float32 [9216], replicated, may hold values from 24.576 to 98.304
Outputs:
- encoded: bfloat16 [24576, 768], P(('row', 'col'))
- input_grad: float32 [24576, 768], P(('row', 'col'))
- loss: float32 [], replicated
- new_master: float32 [48, 768, 192], P('col')
- new_first: float32 [48, 768, 192], P('col')
- new_second: float32 [48, 768, 192], P('col')
- master_copy: bfloat16 [48, 768, 192], P('col')
- vec_new: float32 [9216], replicated
- vec_first_new: float32 [9216], replicated
- vec_second_new: float32 [9216], replicated
Inputs may be any that keep to these rules, and one draw needn't show every extreme that they name: `span_count`: the live spans of a device fill its first slots; the last device has 6 live spans. pair_index[i] = i for padding slots and for live spans without a partner; otherwise j = pair_index[i] is another live span, on any device, with pair_index[j] = i. `owner_list`: each block number once. `left_basis`: each [s] is orthogonal: the columns are orthonormal DCT-II basis vectors, permuted and signed. `right_basis`: each [s] is orthogonal: the columns are orthonormal DCT-II basis vectors, permuted and signed.
All inputs are finite; a program needn't handle non-finite values.
Results may differ from a plain program's by a relative error of at most 0.01.
Values may be sent and summed in bfloat16 or wider, within the bound.
No kernel may reach another device: no remote copies, remote signals or barrier semaphores. Data moves between devices by JAX's collectives and lax.ppermute only.
A program may use at most 192 MiB of HBM per device.

v0:
```python
from functools import partial

import jax
import jax.numpy as jnp
from jax import lax
from jax.experimental import pallas as pl
from jax.experimental.pallas import tpu as pltpu
from jax.sharding import PartitionSpec as P

D = 768
HEADS = 12
HEAD = 64
FF = 3072
SPAN = 128
STEP = 10
GROUP = 8

RATE = 0.01
DECAY = 0.01
VECTOR_RATE = 0.3

LOW = jnp.bfloat16
F32 = jnp.float32
TALL = 2 * SPAN


def dot(left_side, right_side, contract=(1, 0)):
    dims = (((contract[0],), (contract[1],)), ((), ()))
    return lax.dot_general(left_side, right_side, dims, preferred_element_type=F32)


def whole(shape):
    return pl.BlockSpec(shape, lambda *ids: (0,) * len(shape))


def cost(microseconds, transcendentals=0):
    return pl.CostEstimate(
        flops=int(microseconds * 1.1e9), bytes_accessed=0, transcendentals=transcendentals
    )


def params(mebibytes=36):
    return pltpu.CompilerParams(vmem_limit_bytes=mebibytes * 1024 * 1024)


def row_of(rows, index):
    return rows[:, index * D : (index + 1) * D]


def live_rows(place, counts, first_row, height):
    at = first_row + lax.broadcasted_iota(jnp.int32, (height, 1), 0)
    return jnp.where(at < counts[place[0]] * SPAN, 1.0, 0.0)


near = pltpu.VMEM
far = pltpu.HBM


def streamed(*arrays):
    return [pltpu.with_memory_space_constraint(a, pltpu.HBM) for a in arrays]


ANY = pl.BlockSpec(memory_space=pl.ANY)
SMEM = pl.BlockSpec(memory_space=pltpu.SMEM)


def split_heads(pair):
    lane = lax.broadcasted_iota(jnp.int32, pair.shape, 1)
    zero = jnp.zeros_like(pair)
    return jnp.concatenate([jnp.where(lane < HEAD, pair, zero), jnp.where(lane < HEAD, zero, pair)])


def normalise(scores):
    peak = jnp.max(scores, axis=-1, keepdims=True)
    raised = jnp.exp(scores - peak)
    return raised * (1.0 / jnp.sum(raised, axis=-1, keepdims=True))


def attend_kernel(tokens, w_qkv, rows, q_out, k_out, v_out, p_out, a_out):
    block = tokens[...]
    scaling = HEAD ** (-0.5)
    q_out[...] = ((dot(block, w_qkv[0]) + row_of(rows, 4)).astype(LOW) * scaling).astype(LOW)
    k_out[...] = dot(block, w_qkv[1]).astype(LOW)
    v_out[...] = (dot(block, w_qkv[2]) + row_of(rows, 5)).astype(LOW)
    for span in range(TALL // SPAN):
        at = slice(span * SPAN, (span + 1) * SPAN)
        for pair in range(HEADS // 2):
            lanes = slice(pair * 2 * HEAD, (pair + 1) * 2 * HEAD)
            scores = dot(q_out[at, lanes], split_heads(k_out[at, lanes]), (1, 1))
            weights = jnp.concatenate(
                [normalise(scores[:, :SPAN]), normalise(scores[:, SPAN:])], axis=1
            ).astype(LOW)
            p_out[span, pair] = weights
            a_out[at, lanes] = dot(weights, split_heads(v_out[at, lanes])).astype(LOW)


def attend(tokens, w_qkv, rows):
    total = tokens.shape[0]
    tall = pl.BlockSpec((TALL, D), lambda i: (i, 0))
    like = far((total, D), LOW)
    tokens, w_qkv, rows = streamed(tokens, w_qkv, rows)
    spans = TALL // SPAN
    return pl.pallas_call(
        attend_kernel,
        grid=(total // TALL,),
        in_specs=[tall, whole(w_qkv.shape), whole(rows.shape)],
        out_specs=[
            tall,
            tall,
            tall,
            pl.BlockSpec((spans, HEADS // 2, SPAN, 2 * SPAN), lambda i: (i, 0, 0, 0)),
            tall,
        ],
        out_shape=[
            like,
            like,
            like,
            far((total // SPAN, HEADS // 2, SPAN, 2 * SPAN), LOW),
            near((total, D), LOW),
        ],
        compiler_params=params(),
        cost_estimate=cost(10),
        name="attend",
    )(tokens, w_qkv, rows)


def unit_norm(resid):
    centred = resid - jnp.mean(resid, axis=-1, keepdims=True)
    inverse = lax.rsqrt(jnp.mean(centred * centred, axis=-1, keepdims=True) + 1e-06)
    return centred * inverse, inverse


def gelu_pair(x):
    cdf = 0.5 + 0.5 * lax.erf(x * 0.7071067811865476)
    return x * cdf, cdf + x * jnp.exp(-0.5 * x * x) * 0.3989422804014327


def feed_kernel(
    place, counts, tokens, attended, w_attn, w_in, w_out, rows, bias,
    enc_out, hid_out, slope_out, norm_out, u1_out, i1_out, u2_out, i2_out, total,
):
    band = pl.program_id(0)
    chunks = [slice(at, at + TALL) for at in range(0, tokens.shape[0], TALL)]

    @pl.when(band == 0)
    def _():
        for at in chunks:
            resid = tokens[at].astype(F32) + dot(attended[at], w_attn[...]) + row_of(rows, 6)
            unit_one, inverse_one = unit_norm(resid)
            value = unit_one * row_of(rows, 0) + row_of(rows, 2)
            u1_out[at] = unit_one.astype(LOW)
            i1_out[at] = inverse_one
            norm_out[at] = value.astype(LOW)
            total[at] = value + row_of(rows, 7)

    step = 256
    for at in range(0, hid_out.shape[1], step):
        here = slice(at, at + step)
        pre_act = dot(norm_out[...], w_in[:, here]) + bias[:, here]
        hidden, slope = gelu_pair(pre_act)
        hid_out[:, here] = hidden.astype(LOW)
        slope_out[:, here] = slope.astype(LOW)

    @pl.when(band < pl.num_programs(0) - 1)
    def _():
        total[...] += dot(hid_out[...], w_out[...])

    @pl.when(band == pl.num_programs(0) - 1)
    def _():
        for at in chunks:
            resid = total[at] + dot(hid_out[at], w_out[...])
            unit_two, inverse_two = unit_norm(resid)
            u2_out[at] = unit_two.astype(LOW)
            i2_out[at] = inverse_two
            live = live_rows(place, counts, at.start, TALL)
            value = live * (unit_two * row_of(rows, 1) + row_of(rows, 3))
            enc_out[at] = value.astype(LOW)


def feed(place, counts, tokens, attended, w_attn, w_in, w_out, rows):
    total = tokens.shape[0]
    tall = lambda width: pl.BlockSpec((total, width), lambda j: (0, 0))
    band = lambda height: pl.BlockSpec((height, D), lambda j: (0, j))
    tokens, w_attn, w_in, w_out, rows = streamed(tokens, w_attn, w_in, w_out, rows)
    return pl.pallas_call(
        feed_kernel,
        grid=(FF // D,),
        in_specs=[
            SMEM, SMEM, tall(D), tall(D), whole(w_attn.shape), band(D),
            pl.BlockSpec((D, D), lambda j: (j, 0)),
            pl.BlockSpec((1, 8 * D), lambda j: (0, 0)),
            pl.BlockSpec((1, D), lambda j: (0, 8 + j)),
        ],
        out_specs=[
            tall(D), band(total), band(total), tall(D), tall(D), tall(1), tall(D), tall(1),
        ],
        out_shape=[
            jax.ShapeDtypeStruct((total, D), LOW),
            far((total, FF), LOW),
            far((total, FF), LOW),
            far((total, D), LOW),
            far((total, D), LOW),
            far((total, 1), F32),
            near((total, D), LOW),
            near((total, 1), F32),
        ],
        scratch_shapes=[pltpu.VMEM((total, D), F32)],
        compiler_params=params(),
        cost_estimate=cost(20),
        name="feed",
    )(place, counts, tokens, attended, w_attn, w_in, w_out, rows, rows)


def norm_back(grad_out, unit_rows, inverse, gain):
    scaled = grad_out * gain
    along = jnp.mean(scaled * unit_rows, axis=-1, keepdims=True)
    return inverse * (scaled - jnp.mean(scaled, axis=-1, keepdims=True) - unit_rows * along)


def column_sums(*arrays):
    return [jnp.sum(a, axis=0, keepdims=True) for a in arrays]


def outer_kernel(place, counts, out_grad, grad_cls, unit_two, inverse_two, rows, two_out, low_out, vec_out):
    spot = lax.broadcasted_iota(jnp.int32, (SPAN, 1), 0) == 0
    sums = None
    for span in range(out_grad.shape[0] // SPAN):
        at = slice(span * SPAN, (span + 1) * SPAN)
        added = jnp.where(spot, grad_cls[span : span + 1], 0.0)
        live = live_rows(place, counts, span * SPAN, SPAN)
        grad_y = live * (out_grad[at].astype(F32) + added)
        unit_rows = unit_two[at].astype(F32)
        grad_two = norm_back(grad_y, unit_rows, inverse_two[at], row_of(rows, 1))
        two_out[at] = grad_two
        low_out[at] = grad_two.astype(LOW)
        here = column_sums(grad_y * unit_rows, grad_y, grad_two)
        sums = here if sums is None else [a + b for a, b in zip(sums, here)]
    for index, total in enumerate(sums):
        vec_out[index : index + 1] = total


def outer_grad(place, counts, out_grad, grad_cls, unit_two, inverse_two, rows):
    total = out_grad.shape[0]
    return pl.pallas_call(
        outer_kernel,
        in_specs=[SMEM, SMEM] + [pl.BlockSpec(memory_space=pltpu.VMEM)] * 5,
        out_shape=[
            jax.ShapeDtypeStruct((total, D), F32),
            jax.ShapeDtypeStruct((total, D), LOW),
            jax.ShapeDtypeStruct((3, D), F32),
        ],
        compiler_params=params(),
        cost_estimate=cost(5),
        name="outer",
    )(place, counts, out_grad, grad_cls, unit_two, inverse_two, rows)


def weight_kernel(panels, after, side, *refs):
    *sides, out = refs[after:]

    @pl.when(pl.program_id(0) < panels)
    def _():
        out[0] = dot(sides[0][...], sides[1][...], (0, 0)).astype(LOW)

    if len(sides) > 2:

        @pl.when(pl.program_id(0) == panels)
        def _():
            out[0] = dot(sides[2][...], sides[3][...], (0, 0)).astype(LOW)


def weight_half(hint, after, side, left_side, right_side, panels, banded, extra=()):
    total = left_side.shape[0]
    half = D // 2
    every = panels + len(extra) // 2
    tall = lambda width, at: pl.BlockSpec((total, width), at)
    last = lambda panel: jnp.minimum(panel, panels - 1)
    left_at = lambda panel, side: (0, last(panel) * 2 + side[0] if banded else side[0])
    right_at = lambda panel, side: (0, 0 if banded else last(panel))
    more = [tall(half, lambda p, s: (0, s[0])), tall(D, lambda p, s: (0, 0))]
    return pl.pallas_call(
        partial(weight_kernel, panels, len(after)),
        grid_spec=pltpu.PrefetchScalarGridSpec(
            num_scalar_prefetch=1,
            grid=(every,),
            in_specs=[ANY] * len(after)
            + [tall(half, left_at), tall(D, right_at)]
            + more[: len(extra)],
            out_specs=pl.BlockSpec((1, half, D), lambda p, s: (p, 0, 0)),
        ),
        out_shape=jax.ShapeDtypeStruct((every, half, D), LOW),
        compiler_params=params(),
        cost_estimate=cost(hint),
        name="weight",
    )(side.reshape(1), *after, left_side, right_side, *extra)


def inner_kernel(after, *refs):
    low, grad_two, slope, unit_one, inverse_one, w_attn, w_in, w_out, rows = refs[after:-6]
    pre_out, one_out, mixed_out, ga_out, vec_out, total = refs[-6:]
    band = pl.program_id(0)
    last = pl.num_programs(0) - 1
    step = 256
    for at in range(0, D, step):
        here = slice(at, at + step)
        grad_pre = dot(low[...], w_out[here], (1, 1)) * slope[:, here].astype(F32)
        pre_out[:, here] = grad_pre.astype(LOW)
        vec_out[pl.ds(3 + band, 1), here] = jnp.sum(grad_pre, axis=0, keepdims=True)

    @pl.when(band == 0)
    def _():
        total[...] = grad_two[...] + dot(pre_out[...], w_in[...], (1, 1))

    @pl.when((band > 0) & (band < last))
    def _():
        total[...] += dot(pre_out[...], w_in[...], (1, 1))

    @pl.when(band == last)
    def _():
        sums = None
        for first in range(0, low.shape[0], TALL):
            at = slice(first, first + TALL)
            grad_normed = total[at] + dot(pre_out[at], w_in[...], (1, 1))
            unit_rows = unit_one[at].astype(F32)
            grad_one = norm_back(grad_normed, unit_rows, inverse_one[at], row_of(rows, 0))
            one_out[at] = grad_one
            mixed = grad_one.astype(LOW)
            mixed_out[at] = mixed
            ga_out[at] = dot(mixed, w_attn[...], (1, 1)).astype(LOW)
            here = column_sums(grad_normed * unit_rows, grad_normed, grad_one)
            sums = here if sums is None else [a + b for a, b in zip(sums, here)]
        for index, value in enumerate(sums):
            vec_out[index : index + 1] = value


def inner_grad(after, low, grad_two, slope, unit_one, inverse_one, w_attn, w_in, w_out, rows):
    total = low.shape[0]
    bands = FF // D
    slope, w_attn, w_in, w_out, rows = streamed(slope, w_attn, w_in, w_out, rows)
    band = lambda height: pl.BlockSpec((height, D), lambda j: (0, j))
    return pl.pallas_call(
        partial(inner_kernel, len(after)),
        grid=(bands,),
        in_specs=[ANY] * len(after)
        + [
            whole(low.shape), whole(grad_two.shape), band(total), whole(unit_one.shape),
            whole(inverse_one.shape), whole(w_attn.shape), band(D),
            pl.BlockSpec((D, D), lambda j: (j, 0)), whole(rows.shape),
        ],
        out_specs=[band(total)] + [whole((total, D))] * 3 + [whole((3 + bands, D))],
        out_shape=[
            near((total, FF), LOW),
            far((total, D), F32),
            near((total, D), LOW),
            near((total, D), LOW),
            jax.ShapeDtypeStruct((3 + bands, D), F32),
        ],
        scratch_shapes=[pltpu.VMEM((total, D), F32)],
        compiler_params=params(),
        cost_estimate=cost(16),
        name="inner",
    )(*after, low, grad_two, slope, unit_one, inverse_one, w_attn, w_in, w_out, rows)


def unattend_kernel(*refs):
    q, k, v, p, ga, stack_out, vec_out = refs[-7:]
    scaling = HEAD ** (-0.5)
    first = pl.program_id(0) == 0

    @pl.when(first)
    def _():
        vec_out[...] = jnp.zeros_like(vec_out)

    for span in range(p.shape[0]):
        at = slice(span * SPAN, (span + 1) * SPAN)
        for pair in range(HEADS // 2):
            lo = pair * 2 * HEAD
            lanes = slice(lo, lo + 2 * HEAD)
            weights = p[span, pair]
            grad = ga[at, lanes]
            spread_out = dot(grad, split_heads(v[at, lanes]), (1, 1))
            wide = weights.astype(F32)
            parts = []
            for half in range(2):
                cols = slice(half * SPAN, (half + 1) * SPAN)
                wgt, gw = wide[:, cols], spread_out[:, cols]
                parts.append((wgt * (gw - jnp.sum(gw * wgt, axis=-1, keepdims=True))).astype(LOW))
            grad_scores = jnp.concatenate(parts, axis=1)
            grad_q = dot(grad_scores, split_heads(k[at, lanes])) * scaling
            tall_scores = jnp.concatenate(parts, axis=0)
            tall_weights = jnp.concatenate([weights[:, :SPAN], weights[:, SPAN:]], axis=0)
            grad_k = dot(tall_scores, split_heads(q[at, lanes]), (0, 0))
            grad_v = dot(tall_weights, split_heads(grad), (0, 0))
            stack_out[at, lo : lo + 2 * HEAD] = grad_q.astype(LOW)
            stack_out[at, D + lo : D + lo + 2 * HEAD] = grad_k.astype(LOW)
            stack_out[at, 2 * D + lo : 2 * D + lo + 2 * HEAD] = grad_v.astype(LOW)
            vec_out[0:1, lanes] += jnp.sum(grad_q, axis=0, keepdims=True)
            vec_out[1:2, lanes] += jnp.sum(grad_v, axis=0, keepdims=True)


def unattend(after, part, parts, q, k, v, p, ga, stack=None):
    total = q.shape[0]
    count = total // SPAN // parts
    first = part * count
    tall = lambda width: pl.BlockSpec((SPAN, width), lambda i: (first + i, 0))
    after = after if stack is None else [stack] + after
    return pl.pallas_call(
        unattend_kernel,
        grid=(count,),
        in_specs=[ANY] * len(after)
        + [tall(D)] * 3
        + [
            pl.BlockSpec((1, HEADS // 2, SPAN, 2 * SPAN), lambda i: (first + i, 0, 0, 0)),
            tall(D),
        ],
        out_specs=[tall(3 * D), whole((2, D))],
        out_shape=[
far((total, 3 * D), LOW),
            jax.ShapeDtypeStruct((2, D), F32),
        ],
        input_output_aliases={} if stack is None else {0: 0},
        compiler_params=params(),
        cost_estimate=cost(8),
        name="unattend",
    )(*after, q, k, v, p, ga)


def input_kernel(*refs):
    grad_one, stack, w_qkv, out = refs[-4:]
    total = grad_one[...]
    for index in range(3):
        total += dot(stack[:, index * D : (index + 1) * D], w_qkv[index], (1, 1))
    out[...] = total


def input_grad(after, grad_one, stack, w_qkv):
    total = grad_one.shape[0]
    tall = lambda width: pl.BlockSpec((TALL, width), lambda i: (i, 0))
    return pl.pallas_call(
        input_kernel,
        grid=(total // TALL,),
        in_specs=[ANY] * len(after) + [tall(D), tall(3 * D), whole(w_qkv.shape)],
        out_specs=tall(D),
        out_shape=jax.ShapeDtypeStruct((total, D), F32),
        compiler_params=params(),
        cost_estimate=cost(8),
        name="input",
    )(*after, grad_one, stack, w_qkv)


def contrast_kernel(slots, place, rows, counts, partners, loss_out, grad_out):
    total, scale = rows.shape[0], 2.0 * D ** (-0.5)

    def number(shape, axis):
        at = lax.broadcasted_iota(jnp.int32, shape, axis)
        return (at // GROUP) ^ place[0], at % GROUP

    device, slot = number((counts.shape[1], total), 1)
    hit = lax.broadcasted_iota(jnp.int32, device.shape, 0) == device
    count = dot(counts[...].astype(LOW), jnp.where(hit, 1.0, 0.0).astype(LOW))
    live_across = (slot[:1].astype(F32) < count) & (slot[:1] < slots)
    device, slot = number((total, counts.shape[1]), 0)
    hit = lax.broadcasted_iota(jnp.int32, device.shape, 1) == device
    count = jnp.sum(jnp.where(hit, counts[...], 0.0), axis=1, keepdims=True)
    live_down = (slot[:, :1].astype(F32) < count) & (slot[:, :1] < slots)
    device, slot = number((total, partners.shape[1]), 0)
    own_id = device * slots + slot
    hit = lax.broadcasted_iota(jnp.int32, own_id.shape, 1) == own_id
    pair = jnp.sum(jnp.where(hit, partners[...], 0.0), axis=1, keepdims=True)
    device, slot = number((total, total), 0)
    down = (device * slots + slot).astype(F32)
    device, slot = number((total, total), 1)
    across = (device * slots + slot).astype(F32)
    valid = live_across & (down != across)
    matched = jnp.where((slot < slots) & (pair == across), 1.0, 0.0)
    anchor = jnp.where(live_down & (pair != down[:, :1]), 1.0, 0.0)
    similar = dot(rows[...], rows[...], (1, 1)) * scale
    masked = jnp.where(valid, similar, -1e30)
    peak = jnp.max(masked, axis=1, keepdims=True)
    summed = jnp.sum(jnp.where(valid, jnp.exp(masked - peak), 0.0), axis=1, keepdims=True)
    log_total = jnp.log(summed) + peak
    positive = jnp.sum(matched * similar, axis=1, keepdims=True)
    loss_out[...] = jnp.sum(anchor * (log_total - positive), axis=0, keepdims=True)
    grad = (anchor * (jnp.where(valid, jnp.exp(masked - log_total), 0.0) - matched)).astype(LOW)
    own = lax.broadcasted_iota(jnp.int32, (GROUP, total), 0)
    own = jnp.where(own == lax.broadcasted_iota(jnp.int32, (GROUP, total), 1), 1.0, 0.0)
    down_part = dot(dot(own.astype(LOW), grad, (1, 1)).astype(LOW), rows[...])
    grad_out[...] = (dot(grad[: 2 * GROUP], rows[...])[:GROUP] + down_part) * scale


def contrast(cls_rows, span_count, pair_index, device, slots):
    total = cls_rows.shape[0]
    return pl.pallas_call(
        partial(contrast_kernel, slots),
        in_specs=[pl.BlockSpec(memory_space=pltpu.SMEM)]
        + [pl.BlockSpec(memory_space=pltpu.VMEM)] * 3,
        out_shape=[
            jax.ShapeDtypeStruct((1, 1), F32),
            jax.ShapeDtypeStruct((GROUP, D), F32),
        ],
        compiler_params=params(),
        cost_estimate=cost(3),
        name="contrast",
    )(
        device,
        cls_rows,
        span_count.astype(F32).reshape(1, -1),
        pair_index.astype(F32).reshape(1, -1),
    )


def adam_kernel(
    packed, position, gathered, master, first, second, left, right,
    master_out, first_out, second_out, low_out, *scratch,
):
    quarter = D // 4
    slot = pl.program_id(0)
    if packed:
        owned = scratch[0]
        shares, tall, _ = gathered.shape
        rows = D // shares

        @pl.when(slot == 0)
        def _():
            def place(share, carry):
                block = gathered[share].astype(F32)
                at = pl.multiple_of((share ^ position[0]) * rows, rows)
                for index in range(owned.shape[0]):
                    lo = index * rows % tall
                    side = index * rows // tall
                    piece = block[lo : lo + rows, side * quarter : (side + 1) * quarter]
                    owned[index, pl.ds(at, rows), :] = piece
                return carry

            lax.fori_loop(0, shares, place, 0)

        gradient = owned[slot].astype(LOW)
    else:
        gradient = gathered[0]
    low_left, low_right = left[0], right[0].astype(LOW)
    turned = dot(gradient, low_left, (0, 0))
    turned = dot(low_right, turned.astype(LOW), (0, 0))
    new_first = 0.9 * first[0] + 0.1 * turned
    new_second = 0.999 * second[0] + 0.001 * turned * turned
    first_out[0] = new_first
    second_out[0] = new_second
    spread_by = jnp.sqrt(new_second * (1.0 / (1.0 - 0.999**STEP))) + 1e-08
    update = new_first * (1.0 / (1.0 - 0.9**STEP)) / spread_by
    update = dot(update.astype(LOW), low_left, (1, 1))
    update = dot(low_right, update.astype(LOW))
    new_master = master[0] - RATE * (update + DECAY * master[0])
    master_out[0] = new_master
    low_out[0] = new_master.astype(LOW)


def ready_kernel(*refs):
    source, out = refs[-2:]
    out[...] = source[...].astype(out.dtype)


def ready(after, array, kind):
    block = pl.BlockSpec((1,) + array.shape[1:], lambda s: (s, 0, 0))
    return pl.pallas_call(
        ready_kernel,
        grid=(array.shape[0],),
        in_specs=[ANY] * len(after) + [block],
        out_specs=block,
        out_shape=far(array.shape, kind),
        compiler_params=params(16),
        cost_estimate=cost(4),
        name="ready",
    )(*after, *streamed(array))


def to_owned(gathered, position, per_owner):
    quarter = D // 4
    gathered = jnp.take(gathered, jnp.arange(gathered.shape[0]) ^ position, axis=0)
    flat = jnp.concatenate([gathered[..., :quarter], gathered[..., quarter:]], axis=1)
    rows = flat.shape[1] // per_owner
    flat = flat.reshape(flat.shape[0], per_owner, rows, quarter).transpose(1, 0, 2, 3)
    return flat.reshape(per_owner, D, quarter)


def turn(array):
    return array.transpose(0, 2, 1)


def rotated_adam(position, gathered, master, first_moment, second_moment, left_basis, right_basis):
    per_owner, quarter, _ = master.shape
    rows = D // gathered.shape[0]
    packed = rows % 8 == 0 and per_owner % 2 == 0
    if not packed:
        gathered = to_owned(gathered, position, per_owner)
    block = lambda a: pl.BlockSpec((1,) + a.shape[1:], lambda s, p: (s, 0, 0))
    operands = streamed(master, first_moment, second_moment, left_basis, right_basis)
    like = jax.ShapeDtypeStruct(operands[0].shape, F32)
    fixed = pl.BlockSpec(gathered.shape, lambda s, p: (0, 0, 0))
    outputs = pl.pallas_call(
        partial(adam_kernel, packed),
        grid_spec=pltpu.PrefetchScalarGridSpec(
            num_scalar_prefetch=1,
            grid=(per_owner,),
            in_specs=[fixed if packed else block(gathered)] + [block(a) for a in operands],
            out_specs=[block(operands[0])] * 4,
            scratch_shapes=[pltpu.VMEM((per_owner, D, quarter), F32)] if packed else [],
        ),
        out_shape=[like, like, like, jax.ShapeDtypeStruct(like.shape, LOW)],
        compiler_params=params(28),
        cost_estimate=cost(20),
        name="adam",
    )(position.reshape(1), gathered, *operands)
    return [turn(a) for a in outputs]


def axis_bits(name):
    size = lax.axis_size(name)
    return [(name, 1 << k) for k in range(size.bit_length() - 1)]


def bit_of(step):
    return jnp.where((lax.axis_index(step[0]) & step[1]) != 0, 1, 0)


def swap(send, step):
    size = lax.axis_size(step[0])
    return lax.ppermute(send, step[0], [(i, i ^ step[1]) for i in range(size)])


def pick(array, index, dim):
    return lax.dynamic_index_in_dim(array, index, dim, False)


def gather_all(rows):
    for step in axis_bits("col") + axis_bits("row"):
        rows = jnp.concatenate([rows, swap(rows, step)])
    return rows


def row_steps():
    row_bits, col_bits = axis_bits("row"), axis_bits("col")
    core, across = row_bits[:1], row_bits[1:][::-1]
    y_bits, z_bits = col_bits[:-2][::-1], col_bits[-2:]
    return core, across, y_bits, z_bits


def launch(part, step, left, rider=None):
    dim = 1 + left.index(step)
    bit = bit_of(step)
    left.remove(step)
    send, keep = pick(part, 1 - bit, dim), pick(part, bit, dim)
    shape, flat = send.shape, send.reshape(-1, send.shape[-1])
    message = flat
    if rider is not None:
        message = jnp.concatenate([flat, rider.astype(LOW).reshape(-1, flat.shape[1])])
    other = swap(message, step)
    arrived = other[: flat.shape[0]].reshape(shape)
    if rider is not None:
        rider = rider + other[flat.shape[0] :].reshape(rider.shape).astype(F32)
    return message, partial(landed, keep, arrived), rider


def landed(keep, other, tied=None):
    total = keep.astype(F32) + other.astype(F32)
    if tied is not None:
        total += 0.0 * tied[(0,) * tied.ndim].astype(F32)
    return total.astype(LOW)


def begin_sum(send):
    return swap(send, row_steps()[0][0])


class Reduction:
    def __init__(self, other, keep, rider=None):
        core, across, y_bits, z_bits = row_steps()
        left = across + y_bits + z_bits
        part = landed(keep, other)
        self.rider = rider if rider is None else rider + swap(rider, core[0])
        width = part.shape[1] >> len(left)
        part = part.reshape(part.shape[:1] + (2,) * len(left) + (width, D))
        self.steps = list(zip(across + y_bits, y_bits + across)) + [(step,) for step in z_bits]
        self.parts = [part[..., : D // 2], part[..., D // 2 :]]
        self.left = [list(left), list(left)]
        self.start()

    def start(self):
        if not self.steps:
            self.moves = None
            return
        steps = self.steps.pop(0)
        if len(steps) < len(self.parts):
            self.parts, self.left = [jnp.concatenate(self.parts, axis=-1)], self.left[:1]
        self.moves = []
        for side, step in enumerate(steps):
            rider = self.rider if side == 0 else None
            self.moves.append(launch(self.parts[side], step, self.left[side], rider))

    def sent(self):
        return [move[0] for move in self.moves or ()]

    def land(self, tied=None):
        self.parts = [land(tied) for _, land, _ in self.moves]
        self.rider = self.moves[0][2]
        self.start()

    def finish(self):
        while self.moves:
            self.land()
        return self.parts[0]


def slots_kernel(cols, after, owners, *refs):
    parts, out, blocks, packed = refs[after:-3], refs[-3], refs[-2], refs[-1]
    quarter = D // 4
    at = 0
    for part in parts:
        for panel in range(part.shape[0]):
            value = part[panel].astype(F32)
            for index in range(4):
                blocks[at] = value[:, index * quarter : (index + 1) * quarter]
                at += 1
    rows, half = blocks.shape[1], packed.shape[1]
    for slot in range(at):
        col, place = divmod(slot, at // cols)
        value = blocks[owners[slot]]
        first = place * rows
        for side in range(2):
            lo, hi = max(first, side * half), min(first + rows, (side + 1) * half)
            if lo < hi:
                lanes = slice(side * quarter, (side + 1) * quarter)
                packed[col, lo - side * half : hi - side * half, lanes] = value[lo - first : hi - first]
    out[...] = packed[...].astype(LOW)


def to_slots(after, parts, owner_list):
    quarter, cols = D // 4, lax.axis_size("col")
    panels, rows = sum(part.shape[0] for part in parts), parts[0].shape[1]
    shape = (cols, panels * 4 // cols * rows // 2, 2 * quarter)
    return pl.pallas_call(
        partial(slots_kernel, cols, len(after)),
        in_specs=[SMEM] + [ANY] * len(after) + [pl.BlockSpec(memory_space=pltpu.VMEM)] * len(parts),
        out_shape=jax.ShapeDtypeStruct(shape, LOW),
        scratch_shapes=[pltpu.VMEM((panels * 4, rows, quarter), F32), pltpu.VMEM(shape, F32)],
        compiler_params=params(),
        cost_estimate=cost(4),
        name="slots",
    )(owner_list, *after, *parts)


def spread(slots, beside):
    core, across, y_bits, z_bits = row_steps()
    tail = slots.shape[1:]
    left = axis_bits("col")[::-1]
    part = slots.reshape((1,) + (2,) * len(left) + tail)
    made = []
    for step in (y_bits + z_bits)[::-1]:
        dim = 1 + left.index(step)
        bit = bit_of(step)
        send, keep = pick(part, 1 - bit, dim), pick(part, bit, dim)
        other = swap(send, step)
        if len(made) < len(beside):
            made.append(beside[len(made)]([send] + made[-1:]))
            keep += (0.0 * made[-1][(0,) * made[-1].ndim]).astype(LOW)
        part = jnp.concatenate([keep, other])
        left.remove(step)
    for step in (core + across)[::-1]:
        part = jnp.concatenate([part, swap(part, step)])
    return part, made


def row_place():
    place = 0
    for group in row_steps():
        for step in group:
            place = place * 2 + bit_of(step)
    return place


def shards(
    tokens,
    w_qkv,
    w_attn_out,
    w_in,
    w_out,
    vectors,
    out_grad,
    span_count,
    pair_index,
    owner_list,
    master,
    first_moment,
    second_moment,
    left_basis,
    right_basis,
    vec_first,
    vec_second,
):
    slots = tokens.shape[0] // SPAN
    device = (lax.axis_index("row") * lax.axis_size("col") + lax.axis_index("col")).reshape(1)
    core, across, y_bits, z_bits = row_steps()
    core_bit = bit_of(core[0])
    rows = vectors.reshape(1, -1)
    q, k, v, p, attended = attend(tokens, w_qkv, rows)
    encoded, hidden, slope, normed_low, unit_one, inverse_one, unit_two, inverse_two = feed(
        device, span_count, tokens, attended, w_attn_out, w_in, w_out, rows
    )
    cls_rows = jnp.pad(encoded.reshape(slots, SPAN, D)[:, 0], ((0, GROUP - slots), (0, 0)))
    loss, grad_cls = contrast(gather_all(cls_rows), span_count, pair_index, device, slots)
    grad_two, outer_low, vec_two = outer_grad(
        device, span_count, out_grad, grad_cls, unit_two, inverse_two, rows
    )
    outer_args = (hidden, outer_low, FF // D, True)
    outer_away = weight_half(8, [], 1 - core_bit, *outer_args)
    outer_here = weight_half(60, [outer_away], core_bit, *outer_args)
    outer_run = Reduction(begin_sum(outer_away), outer_here)
    pre_low, grad_one, mixed_low, grad_attended, vec_one = inner_grad(
        outer_run.sent(), outer_low, grad_two, slope, unit_one, inverse_one,
        w_attn_out, w_in, w_out, rows,
    )
    outer_run.land(vec_one)
    inner_args = (normed_low, pre_low, FF // D, False, (attended, mixed_low))
    inner_away = weight_half(8, outer_run.sent(), 1 - core_bit, *inner_args)
    outer_run.land(inner_away)
    inner_here = weight_half(60, [inner_away] + outer_run.sent(), core_bit, *inner_args)
    outer_run.land(inner_here)
    inner_run = Reduction(begin_sum(inner_away), inner_here)
    early, vec_early = unattend(
        outer_run.sent() + inner_run.sent(), 0, 2, q, k, v, p, grad_attended
    )
    outer_run.land(vec_early)
    stack_low, vec_late = unattend([], 1, 2, q, k, v, p, grad_attended, early)
    inner_run.land(vec_late)
    project_args = (tokens, stack_low, 3, False)
    project_away = weight_half(8, inner_run.sent(), 1 - core_bit, *project_args)
    project_here = weight_half(60, [project_away], core_bit, *project_args)
    inner_run.land(project_here)
    vec_heads = vec_early + vec_late
    grad_vector = jnp.concatenate(
        [
            jnp.stack([vec_one[0], vec_two[0], vec_one[1], vec_two[1]]),
            vec_heads,
            jnp.stack([vec_one[2], vec_two[2]]),
            vec_one[3:],
        ]
    )
    project_run = Reduction(begin_sum(project_away), project_here, grad_vector)
    grad_tokens = input_grad(
        inner_run.sent() + project_run.sent(), grad_one, stack_low, w_qkv
    )
    project_run.land(grad_tokens)
    inner_run.land(grad_tokens)
    outer_sum, inner_sum, project_sum = (
        run.finish() for run in (outer_run, inner_run, project_run)
    )
    vec_grad = project_run.rider
    parts = (project_sum, inner_sum[-1:], inner_sum[:-1], outer_sum)
    gathered, (low_left,) = spread(
        to_slots([], parts, owner_list), [lambda after: ready(after, left_basis, LOW)]
    )
    vec_grad = vec_grad.reshape(-1)
    new_master, new_first, new_second, master_copy = rotated_adam(
        row_place(), gathered, turn(master), turn(first_moment), turn(second_moment),
        low_left, right_basis,
    )
    vec_first_new = 0.9 * vec_first + 0.1 * vec_grad
    vec_second_new = 0.999 * vec_second + 0.001 * vec_grad * vec_grad
    vec_step = (
        vec_first_new / (1.0 - 0.9**STEP) / (jnp.sqrt(vec_second_new / (1.0 - 0.999**STEP)) + 1e-08)
    )
    vec_new = vectors - VECTOR_RATE * vec_step
    return (
        encoded,
        grad_tokens,
        loss[0, 0],
        new_master,
        new_first,
        new_second,
        master_copy,
        vec_new,
        vec_first_new,
        vec_second_new,
    )


def solution(mesh):
    in_specs = (
        P(("row", "col"), None),
        P(),
        P(),
        P(),
        P(),
        P(),
        P(("row", "col"), None),
        P(),
        P(),
        P(),
        P("col", None, None),
        P("col", None, None),
        P("col", None, None),
        P("col", None, None),
        P("col", None, None),
        P(),
        P(),
    )
    out_specs = (
        P(("row", "col"), None),
        P(("row", "col"), None),
        P(),
        P("col", None, None),
        P("col", None, None),
        P("col", None, None),
        P("col", None, None),
        P(),
        P(),
        P(),
    )
    return jax.shard_map(shards, mesh=mesh, in_specs=in_specs, out_specs=out_specs, check_vma=False)
```

profile of v0, /device:TPU:0, one launch (start us, length us, event | category | flops | bytes accessed | tf_op | source)
XLA Modules:
  0.0 236.9 jit_solution(12244849483934182948)
XLA Ops:
  0.7 10.4 %attend.1 = (bf16[768,768]{1,0:T(8,128)(2,1)}, bf16[768,768]{1,0:T(8,128)(2,1)}, bf16[768,768]{1,0:T(8,128)(2,1)}, bf16[6,6,128,256]{3,2,1,0:T(8,128)(2,1)}, bf16[768,768]{1,0:T(8,128)(2,1)S(1)}) custom-call(bf16[768,768]{1,0:T(8,128)(2,1)} %refs_1_.2, bf16[3,768,768]{2,1,0:T(8,128)(2,1)} %refs_5_.1, f32[1,9216]{1,0:T(1,128)} %bitcast.208), custom_call_target="tpu_custom_call" | custom-call | flops 11000000512 | tf_op jit(solution)/shard_map/attend/pallas_call | solution.py:103
  11.1 19.0 %feed.1 = (bf16[768,768]{1,0:T(8,128)(2,1)}, bf16[768,3072]{1,0:T(8,128)(2,1)}, bf16[768,3072]{1,0:T(8,128)(2,1)}, bf16[768,768]{1,0:T(8,128)(2,1)}, bf16[768,76...) custom-call(s32[1]{0:T(128)} %bitcast.place, s32[32]{0:T(128)S(1)} %copy-done.5, ...), custom_call_target="tpu_custom_call" | custom-call | flops 22000001024 | tf_op jit(solution)/shard_map/feed/pallas_call | solution.py:185
  31.0 3.0 %collective-permute-start = (bf16[8,768]{1,0:T(8,128)(2,1)S(1)}, bf16[8,768]{1,0:T(8,128)(2,1)S(1)}, u32[]{:S(2)}, u32[]{:S(2)}) collective-permute-start(bf16[8,768]{1,0:T(8,128)(2,1)S(1)} %get-tuple-element.119), channel_id=1, source_target_pairs={{0,1},{1,0},{2,3},{3,2},{4,5},{5,4},{6,7},{7,6},{8,9},{9,8},{10,11... | collective-permute-start | bytes 36872 | tf_op jit(solution)/shard_map/ppermute | solution.py:626
  35.7 2.1 collective-permute-start.1
  39.6 3.0 %collective-permute-start.2 = (bf16[32,768]{1,0:T(8,128)(2,1)S(1)}, bf16[32,768]{1,0:T(8,128)(2,1)S(1)}, u32[]{:S(2)}, u32[]{:S(2)}) collective-permute-start(bf16[32,768]{1,0:T(8,128)(2,1)S(1)} %pad_maximum_fusion.8), channel_id=1, source_target_pairs={{0,4},{1,5},{2,6},{3,7},{4,0},{5,1},{6,2},{7,3},{8,12},{9,13},{10,... | collective-permute-start | bytes 147464 | tf_op jit(solution)/shard_map/ppermute | solution.py:626
  42.6 2.1 collective-permute-done.2
  48.0 5.2 %collective-permute-done.4 = bf16[128,768]{1,0:T(8,128)(2,1)S(1)} collective-permute-done((bf16[128,768]{1,0:T(8,128)(2,1)S(1)}, bf16[128,768]{1,0:T(8,128)(2,1)S(1)}, u32[]{:S(2)}, u32[]{:S(2)}) %collective-permute-start.4) | collective-permute-done | bytes 196640 | tf_op jit(solution)/shard_map/ppermute | solution.py:626
  54.5 2.2 outer.1
  56.8 3.2 %weight.6.refs_0_ = bf16[4,384,768]{2,1,0:T(8,128)(2,1)S(1)} custom-call(s32[1]{0:T(128)} %bitcast.3.side, bf16[768,3072]{1,0:T(8,128)(2,1)S(1)} %bitcast.215, bf16[768,768]{1,0:T(8,128)(2,1)S(1)} %get-tuple-element.47.refs_1_.refs_2_), custom_call_target="tpu_custom_call" | custom-call | flops 8800000000 | tf_op jit(solution)/shard_map/weight/pallas_call | solution.py:281
  60.0 3.3 %weight.7 = bf16[4,384,768]{2,1,0:T(8,128)(2,1)S(1)} custom-call(s32[1]{0:T(128)} %bitcast.2.side, bf16[4,384,768]{2,1,0:T(8,128)(2,1)S(1)} %weight.6.refs_0_, bf16[768,3072]{1,0:T(8,128)(2,1)S(1)} %bitcast.215, bf16[768,768]{1,0:T(8,128)(2,1)S(1)} %get-tuple-element.47.refs_1_.refs_2_), custom_call_target="tpu_custom_call" | custom-call | flops 65999998976 | tf_op jit(solution)/shard_map/weight/pallas_call | solution.py:281
  69.2 15.6 %inner.1 = (bf16[768,3072]{1,0:T(8,128)(2,1)S(1)}, f32[768,768]{1,0:T(8,128)}, bf16[768,768]{1,0:T(8,128)(2,1)S(1)}, bf16[768,768]{1,0:T(8,128)(2,1)S(1)}, f32[7,768]{1,0:T(8,128)S(1)}) custom-call(bf16[768,384]{1,0:T(8,128)(2,1)S(1)} %bitcast.187, bf16[768,384]{1,0:T(8,128)(2,1)S(1)} %bitcast.189, bf16[768,768]{1,0:T(8,128)(2,1)S(1)} %get-tuple-element.47.refs_1_.refs_2_, ...), custom_call_target="tpu_custom_call" | custom-call | flops 17600000000 | tf_op jit(solution)/shard_map/inner/pallas_call | solution.py:341
  87.7 4.0 %weight.8.refs_0_ = bf16[5,384,768]{2,1,0:T(8,128)(2,1)S(1)} custom-call(s32[1]{0:T(128)} %bitcast.3.side, bf16[384,384]{1,0:T(8,128)(2,1)S(1)} %bitcast.203, bf16[384,384]{1,0:T(8,128)(2,1)S(1)} %bitcast.201, bf16[768,768]{1,0:T(8,128)(2,1)S(1)} %copy-done.10, bf16[768,3072]{1,0:T(8,128)(2,1)S(1)} %get-tuple-element.54.refs_3_, ...), custom_call_target="tpu_custom_call" | custom-call | flops 8800000000 | tf_op jit(solution)/shard_map/weight/pallas_call | solution.py:281
  92.9 2.3 collective-permute-done.9
  97.3 4.0 %weight.9 = bf16[5,384,768]{2,1,0:T(8,128)(2,1)S(1)} custom-call(s32[1]{0:T(128)} %bitcast.2.side, bf16[5,384,768]{2,1,0:T(8,128)(2,1)S(1)} %weight.8.refs_0_, bf16[192,768]{1,0:T(8,128)(2,1)S(1)} %bitcast.205, bf16[768,768]{1,0:T(8,128)(2,1)S(1)} %copy-done.10, bf16[768,3072]{1,0:T(8,128)(2,1)S(1)} %get-tuple-element.54.refs_3_, ...), custom_call_target="tpu_custom_call" | custom-call | flops 65999998976 | tf_op jit(solution)/shard_map/weight/pallas_call | solution.py:281
  107.6 7.1 %unattend.2 = (bf16[768,2304]{1,0:T(8,128)(2,1)}, f32[2,768]{1,0:T(2,128)S(1)}) custom-call(bf16[96,768]{1,0:T(8,128)(2,1)S(1)} %bitcast.206, bf16[960,384]{1,0:T(8,128)(2,1)S(1)} %bitcast.183, bf16[960,384]{1,0:T(8,128)(2,1)S(1)} %bitcast.185, bf16[768,768]{1,0:T(8,128)(2,1)S(1)} %copy-done.11, bf16[768,768]{1,0:T(8,128)(2,1)S(1)} %copy-done.12, ...), custom_call_target="tpu_custom_call" | custom-call | flops 8800000000 | tf_op jit(solution)/shard_map/unattend/pallas_call | solution.py:407
  114.7 6.9 %unattend.3 = (bf16[768,2304]{1,0:T(8,128)(2,1)}, f32[2,768]{1,0:T(2,128)S(1)}) custom-call(bf16[768,2304]{1,0:T(8,128)(2,1)} %get-tuple-element.61.refs_0_, bf16[768,768]{1,0:T(8,128)(2,1)S(1)} %copy-done.11, bf16[768,768]{1,0:T(8,128)(2,1)S(1)} %copy-done.12, bf16[768,768]{1,0:T(8,128)(2,1)S(1)} %copy-done.13, ...), custom_call_target="tpu_custom_call", output_to_operand_aliasing={{0}: (0, {})} | custom-call | flops 8800000000 | tf_op jit(solution)/shard_map/unattend/pallas_call | solution.py:407
  121.7 2.9 %collective-permute-start.26 = (bf16[96,768]{1,0:T(8,128)(2,1)S(1)}, bf16[96,768]{1,0:T(8,128)(2,1)}, u32[]{:S(2)}, u32[]{:S(2)}) collective-permute-start(bf16[96,768]{1,0:T(8,128)(2,1)S(1)} %bitcast.207), channel_id=1, source_target_pairs={{0,4},{1,5},{2,6},{3,7},{4,0},{5,1},{6,2},{7,3},{8,12},{9,13},{10,... | collective-permute-start | bytes 442376 | tf_op jit(solution)/shard_map/ppermute | solution.py:626
  132.2 2.4 %weight.10.refs_0_ = bf16[3,384,768]{2,1,0:T(8,128)(2,1)S(1)} custom-call(s32[1]{0:T(128)} %bitcast.3.side, bf16[480,384]{1,0:T(8,128)(2,1)S(1)} %bitcast.199, bf16[480,384]{1,0:T(8,128)(2,1)S(1)} %bitcast.197, bf16[768,768]{1,0:T(8,128)(2,1)S(1)} %copy-done.4, bf16[768,2304]{1,0:T(8,128)(2,1)S(1)} %copy-done.7), custom_call_target="tpu_custom_call" | custom-call | flops 8800000000 | tf_op jit(solution)/shard_map/weight/pallas_call | solution.py:281
  134.7 2.4 %weight.11 = bf16[3,384,768]{2,1,0:T(8,128)(2,1)S(1)} custom-call(s32[1]{0:T(128)} %bitcast.2.side, bf16[3,384,768]{2,1,0:T(8,128)(2,1)S(1)} %weight.10.refs_0_, bf16[768,768]{1,0:T(8,128)(2,1)S(1)} %copy-done.4, bf16[768,2304]{1,0:T(8,128)(2,1)S(1)} %copy-done.7), custom_call_target="tpu_custom_call" | custom-call | flops 65999998976 | tf_op jit(solution)/shard_map/weight/pallas_call | solution.py:281
  138.3 2.5 %collective-permute-done.15 = bf16[480,384]{1,0:T(8,128)(2,1)S(1)} collective-permute-done((bf16[480,384]{1,0:T(8,128)(2,1)S(1)}, bf16[480,384]{1,0:T(8,128)(2,1)S(1)}, u32[]{:S(2)}, u32[]{:S(2)}) %collective-permute-start.15) | collective-permute-done | bytes 368672 | tf_op jit(solution)/shard_map/ppermute | solution.py:626
  145.1 4.3 %input.1 = f32[768,768]{1,0:T(8,128)} custom-call(bf16[240,768]{1,0:T(8,128)(2,1)S(1)} %bitcast.194, bf16[600,384]{1,0:T(8,128)(2,1)S(1)} %pad_maximum_fusion.2.refs_1_, bf16[576,384]{1,0:T(8,128)(2,1)S(1)} %bitcast.191, f32[768,768]{1,0:T(8,128)S(1)} %copy-done.8, bf16[768,2304]{1,0:T(8,128)(2,1)S(1)} %copy-done.7, bf16[3,768,768]{2,1,0:T(8,128)(2,1)S(1)} %copy-done.2), custom_call_target="tpu_custom_call" | custom-call | flops 8800000000 | tf_op jit(solution)/shard_map/input/pallas_call | solution.py:439
  151.2 2.7 %collective-permute-done.20 = bf16[576,384]{1,0:T(8,128)(2,1)S(1)} collective-permute-done((bf16[576,384]{1,0:T(8,128)(2,1)S(1)}, bf16[576,384]{1,0:T(8,128)(2,1)S(1)}, u32[]{:S(2)}, u32[]{:S(2)}) %collective-permute-start.20) | collective-permute-done | bytes 442400 | tf_op jit(solution)/shard_map/ppermute | solution.py:626
  164.3 6.7 %collective-permute-done.24 = bf16[240,768]{1,0:T(8,128)(2,1)S(1)} collective-permute-done((bf16[240,768]{1,0:T(8,128)(2,1)S(1)}, bf16[240,768]{1,0:T(8,128)(2,1)S(1)}, u32[]{:S(2)}, u32[]{:S(2)}) %collective-permute-start.24) | collective-permute-done | bytes 368672 | tf_op jit(solution)/shard_map/ppermute | solution.py:626
  171.4 3.0 %collective-permute-done.22 = bf16[156,768]{1,0:T(8,128)(2,1)S(1)} collective-permute-done((bf16[156,768]{1,0:T(8,128)(2,1)S(1)}, bf16[156,768]{1,0:T(8,128)(2,1)S(1)}, u32[]{:S(2)}, u32[]{:S(2)}) %collective-permute-start.22) | collective-permute-done | bytes 239648 | tf_op jit(solution)/shard_map/ppermute | solution.py:626
  174.9 5.8 %collective-permute-done.25 = bf16[120,768]{1,0:T(8,128)(2,1)S(1)} collective-permute-done((bf16[120,768]{1,0:T(8,128)(2,1)S(1)}, bf16[120,768]{1,0:T(8,128)(2,1)S(1)}, u32[]{:S(2)}, u32[]{:S(2)}) %collective-permute-start.25) | collective-permute-done | bytes 184352 | tf_op jit(solution)/shard_map/ppermute | solution.py:626
  180.8 2.8 %collective-permute-done.23 = bf16[84,768]{1,0:T(8,128)(2,1)S(1)} collective-permute-done((bf16[84,768]{1,0:T(8,128)(2,1)S(1)}, bf16[84,768]{1,0:T(8,128)(2,1)S(1)}, u32[]{:S(2)}, u32[]{:S(2)}) %collective-permute-start.23) | collective-permute-done | bytes 129056 | tf_op jit(solution)/shard_map/ppermute | solution.py:626
  184.8 9.0 %ready.1.left = bf16[6,768,768]{2,1,0:T(8,128)(2,1)} custom-call(bf16[1,2,2,72,384]{4,3,2,1,0:T(8,128)(2,1)S(1)} %dynamic-slice_bitcast_fusion.refs_0_, f32[6,768,768]{2,1,0:T(8,128)} %refs_1_.3), custom_call_target="tpu_custom_call" | custom-call | flops 4400000000 | tf_op jit(solution)/shard_map/ready/pallas_call | solution.py:563
  195.7 2.7 %collective-permute-start.28 = (bf16[2,2,72,384]{3,2,1,0:T(8,128)(2,1)S(1)}, bf16[2,2,72,384]{3,2,1,0:T(8,128)(2,1)S(1)}, u32[]{:S(2)}, u32[]{:S(2)}) collective-permute-start(bf16[2,2,72,384]{3,2,1,0:T(8,128)(2,1)S(1)} %get-tuple-element.101), channel_id=1, source_target_pairs={{0,2},{1,3},{2,0},{3,1},{4,6},{5,7},{6,4},{7,5},{8,10},{9,11},{10,... | collective-permute-start | bytes 663560 | tf_op jit(solution)/shard_map/ppermute | solution.py:626
  198.5 3.9 %collective-permute-done.28 = bf16[2,2,72,384]{3,2,1,0:T(8,128)(2,1)S(1)} collective-permute-done((bf16[2,2,72,384]{3,2,1,0:T(8,128)(2,1)S(1)}, bf16[2,2,72,384]{3,2,1,0:T(8,128)(2,1)S(1)}, u32[]{:S(2)}, u32[]{:S(2)}) %collective-permute-start.28) | collective-permute-done | bytes 221216 | tf_op jit(solution)/shard_map/ppermute | solution.py:626
  203.4 5.1 %collective-permute-done.29 = bf16[4,72,384]{2,1,0:T(8,128)(2,1)S(1)} collective-permute-done((bf16[4,72,384]{2,1,0:T(8,128)(2,1)S(1)}, bf16[4,72,384]{2,1,0:T(8,128)(2,1)S(1)}, u32[]{:S(2)}, u32[]{:S(2)}) %collective-permute-start.29) | collective-permute-done | bytes 221216 | tf_op jit(solution)/shard_map/ppermute | solution.py:626
  209.5 7.4 %collective-permute-done.30 = bf16[8,72,384]{2,1,0:T(8,128)(2,1)S(1)} collective-permute-done((bf16[8,72,384]{2,1,0:T(8,128)(2,1)S(1)}, bf16[8,72,384]{2,1,0:T(8,128)(2,1)S(1)}, u32[]{:S(2)}, u32[]{:S(2)}) %collective-permute-start.30) | collective-permute-done | bytes 442400 | tf_op jit(solution)/shard_map/ppermute | solution.py:626
  219.7 17.1 %adam.1 = (f32[6,192,768]{2,1,0:T(8,128)}, f32[6,192,768]{2,1,0:T(8,128)}, f32[6,192,768]{2,1,0:T(8,128)}, bf16[6,192,768]{2,1,0:T(8,128)(2,1)}) custom-call(s32[1]{0:T(128)} %bitcast.48.position, bf16[32,72,384]{2,1,0:T(8,128)(2,1)S(1)} %pad_maximum_fusion.gathered, f32[6,192,768]{2,1,0:T(8,128)} %bitcast.240, f32[6,192,768]{2,1,0:T(8,128)} %bitcast.241, ...), custom_call_target="tpu_custom_call" | custom-call | flops 22000001024 | tf_op jit(solution)/shard_map/adam/pallas_call | solution.py:598
  (204 shorter events, 56.0 us)
Async XLA Ops:
  31.0 4.7 %collective-permute-start = (bf16[8,768]{1,0:T(8,128)(2,1)S(1)}, bf16[8,768]{1,0:T(8,128)(2,1)S(1)}, u32[]{:S(2)}, u32[]{:S(2)}) collective-permute-start(bf16[8,768]{1,0:T(8,128)(2,1)S(1)} %get-tuple-element.119), channel_id=1, source_target_pairs={{0,1},{1,0},{2,3},{3,2},{4,5},{5,4},{6,7},{7,6},{8,9},{9,8},{10,11... | collective-permute-start | bytes 36872 | tf_op jit(solution)/shard_map/ppermute | solution.py:626
  35.7 3.9 %collective-permute-start.1 = (bf16[16,768]{1,0:T(8,128)(2,1)S(1)}, bf16[16,768]{1,0:T(8,128)(2,1)S(1)}, u32[]{:S(2)}, u32[]{:S(2)}) collective-permute-start(bf16[16,768]{1,0:T(8,128)(2,1)S(1)} %pad_maximum_fusion.9), channel_id=1, source_target_pairs={{0,2},{1,3},{2,0},{3,1},{4,6},{5,7},{6,4},{7,5},{8,10},{9,11},{10,... | collective-permute-start | bytes 73736 | tf_op jit(solution)/shard_map/ppermute | solution.py:626
  39.6 5.1 %collective-permute-start.2 = (bf16[32,768]{1,0:T(8,128)(2,1)S(1)}, bf16[32,768]{1,0:T(8,128)(2,1)S(1)}, u32[]{:S(2)}, u32[]{:S(2)}) collective-permute-start(bf16[32,768]{1,0:T(8,128)(2,1)S(1)} %pad_maximum_fusion.8), channel_id=1, source_target_pairs={{0,4},{1,5},{2,6},{3,7},{4,0},{5,1},{6,2},{7,3},{8,12},{9,13},{10,... | collective-permute-start | bytes 147464 | tf_op jit(solution)/shard_map/ppermute | solution.py:626
  44.7 1.4 collective-permute-start.3
  46.1 7.1 %collective-permute-start.4 = (bf16[128,768]{1,0:T(8,128)(2,1)S(1)}, bf16[128,768]{1,0:T(8,128)(2,1)S(1)}, u32[]{:S(2)}, u32[]{:S(2)}) collective-permute-start(bf16[128,768]{1,0:T(8,128)(2,1)S(1)} %get-tuple-element.103), channel_id=1, source_target_pairs={{0,16},{8,24},{16,0},{24,8},{1,17},{9,25},{17,1},{25,9},{2,18},{10... | collective-permute-start | bytes 589832 | tf_op jit(solution)/shard_map/ppermute | solution.py:626
  59.9 4.6 %collective-permute-start.5 = (bf16[4,384,768]{2,1,0:T(8,128)(2,1)S(1)}, bf16[4,384,768]{2,1,0:T(8,128)(2,1)S(1)}, u32[]{:S(2)}, u32[]{:S(2)}) collective-permute-start(bf16[4,384,768]{2,1,0:T(8,128)(2,1)S(1)} %weight.6.refs_0_), channel_id=1, source_target_pairs={{0,8},{8,0},{16,24},{24,16},{1,9},{9,1},{17,25},{25,17},{2,10},{10... | collective-permute-start | bytes 7077896 | tf_op jit(solution)/shard_map/ppermute | solution.py:626
  65.7 20.3 %collective-permute-start.7 = (bf16[768,384]{1,0:T(8,128)(2,1)S(1)}, bf16[768,384]{1,0:T(8,128)(2,1)S(1)}, u32[]{:S(2)}, u32[]{:S(2)}) collective-permute-start(bf16[768,384]{1,0:T(8,128)(2,1)S(1)} %bitcast.188), channel_id=1, source_target_pairs={{0,1},{1,0},{2,3},{3,2},{4,5},{5,4},{6,7},{7,6},{8,9},{9,8},{10,11... | collective-permute-start | bytes 1769480 | tf_op jit(solution)/shard_map/ppermute | solution.py:626
  67.6 18.7 %collective-permute-start.6 = (bf16[768,384]{1,0:T(8,128)(2,1)S(1)}, bf16[768,384]{1,0:T(8,128)(2,1)S(1)}, u32[]{:S(2)}, u32[]{:S(2)}) collective-permute-start(bf16[768,384]{1,0:T(8,128)(2,1)S(1)} %bitcast.186), channel_id=1, source_target_pairs={{0,16},{8,24},{16,0},{24,8},{1,17},{9,25},{17,1},{25,9},{2,18},{10... | collective-permute-start | bytes 1769480 | tf_op jit(solution)/shard_map/ppermute | solution.py:626
  86.6 8.6 %collective-permute-start.9 = (bf16[384,384]{1,0:T(8,128)(2,1)S(1)}, bf16[384,384]{1,0:T(8,128)(2,1)S(1)}, u32[]{:S(2)}, u32[]{:S(2)}) collective-permute-start(bf16[384,384]{1,0:T(8,128)(2,1)S(1)} %bitcast.200), channel_id=1, source_target_pairs={{0,16},{8,24},{16,0},{24,8},{1,17},{9,25},{17,1},{25,9},{2,18},{10... | collective-permute-start | bytes 884744 | tf_op jit(solution)/shard_map/ppermute | solution.py:626
  87.2 8.2 %collective-permute-start.8 = (bf16[384,384]{1,0:T(8,128)(2,1)S(1)}, bf16[384,384]{1,0:T(8,128)(2,1)S(1)}, u32[]{:S(2)}, u32[]{:S(2)}) collective-permute-start(bf16[384,384]{1,0:T(8,128)(2,1)S(1)} %bitcast.202), channel_id=1, source_target_pairs={{0,1},{1,0},{2,3},{3,2},{4,5},{5,4},{6,7},{7,6},{8,9},{9,8},{10,11... | collective-permute-start | bytes 884744 | tf_op jit(solution)/shard_map/ppermute | solution.py:626
  92.2 11.0 %collective-permute-start.10 = (bf16[5,384,768]{2,1,0:T(8,128)(2,1)S(1)}, bf16[5,384,768]{2,1,0:T(8,128)(2,1)S(1)}, u32[]{:S(2)}, u32[]{:S(2)}) collective-permute-start(bf16[5,384,768]{2,1,0:T(8,128)(2,1)S(1)} %weight.8.refs_0_), channel_id=1, source_target_pairs={{0,8},{8,0},{16,24},{24,16},{1,9},{9,1},{17,25},{25,17},{2,10},{10... | collective-permute-start | bytes 8847368 | tf_op jit(solution)/shard_map/ppermute | solution.py:626
  95.7 7.4 %collective-permute-start.12 = (bf16[192,768]{1,0:T(8,128)(2,1)S(1)}, bf16[192,768]{1,0:T(8,128)(2,1)S(1)}, u32[]{:S(2)}, u32[]{:S(2)}) collective-permute-start(bf16[192,768]{1,0:T(8,128)(2,1)S(1)} %bitcast.204), channel_id=1, source_target_pairs={{0,2},{1,3},{2,0},{3,1},{4,6},{5,7},{6,4},{7,5},{8,10},{9,11},{10,... | collective-permute-start | bytes 884744 | tf_op jit(solution)/shard_map/ppermute | solution.py:626
  105.0 22.0 %collective-permute-start.14 = (bf16[960,384]{1,0:T(8,128)(2,1)S(1)}, bf16[960,384]{1,0:T(8,128)(2,1)}, u32[]{:S(2)}, u32[]{:S(2)}) collective-permute-start(bf16[960,384]{1,0:T(8,128)(2,1)S(1)} %bitcast.184), channel_id=1, source_target_pairs={{0,1},{1,0},{2,3},{3,2},{4,5},{5,4},{6,7},{7,6},{8,9},{9,8},{10,11... | collective-permute-start | bytes 2211848 | tf_op jit(solution)/shard_map/ppermute | solution.py:626
  106.7 21.8 %collective-permute-start.11 = (bf16[960,384]{1,0:T(8,128)(2,1)S(1)}, bf16[960,384]{1,0:T(8,128)(2,1)}, u32[]{:S(2)}, u32[]{:S(2)}) collective-permute-start(bf16[960,384]{1,0:T(8,128)(2,1)S(1)} %bitcast.182), channel_id=1, source_target_pairs={{0,16},{8,24},{16,0},{24,8},{1,17},{9,25},{17,1},{25,9},{2,18},{10... | collective-permute-start | bytes 2211848 | tf_op jit(solution)/shard_map/ppermute | solution.py:626
  121.6 5.3 %collective-permute-start.17 = (f32[12,768]{1,0:T(8,128)S(1)}, f32[12,768]{1,0:T(8,128)S(1)}, u32[]{:S(2)}, u32[]{:S(2)}) collective-permute-start(f32[12,768]{1,0:T(8,128)S(1)} %concatenate.67), channel_id=1, source_target_pairs={{0,8},{8,0},{16,24},{24,16},{1,9},{9,1},{17,25},{25,17},{2,10},{10... | collective-permute-start | bytes 110600 | tf_op jit(solution)/shard_map/ppermute | solution.py:626
  121.7 35.7 %collective-permute-start.26 = (bf16[96,768]{1,0:T(8,128)(2,1)S(1)}, bf16[96,768]{1,0:T(8,128)(2,1)}, u32[]{:S(2)}, u32[]{:S(2)}) collective-permute-start(bf16[96,768]{1,0:T(8,128)(2,1)S(1)} %bitcast.207), channel_id=1, source_target_pairs={{0,4},{1,5},{2,6},{3,7},{4,0},{5,1},{6,2},{7,3},{8,12},{9,13},{10,... | collective-permute-start | bytes 442376 | tf_op jit(solution)/shard_map/ppermute | solution.py:626
  130.1 10.7 %collective-permute-start.15 = (bf16[480,384]{1,0:T(8,128)(2,1)S(1)}, bf16[480,384]{1,0:T(8,128)(2,1)S(1)}, u32[]{:S(2)}, u32[]{:S(2)}) collective-permute-start(bf16[480,384]{1,0:T(8,128)(2,1)S(1)} %bitcast.196), channel_id=1, source_target_pairs={{0,16},{8,24},{16,0},{24,8},{1,17},{9,25},{17,1},{25,9},{2,18},{10... | collective-permute-start | bytes 1105928 | tf_op jit(solution)/shard_map/ppermute | solution.py:626
  131.3 10.4 %collective-permute-start.13 = (bf16[480,384]{1,0:T(8,128)(2,1)S(1)}, bf16[480,384]{1,0:T(8,128)(2,1)S(1)}, u32[]{:S(2)}, u32[]{:S(2)}) collective-permute-start(bf16[480,384]{1,0:T(8,128)(2,1)S(1)} %bitcast.198), channel_id=1, source_target_pairs={{0,1},{1,0},{2,3},{3,2},{4,5},{5,4},{6,7},{7,6},{8,9},{9,8},{10,11... | collective-permute-start | bytes 1105928 | tf_op jit(solution)/shard_map/ppermute | solution.py:626
  134.6 7.2 %collective-permute-start.16 = (bf16[3,384,768]{2,1,0:T(8,128)(2,1)S(1)}, bf16[3,384,768]{2,1,0:T(8,128)(2,1)S(1)}, u32[]{:S(2)}, u32[]{:S(2)}) collective-permute-start(bf16[3,384,768]{2,1,0:T(8,128)(2,1)S(1)} %weight.10.refs_0_), channel_id=1, source_target_pairs={{0,8},{8,0},{16,24},{24,16},{1,9},{9,1},{17,25},{25,17},{2,10},{10... | collective-permute-start | bytes 5308424 | tf_op jit(solution)/shard_map/ppermute | solution.py:626
  142.7 11.2 %collective-permute-start.20 = (bf16[576,384]{1,0:T(8,128)(2,1)S(1)}, bf16[576,384]{1,0:T(8,128)(2,1)S(1)}, u32[]{:S(2)}, u32[]{:S(2)}) collective-permute-start(bf16[576,384]{1,0:T(8,128)(2,1)S(1)} %bitcast.190), channel_id=1, source_target_pairs={{0,1},{1,0},{2,3},{3,2},{4,5},{5,4},{6,7},{7,6},{8,9},{9,8},{10,11... | collective-permute-start | bytes 1327112 | tf_op jit(solution)/shard_map/ppermute | solution.py:626
  143.8 11.9 %collective-permute-start.18 = (bf16[600,384]{1,0:T(8,128)(2,1)S(1)}, bf16[600,384]{1,0:T(8,128)(2,1)S(1)}, u32[]{:S(2)}, u32[]{:S(2)}) collective-permute-start(bf16[600,384]{1,0:T(8,128)(2,1)S(1)} %pad_maximum_fusion.2.refs_1_), channel_id=1, source_target_pairs={{0,16},{8,24},{16,0},{24,8},{1,17},{9,25},{17,1},{25,9},{2,18},{10... | collective-permute-start | bytes 1382408 | tf_op jit(solution)/shard_map/ppermute | solution.py:626
  154.8 6.2 %collective-permute-start.21 = (bf16[288,384]{1,0:T(8,128)(2,1)}, bf16[288,384]{1,0:T(8,128)(2,1)}, u32[]{:S(2)}, u32[]{:S(2)}) collective-permute-start(bf16[288,384]{1,0:T(8,128)(2,1)} %bitcast.58), channel_id=1, source_target_pairs={{0,16},{8,24},{16,0},{24,8},{1,17},{9,25},{17,1},{25,9},{2,18},{10... | collective-permute-start | bytes 663560 | tf_op jit(solution)/shard_map/ppermute | solution.py:626
  156.1 6.2 %collective-permute-start.19 = (bf16[312,384]{1,0:T(8,128)(2,1)S(1)}, bf16[312,384]{1,0:T(8,128)(2,1)S(1)}, u32[]{:S(2)}, u32[]{:S(2)}) collective-permute-start(bf16[312,384]{1,0:T(8,128)(2,1)S(1)} %pad_maximum_fusion.5), channel_id=1, source_target_pairs={{0,1},{1,0},{2,3},{3,2},{4,5},{5,4},{6,7},{7,6},{8,9},{9,8},{10,11... | collective-permute-start | bytes 718856 | tf_op jit(solution)/shard_map/ppermute | solution.py:626
  158.3 12.7 %collective-permute-start.24 = (bf16[240,768]{1,0:T(8,128)(2,1)S(1)}, bf16[240,768]{1,0:T(8,128)(2,1)S(1)}, u32[]{:S(2)}, u32[]{:S(2)}) collective-permute-start(bf16[240,768]{1,0:T(8,128)(2,1)S(1)} %bitcast.195), channel_id=1, source_target_pairs={{0,2},{1,3},{2,0},{3,1},{4,6},{5,7},{6,4},{7,5},{8,10},{9,11},{10,... | collective-permute-start | bytes 1105928 | tf_op jit(solution)/shard_map/ppermute | solution.py:626
  162.5 11.8 %collective-permute-start.22 = (bf16[156,768]{1,0:T(8,128)(2,1)S(1)}, bf16[156,768]{1,0:T(8,128)(2,1)S(1)}, u32[]{:S(2)}, u32[]{:S(2)}) collective-permute-start(bf16[156,768]{1,0:T(8,128)(2,1)S(1)} %pad_maximum_fusion.4), channel_id=1, source_target_pairs={{0,2},{1,3},{2,0},{3,1},{4,6},{5,7},{6,4},{7,5},{8,10},{9,11},{10,... | collective-permute-start | bytes 718856 | tf_op jit(solution)/shard_map/ppermute | solution.py:626
  171.2 9.5 %collective-permute-start.25 = (bf16[120,768]{1,0:T(8,128)(2,1)S(1)}, bf16[120,768]{1,0:T(8,128)(2,1)S(1)}, u32[]{:S(2)}, u32[]{:S(2)}) collective-permute-start(bf16[120,768]{1,0:T(8,128)(2,1)S(1)} %bitcast.237), channel_id=1, source_target_pairs={{0,4},{1,5},{2,6},{3,7},{4,0},{5,1},{6,2},{7,3},{8,12},{9,13},{10,... | collective-permute-start | bytes 552968 | tf_op jit(solution)/shard_map/ppermute | solution.py:626
  174.5 9.1 %collective-permute-start.23 = (bf16[84,768]{1,0:T(8,128)(2,1)S(1)}, bf16[84,768]{1,0:T(8,128)(2,1)S(1)}, u32[]{:S(2)}, u32[]{:S(2)}) collective-permute-start(bf16[84,768]{1,0:T(8,128)(2,1)S(1)} %pad_maximum_fusion.6), channel_id=1, source_target_pairs={{0,4},{1,5},{2,6},{3,7},{4,0},{5,1},{6,2},{7,3},{8,12},{9,13},{10,... | collective-permute-start | bytes 387080 | tf_op jit(solution)/shard_map/ppermute | solution.py:626
  184.7 11.0 %collective-permute-start.27 = (bf16[1,2,2,72,384]{4,3,2,1,0:T(8,128)(2,1)S(1)}, bf16[1,2,2,72,384]{4,3,2,1,0:T(8,128)(2,1)S(1)}, u32[]{:S(2)}, u32[]{:S(2)}) collective-permute-start(bf16[1,2,2,72,384]{4,3,2,1,0:T(8,128)(2,1)S(1)} %dynamic-slice_bitcast_fusion.refs_0_), channel_id=1, source_target_pairs={{0,4},{1,5},{2,6},{3,7},{4,0},{5,1},{6,2},{7,3},{8,12},{9,13},{10,... | collective-permute-start | bytes 663560 | tf_op jit(solution)/shard_map/ppermute | solution.py:626
  195.7 6.7 %collective-permute-start.28 = (bf16[2,2,72,384]{3,2,1,0:T(8,128)(2,1)S(1)}, bf16[2,2,72,384]{3,2,1,0:T(8,128)(2,1)S(1)}, u32[]{:S(2)}, u32[]{:S(2)}) collective-permute-start(bf16[2,2,72,384]{3,2,1,0:T(8,128)(2,1)S(1)} %get-tuple-element.101), channel_id=1, source_target_pairs={{0,2},{1,3},{2,0},{3,1},{4,6},{5,7},{6,4},{7,5},{8,10},{9,11},{10,... | collective-permute-start | bytes 663560 | tf_op jit(solution)/shard_map/ppermute | solution.py:626
  202.4 6.0 %collective-permute-start.29 = (bf16[4,72,384]{2,1,0:T(8,128)(2,1)S(1)}, bf16[4,72,384]{2,1,0:T(8,128)(2,1)S(1)}, u32[]{:S(2)}, u32[]{:S(2)}) collective-permute-start(bf16[4,72,384]{2,1,0:T(8,128)(2,1)S(1)} %get-tuple-element.100), channel_id=1, source_target_pairs={{0,1},{1,0},{2,3},{3,2},{4,5},{5,4},{6,7},{7,6},{8,9},{9,8},{10,11... | collective-permute-start | bytes 663560 | tf_op jit(solution)/shard_map/ppermute | solution.py:626
  208.5 8.4 %collective-permute-start.30 = (bf16[8,72,384]{2,1,0:T(8,128)(2,1)S(1)}, bf16[8,72,384]{2,1,0:T(8,128)(2,1)S(1)}, u32[]{:S(2)}, u32[]{:S(2)}) collective-permute-start(bf16[8,72,384]{2,1,0:T(8,128)(2,1)S(1)} %pad_maximum_fusion.3), channel_id=1, source_target_pairs={{0,16},{8,24},{16,0},{24,8},{1,17},{9,25},{17,1},{25,9},{2,18},{10... | collective-permute-start | bytes 1327112 | tf_op jit(solution)/shard_map/ppermute | solution.py:626
  217.0 2.5 %collective-permute-start.31 = (bf16[16,72,384]{2,1,0:T(8,128)(2,1)S(1)}, bf16[16,72,384]{2,1,0:T(8,128)(2,1)S(1)}, u32[]{:S(2)}, u32[]{:S(2)}) collective-permute-start(bf16[16,72,384]{2,1,0:T(8,128)(2,1)S(1)} %pad_maximum_fusion.1), channel_id=1, source_target_pairs={{0,8},{8,0},{16,24},{24,16},{1,9},{9,1},{17,25},{25,17},{2,10},{10... | collective-permute-start | bytes 2654216 | tf_op jit(solution)/shard_map/ppermute | solution.py:626
  (24 other events, 146.6 us)
where the time goes:
time: 237 us
  Pallas kernels  113 us (48%)
  waiting for transfers between devices  59 us (25%)
  starting transfers between devices  37.5 us (16%)
  other arithmetic  10.5 us (4%)
  local copies, waits for them, and re-layouts  9.92 us (4%)
  between operations  6.97 us (3%)
    ppermute x32, waiting for transfers between devices, swap(): return lax.ppermute(send, step[0], [(i, i ^ step[1]) for i in range(size)])  59 us
    ppermute x32, starting transfers between devices, swap(): return lax.ppermute(send, step[0], [(i, i ^ step[1]) for i in range(size)])  37.5 us
    pallas_call x6, Pallas kernels, weight_half(): pl.pallas_call(partial(weight_kernel, panels, len(after)), grid_spec=pltp...  19.2 us
    pallas_call x1, Pallas kernels, feed(): pl.pallas_call(feed_kernel, grid=(FF // D,), in_specs=[SMEM, SMEM, tall(D...  19 us
    pallas_call x1, Pallas kernels, rotated_adam(): pl.pallas_call(partial(adam_kernel, packed), grid_spec=pltpu.PrefetchScal...  17.1 us
    pallas_call x1, Pallas kernels, inner_grad(): pl.pallas_call(partial(inner_kernel, len(after)), grid=(bands,), in_specs...  15.6 us
    pallas_call x2, Pallas kernels, unattend(): pl.pallas_call(unattend_kernel, grid=(count,), in_specs=[ANY] * len(after...  14 us
    pallas_call x1, Pallas kernels, attend(): pl.pallas_call(attend_kernel, grid=(total // TALL,), in_specs=[tall, whol...  10.4 us
  transfers between devices with their start and end apart: 32, of which 22 were waited for; matrix products, arithmetic and copies ran while one was open for 7% of the time, Pallas kernels for 25%

commit v1 on v0

--- a/solution.py
+++ b/solution.py
@@ -137,7 +137,7 @@
 
 def feed_kernel(
     place, counts, tokens, attended, w_attn, w_in, w_out, rows, bias,
-    enc_out, hid_out, slope_out, norm_out, u1_out, i1_out, u2_out, i2_out, total,
+    enc_out, hid_out, slope_out, norm_out, u1_out, i1_out, u2_out, i2_out, cls_out, total, firsts,
 ):
     band = pl.program_id(0)
     chunks = [slice(at, at + TALL) for at in range(0, tokens.shape[0], TALL)]
@@ -175,6 +175,11 @@
             live = live_rows(place, counts, at.start, TALL)
             value = live * (unit_two * row_of(rows, 1) + row_of(rows, 3))
             enc_out[at] = value.astype(LOW)
+            for first in range(at.start, at.stop, SPAN):
+                row = first - at.start
+                firsts[first // SPAN : first // SPAN + 1] = value[row : row + 1]
+        firsts[tokens.shape[0] // SPAN :] = jnp.zeros((GROUP - tokens.shape[0] // SPAN, D), F32)
+        cls_out[...] = firsts[...].astype(LOW)
 
 
 def feed(place, counts, tokens, attended, w_attn, w_in, w_out, rows):
@@ -193,6 +198,7 @@
         ],
         out_specs=[
             tall(D), band(total), band(total), tall(D), tall(D), tall(1), tall(D), tall(1),
+            whole((GROUP, D)),
         ],
         out_shape=[
             jax.ShapeDtypeStruct((total, D), LOW),
@@ -203,8 +209,9 @@
             far((total, 1), F32),
             near((total, D), LOW),
             near((total, 1), F32),
+            jax.ShapeDtypeStruct((GROUP, D), LOW),
         ],
-        scratch_shapes=[pltpu.VMEM((total, D), F32)],
+        scratch_shapes=[pltpu.VMEM((total, D), F32), pltpu.VMEM((GROUP, D), F32)],
         compiler_params=params(),
         cost_estimate=cost(20),
         name="feed",
@@ -362,15 +369,27 @@
     )(*after, low, grad_two, slope, unit_one, inverse_one, w_attn, w_in, w_out, rows)
 
 
-def unattend_kernel(*refs):
-    q, k, v, p, ga, stack_out, vec_out = refs[-7:]
+def unattend_kernel(after, sums, *refs):
+    q, k, v, p, ga = refs[after : after + 5]
+    vec_one, vec_two, vec_early = refs[after + 5 : -2] if sums else (None, None, None)
+    stack_out, vec_out = refs[-2:]
     scaling = HEAD ** (-0.5)
     first = pl.program_id(0) == 0
 
     @pl.when(first)
     def _():
-        vec_out[...] = jnp.zeros_like(vec_out)
-
+        if not sums:
+            vec_out[...] = jnp.zeros_like(vec_out)
+            return
+        for index in range(2):
+            vec_out[2 * index : 2 * index + 1] = vec_one[index : index + 1]
+            vec_out[2 * index + 1 : 2 * index + 2] = vec_two[index : index + 1]
+        vec_out[4:6] = vec_early[...]
+        vec_out[6:7] = vec_one[2:3]
+        vec_out[7:8] = vec_two[2:3]
+        vec_out[8:] = vec_one[3:]
+
+    place = 4 if sums else 0
     for span in range(p.shape[0]):
         at = slice(span * SPAN, (span + 1) * SPAN)
         for pair in range(HEADS // 2):
@@ -394,35 +413,34 @@
             stack_out[at, lo : lo + 2 * HEAD] = grad_q.astype(LOW)
             stack_out[at, D + lo : D + lo + 2 * HEAD] = grad_k.astype(LOW)
             stack_out[at, 2 * D + lo : 2 * D + lo + 2 * HEAD] = grad_v.astype(LOW)
-            vec_out[0:1, lanes] += jnp.sum(grad_q, axis=0, keepdims=True)
-            vec_out[1:2, lanes] += jnp.sum(grad_v, axis=0, keepdims=True)
-
-
-def unattend(after, part, parts, q, k, v, p, ga, stack=None):
+            vec_out[place : place + 1, lanes] += jnp.sum(grad_q, axis=0, keepdims=True)
+            vec_out[place + 1 : place + 2, lanes] += jnp.sum(grad_v, axis=0, keepdims=True)
+
+
+def unattend(after, part, parts, q, k, v, p, ga, stack=None, sums=()):
     total = q.shape[0]
     count = total // SPAN // parts
     first = part * count
     tall = lambda width: pl.BlockSpec((SPAN, width), lambda i: (first + i, 0))
     after = after if stack is None else [stack] + after
+    vec_shape = (12, D) if sums else (2, D)
     return pl.pallas_call(
-        unattend_kernel,
+        partial(unattend_kernel, len(after), bool(sums)),
         grid=(count,),
         in_specs=[ANY] * len(after)
         + [tall(D)] * 3
         + [
             pl.BlockSpec((1, HEADS // 2, SPAN, 2 * SPAN), lambda i: (first + i, 0, 0, 0)),
             tall(D),
-        ],
-        out_specs=[tall(3 * D), whole((2, D))],
-        out_shape=[
-far((total, 3 * D), LOW),
-            jax.ShapeDtypeStruct((2, D), F32),
-        ],
+        ]
+        + [whole(a.shape) for a in sums],
+        out_specs=[tall(3 * D), whole(vec_shape)],
+        out_shape=[far((total, 3 * D), LOW), jax.ShapeDtypeStruct(vec_shape, F32)],
         input_output_aliases={} if stack is None else {0: 0},
         compiler_params=params(),
         cost_estimate=cost(8),
         name="unattend",
-    )(*after, q, k, v, p, ga)
+    )(*after, q, k, v, p, ga, *sums)
 
 
 def input_kernel(*refs):
@@ -448,12 +466,15 @@
     )(*after, grad_one, stack, w_qkv)
 
 
-def contrast_kernel(slots, place, rows, counts, partners, loss_out, grad_out):
+def contrast_kernel(slots, masks, place, rows, counts, partners, loss_out, grad_out):
     total, scale = rows.shape[0], 2.0 * D ** (-0.5)
 
     def number(shape, axis):
         at = lax.broadcasted_iota(jnp.int32, shape, axis)
-        return (at // GROUP) ^ place[0], at % GROUP
+        device, block = jnp.full(shape, place[0], jnp.int32), at // GROUP
+        for bit, mask in enumerate(masks):
+            device = device ^ (((block >> bit) & 1) * mask)
+        return device, at % GROUP
 
     device, slot = number((counts.shape[1], total), 1)
     hit = lax.broadcasted_iota(jnp.int32, device.shape, 0) == device
@@ -467,13 +488,13 @@
     own_id = device * slots + slot
     hit = lax.broadcasted_iota(jnp.int32, own_id.shape, 1) == own_id
     pair = jnp.sum(jnp.where(hit, partners[...], 0.0), axis=1, keepdims=True)
-    device, slot = number((total, total), 0)
-    down = (device * slots + slot).astype(F32)
-    device, slot = number((total, total), 1)
-    across = (device * slots + slot).astype(F32)
+    device, slot = number((total, 128), 0)
+    down = (device * slots + slot).astype(F32)[:, :1]
+    device, slot = number((8, total), 1)
+    across, slot = (device * slots + slot).astype(F32)[:1], slot[:1]
     valid = live_across & (down != across)
     matched = jnp.where((slot < slots) & (pair == across), 1.0, 0.0)
-    anchor = jnp.where(live_down & (pair != down[:, :1]), 1.0, 0.0)
+    anchor = jnp.where(live_down & (pair != down), 1.0, 0.0)
     similar = dot(rows[...], rows[...], (1, 1)) * scale
     masked = jnp.where(valid, similar, -1e30)
     peak = jnp.max(masked, axis=1, keepdims=True)
@@ -490,8 +511,10 @@
 
 def contrast(cls_rows, span_count, pair_index, device, slots):
     total = cls_rows.shape[0]
+    scale = {"row": lax.axis_size("col"), "col": 1}
+    masks = [scale[name] * bit for name, bit in gather_steps()]
     return pl.pallas_call(
-        partial(contrast_kernel, slots),
+        partial(contrast_kernel, slots, masks),
         in_specs=[pl.BlockSpec(memory_space=pltpu.SMEM)]
         + [pl.BlockSpec(memory_space=pltpu.VMEM)] * 3,
         out_shape=[
@@ -510,33 +533,33 @@
 
 
 def adam_kernel(
-    packed, position, gathered, master, first, second, left, right,
-    master_out, first_out, second_out, low_out, *scratch,
+    packed, parts, position, *refs,
 ):
+    gathered = refs[:parts]
+    master, first, second, left, right, master_out, first_out, second_out, low_out, *scratch = refs[parts:]
     quarter = D // 4
     slot = pl.program_id(0)
     if packed:
         owned = scratch[0]
-        shares, tall, _ = gathered.shape
-        rows = D // shares
+        shares, tall, _ = gathered[0].shape
+        rows = D // (shares * parts)
 
         @pl.when(slot == 0)
         def _():
-            def place(share, carry):
-                block = gathered[share].astype(F32)
-                at = pl.multiple_of((share ^ position[0]) * rows, rows)
-                for index in range(owned.shape[0]):
-                    lo = index * rows % tall
-                    side = index * rows // tall
-                    piece = block[lo : lo + rows, side * quarter : (side + 1) * quarter]
-                    owned[index, pl.ds(at, rows), :] = piece
-                return carry
-
-            lax.fori_loop(0, shares, place, 0)
+            for part in range(parts):
+                for share in range(shares):
+                    block = gathered[part][share].astype(F32)
+                    number = part * shares + share
+                    at = pl.multiple_of((number ^ position[0]) * rows, rows)
+                    for index in range(owned.shape[0]):
+                        lo = index * rows % tall
+                        side = index * rows // tall
+                        piece = block[lo : lo + rows, side * quarter : (side + 1) * quarter]
+                        owned[index, pl.ds(at, rows), :] = piece
 
         gradient = owned[slot].astype(LOW)
     else:
-        gradient = gathered[0]
+        gradient = gathered[0][0]
     low_left, low_right = left[0], right[0].astype(LOW)
     turned = dot(gradient, low_left, (0, 0))
     turned = dot(low_right, turned.astype(LOW), (0, 0))
@@ -587,20 +610,21 @@
 
 def rotated_adam(position, gathered, master, first_moment, second_moment, left_basis, right_basis):
     per_owner, quarter, _ = master.shape
-    rows = D // gathered.shape[0]
+    rows = D // sum(part.shape[0] for part in gathered)
     packed = rows % 8 == 0 and per_owner % 2 == 0
     if not packed:
-        gathered = to_owned(gathered, position, per_owner)
+        gathered = [to_owned(jnp.concatenate(gathered), position, per_owner)]
     block = lambda a: pl.BlockSpec((1,) + a.shape[1:], lambda s, p: (s, 0, 0))
     operands = streamed(master, first_moment, second_moment, left_basis, right_basis)
     like = jax.ShapeDtypeStruct(operands[0].shape, F32)
-    fixed = pl.BlockSpec(gathered.shape, lambda s, p: (0, 0, 0))
+    fixed = pl.BlockSpec(gathered[0].shape, lambda s, p: (0, 0, 0))
     outputs = pl.pallas_call(
-        partial(adam_kernel, packed),
+        partial(adam_kernel, packed, len(gathered)),
         grid_spec=pltpu.PrefetchScalarGridSpec(
             num_scalar_prefetch=1,
             grid=(per_owner,),
-            in_specs=[fixed if packed else block(gathered)] + [block(a) for a in operands],
+            in_specs=[fixed if packed else block(part) for part in gathered]
+            + [block(a) for a in operands],
             out_specs=[block(operands[0])] * 4,
             scratch_shapes=[pltpu.VMEM((per_owner, D, quarter), F32)] if packed else [],
         ),
@@ -608,7 +632,7 @@
         compiler_params=params(28),
         cost_estimate=cost(20),
         name="adam",
-    )(position.reshape(1), gathered, *operands)
+    )(position.reshape(1), *gathered, *operands)
     return [turn(a) for a in outputs]
 
 
@@ -626,12 +650,13 @@
     return lax.ppermute(send, step[0], [(i, i ^ step[1]) for i in range(size)])
 
 
-def pick(array, index, dim):
-    return lax.dynamic_index_in_dim(array, index, dim, False)
+def gather_steps():
+    core, across, y_bits, z_bits = row_steps()
+    return z_bits[::-1] + y_bits + across + core
 
 
 def gather_all(rows):
-    for step in axis_bits("col") + axis_bits("row"):
+    for step in gather_steps():
         rows = jnp.concatenate([rows, swap(rows, step)])
     return rows
 
@@ -643,82 +668,149 @@
     return core, across, y_bits, z_bits
 
 
-def launch(part, step, left, rider=None):
-    dim = 1 + left.index(step)
-    bit = bit_of(step)
-    left.remove(step)
-    send, keep = pick(part, 1 - bit, dim), pick(part, bit, dim)
-    shape, flat = send.shape, send.reshape(-1, send.shape[-1])
-    message = flat
+def pack_rider(rider, rows, width):
+    parts = [rider[:, at : at + width] for at in range(0, D, width)]
+    tall = rider.shape[0]
+    if rows < tall:
+        return [part[at : at + rows] for part in parts for at in range(0, tall, rows)]
+    fold = rows // tall
+    parts += parts[-1:] * (-len(parts) % fold)
+    return [jnp.concatenate(parts[at : at + fold]) for at in range(0, len(parts), fold)]
+
+
+def unpack_rider(blocks, tall):
+    rows, width = blocks[0].shape
+    if rows < tall:
+        fold = tall // rows
+        parts = [jnp.concatenate(blocks[at : at + fold]) for at in range(0, len(blocks), fold)]
+    else:
+        parts = [block[at : at + tall] for block in blocks for at in range(0, rows, tall)]
+    parts = parts[: D // width]
+    return parts[0] if len(parts) == 1 else jnp.concatenate(parts, axis=1)
+
+
+def rider_blocks(rows, width, tall=12):
+    return -(-tall * D // (rows * width))
+
+
+def land_kernel(after, outs, rider, bits, *refs):
+    refs = refs[after:]
+    sides = len({source[0] for out in outs for source in out[3]})
+    keeps, others = refs[0 : 2 * sides : 2], refs[1 : 2 * sides : 2]
+    results = refs[2 * sides + (0 if rider is None else 1 + (rider == "array")) :]
     if rider is not None:
-        message = jnp.concatenate([flat, rider.astype(LOW).reshape(-1, flat.shape[1])])
-    other = swap(message, step)
-    arrived = other[: flat.shape[0]].reshape(shape)
-    if rider is not None:
-        rider = rider + other[flat.shape[0] :].reshape(rider.shape).astype(F32)
-    return message, partial(landed, keep, arrived), rider
-
-
-def landed(keep, other, tied=None):
-    total = keep.astype(F32) + other.astype(F32)
-    if tied is not None:
-        total += 0.0 * tied[(0,) * tied.ndim].astype(F32)
-    return total.astype(LOW)
-
-
-def begin_sum(send):
-    return swap(send, row_steps()[0][0])
+        total = refs[2 * sides][...]
+        tall = total.shape[0]
+        if rider == "array":
+            total += refs[2 * sides + 1][...]
+        else:
+            blocks = [others[0][at].astype(F32) for at in range(keeps[0].shape[0], others[0].shape[0])]
+            total += unpack_rider(blocks, tall)
+        results[-1][...] = total
+    for number, (at_bit, before, behind, sources) in enumerate(outs):
+        bit = bits[at_bit]
+        for which, target in enumerate(results[2 * number : 2 * number + 2]):
+            half = bit if which else 1 - bit
+            for at in range(before):
+                here = pl.ds((2 * at + half) * behind, behind)
+                there = slice(at * behind, (at + 1) * behind)
+                for side, lanes, into in sources:
+                    target[there, :, into] = keeps[side][here, :, lanes] + others[side][here, :, lanes]
+        if rider is not None and number == 0:
+            away = results[0]
+            count, rows, width = away.shape
+            blocks = pack_rider(total, rows, width)
+            for index, block in enumerate(blocks):
+                away[count - len(blocks) + index] = block.astype(LOW)
 
 
 class Reduction:
-    def __init__(self, other, keep, rider=None):
+    def __init__(self, bits, ways, send, keep, rider=None):
         core, across, y_bits, z_bits = row_steps()
+        self.bits, self.order = bits, core + across + y_bits + z_bits
         left = across + y_bits + z_bits
-        part = landed(keep, other)
-        self.rider = rider if rider is None else rider + swap(rider, core[0])
-        width = part.shape[1] >> len(left)
-        part = part.reshape(part.shape[:1] + (2,) * len(left) + (width, D))
-        self.steps = list(zip(across + y_bits, y_bits + across)) + [(step,) for step in z_bits]
-        self.parts = [part[..., : D // 2], part[..., D // 2 :]]
-        self.left = [list(left), list(left)]
-        self.start()
-
-    def start(self):
-        if not self.steps:
-            self.moves = None
-            return
-        steps = self.steps.pop(0)
-        if len(steps) < len(self.parts):
-            self.parts, self.left = [jnp.concatenate(self.parts, axis=-1)], self.left[:1]
-        self.moves = []
-        for side, step in enumerate(steps):
-            rider = self.rider if side == 0 else None
-            self.moves.append(launch(self.parts[side], step, self.left[side], rider))
+        self.panels, height, _ = keep.shape
+        self.rows = height >> len(left)
+        other = swap(send, core[0])
+        self.rider = None if rider is None else (rider, swap(rider, core[0]))
+        split = lambda a: a.reshape(-1, self.rows, D)
+        self.sides = [(split(keep), split(other), left)]
+        cycle = [across, y_bits, z_bits[:1]][:ways]
+        orders = [sum(cycle[at:] + cycle[:at], []) for at in range(ways)]
+        self.stages = list(zip(*orders)) + [(step,) for step in z_bits[ways - 2 :]]
+        self.ways = ways
+        self.messages = []
 
     def sent(self):
-        return [move[0] for move in self.moves or ()]
-
-    def land(self, tied=None):
-        self.parts = [land(tied) for _, land, _ in self.moves]
-        self.rider = self.moves[0][2]
-        self.start()
+        return self.messages
+
+    def landing(self):
+        return [side[1] for side in self.sides]
+
+    def land(self, *after):
+        stage = self.stages.pop(0)
+        outs, shapes, lefts = [], [], []
+        part = D // self.ways
+        lanes = [slice(at, at + part) for at in range(0, D, part)]
+        for index, step in enumerate(stage):
+            if len(self.sides) == len(stage):
+                width = self.sides[index][0].shape[2]
+                sources = [(index, slice(0, width), slice(0, width))]
+                left = self.sides[index][2]
+            elif len(stage) > 1:
+                width, left = part, self.sides[0][2]
+                sources = [(0, lanes[index], slice(0, part))]
+            else:
+                width, left = D, self.sides[0][2]
+                sources = [(side, slice(0, part), lanes[side]) for side in range(self.ways)]
+            dim = left.index(step)
+            behind = 1 << (len(left) - dim - 1)
+            before = self.panels << dim
+            outs.append((self.order.index(step), before, behind, sources))
+            extra = rider_blocks(self.rows, width) if self.rider and index == 0 else 0
+            shapes += [(before * behind + extra, self.rows, width), (before * behind, self.rows, width)]
+            lefts.append([other for other in left if other != step])
+        rider = None if self.rider is None else ("array" if len(self.rider) == 2 else "message")
+        inputs = [a for keep, other, _ in self.sides for a in (keep, other)] + list(self.rider or ())
+        out_shape = [jax.ShapeDtypeStruct(shape, LOW) for shape in shapes]
+        if rider:
+            out_shape.append(jax.ShapeDtypeStruct(self.rider[0].shape, F32))
+        results = pl.pallas_call(
+            partial(land_kernel, len(after), outs, rider),
+            in_specs=[SMEM] + [ANY] * len(after) + [pl.BlockSpec(memory_space=pltpu.VMEM)] * len(inputs),
+            out_shape=out_shape,
+            compiler_params=params(24),
+            cost_estimate=cost(2),
+            name="land",
+        )(self.bits, *after, *inputs)
+        if rider:
+            self.rider = (results[-1],)
+        self.messages = list(results[0 : 2 * len(stage) : 2])
+        keeps = results[1 : 2 * len(stage) : 2]
+        self.sides = [
+            (keep, swap(message, step), left)
+            for keep, message, step, left in zip(keeps, self.messages, stage, lefts)
+        ]
 
     def finish(self):
-        while self.moves:
+        while self.stages:
             self.land()
-        return self.parts[0]
-
-
-def slots_kernel(cols, after, owners, *refs):
-    parts, out, blocks, packed = refs[after:-3], refs[-3], refs[-2], refs[-1]
+
+
+def slots_kernel(cols, panels, bits, owners, *refs):
+    sums, rider = refs[:6], refs[6]
+    away, here, rider_out, blocks, packed = refs[7:]
     quarter = D // 4
+    found = [(sums[2 * run], sums[2 * run + 1], i) for run in range(3) for i in range(sums[2 * run].shape[0])]
     at = 0
-    for part in parts:
-        for panel in range(part.shape[0]):
-            value = part[panel].astype(F32)
-            for index in range(4):
-                blocks[at] = value[:, index * quarter : (index + 1) * quarter]
-                at += 1
+    for panel in panels:
+        keep, other, index = found[panel]
+        value = keep[index].astype(F32) + other[index].astype(F32)
+        for part in range(4):
+            blocks[at] = value[:, part * quarter : (part + 1) * quarter]
+            at += 1
+    tail = [sums[1][index].astype(F32) for index in range(sums[0].shape[0], sums[1].shape[0])]
+    rider_out[...] = rider[...] + unpack_rider(tail, rider.shape[0])
     rows, half = blocks.shape[1], packed.shape[1]
     for slot in range(at):
         col, place = divmod(slot, at // cols)
@@ -729,43 +821,74 @@
             if lo < hi:
                 lanes = slice(side * quarter, (side + 1) * quarter)
                 packed[col, lo - side * half : hi - side * half, lanes] = value[lo - first : hi - first]
-    out[...] = packed[...].astype(LOW)
-
-
-def to_slots(after, parts, owner_list):
+    bit = bits[bits.shape[0] - 1]
+    count = cols // 2
+    away[...] = packed[pl.ds((1 - bit) * count, count)].astype(LOW)
+    here[...] = packed[pl.ds(bit * count, count)].astype(LOW)
+
+
+def to_slots(bits, runs, panels, owner_list):
     quarter, cols = D // 4, lax.axis_size("col")
-    panels, rows = sum(part.shape[0] for part in parts), parts[0].shape[1]
-    shape = (cols, panels * 4 // cols * rows // 2, 2 * quarter)
+    arrays = [a for run in runs for a in run.sides[0][:2]]
+    rows = runs[0].rows
+    shape = (cols, len(panels) * 4 // cols * rows // 2, 2 * quarter)
+    like = jax.ShapeDtypeStruct((cols // 2,) + shape[1:], LOW)
+    rider = runs[0].rider[0]
     return pl.pallas_call(
-        partial(slots_kernel, cols, len(after)),
-        in_specs=[SMEM] + [ANY] * len(after) + [pl.BlockSpec(memory_space=pltpu.VMEM)] * len(parts),
-        out_shape=jax.ShapeDtypeStruct(shape, LOW),
-        scratch_shapes=[pltpu.VMEM((panels * 4, rows, quarter), F32), pltpu.VMEM(shape, F32)],
-        compiler_params=params(),
+        partial(slots_kernel, cols, panels),
+        in_specs=[SMEM, SMEM] + [pl.BlockSpec(memory_space=pltpu.VMEM)] * 7,
+        out_shape=[like, like, jax.ShapeDtypeStruct(rider.shape, F32)],
+        scratch_shapes=[pltpu.VMEM((len(panels) * 4, rows, quarter), F32), pltpu.VMEM(shape, F32)],
+        compiler_params=params(24),
         cost_estimate=cost(4),
         name="slots",
-    )(owner_list, *after, *parts)
-
-
-def spread(slots, beside):
+    )(bits, owner_list, *arrays, rider)
+
+
+def regroup_kernel(after, at_bit, before, behind, bits, *refs):
+    parts, (away, here) = refs[after:-2], refs[-2:]
+    bit = bits[at_bit]
+    for which, target in ((1 - bit, away), (bit, here)):
+        to = 0
+        for part in parts:
+            for at in range(before):
+                target[to : to + behind] = part[pl.ds((2 * at + which) * behind, behind)]
+                to += behind
+
+
+def regroup(bits, at_bit, after, parts, before, behind):
+    count, tall, width = parts[0].shape
+    like = jax.ShapeDtypeStruct((count * len(parts) // 2, tall, width), LOW)
+    return pl.pallas_call(
+        partial(regroup_kernel, len(after), at_bit, before, behind),
+        in_specs=[SMEM] + [ANY] * len(after) + [pl.BlockSpec(memory_space=pltpu.VMEM)] * len(parts),
+        out_shape=[like, like],
+        compiler_params=params(24),
+        cost_estimate=cost(2),
+        name="regroup",
+    )(bits, *after, *parts)
+
+
+def spread(bits, away, here, beside):
     core, across, y_bits, z_bits = row_steps()
-    tail = slots.shape[1:]
+    order = core + across + y_bits + z_bits
     left = axis_bits("col")[::-1]
-    part = slots.reshape((1,) + (2,) * len(left) + tail)
-    made = []
+    made, shares = [], 1
     for step in (y_bits + z_bits)[::-1]:
-        dim = 1 + left.index(step)
-        bit = bit_of(step)
-        send, keep = pick(part, 1 - bit, dim), pick(part, bit, dim)
-        other = swap(send, step)
+        dim = left.index(step)
+        if shares > 1:
+            after = streamed(*made[-1:]) if len(made) == shares.bit_length() - 1 else []
+            behind = 1 << (len(left) - dim - 1)
+            before = shares // 2 << dim
+            away, here = regroup(bits, order.index(step), after, parts, before, behind)
+        left.remove(step)
+        parts = [here, swap(away, step)]
         if len(made) < len(beside):
-            made.append(beside[len(made)]([send] + made[-1:]))
-            keep += (0.0 * made[-1][(0,) * made[-1].ndim]).astype(LOW)
-        part = jnp.concatenate([keep, other])
-        left.remove(step)
+            made.append(beside[len(made)]([away] + streamed(*made[-1:])))
+        shares *= 2
     for step in (core + across)[::-1]:
-        part = jnp.concatenate([part, swap(part, step)])
-    return part, made
+        parts = parts + [swap(part, step) for part in parts]
+    return parts, made
 
 
 def row_place():
@@ -799,12 +922,12 @@
     device = (lax.axis_index("row") * lax.axis_size("col") + lax.axis_index("col")).reshape(1)
     core, across, y_bits, z_bits = row_steps()
     core_bit = bit_of(core[0])
+    bits = jnp.stack([bit_of(step) for step in core + across + y_bits + z_bits])
     rows = vectors.reshape(1, -1)
     q, k, v, p, attended = attend(tokens, w_qkv, rows)
-    encoded, hidden, slope, normed_low, unit_one, inverse_one, unit_two, inverse_two = feed(
-        device, span_count, tokens, attended, w_attn_out, w_in, w_out, rows
-    )
-    cls_rows = jnp.pad(encoded.reshape(slots, SPAN, D)[:, 0], ((0, GROUP - slots), (0, 0)))
+    encoded, hidden, slope, normed_low, unit_one, inverse_one, unit_two, inverse_two, cls_rows = (
+        feed(device, span_count, tokens, attended, w_attn_out, w_in, w_out, rows)
+    )
     loss, grad_cls = contrast(gather_all(cls_rows), span_count, pair_index, device, slots)
     grad_two, outer_low, vec_two = outer_grad(
         device, span_count, out_grad, grad_cls, unit_two, inverse_two, rows
@@ -812,7 +935,8 @@
     outer_args = (hidden, outer_low, FF // D, True)
     outer_away = weight_half(8, [], 1 - core_bit, *outer_args)
     outer_here = weight_half(60, [outer_away], core_bit, *outer_args)
-    outer_run = Reduction(begin_sum(outer_away), outer_here)
+    outer_run = Reduction(bits, 2, outer_away, outer_here)
+    outer_run.land()
     pre_low, grad_one, mixed_low, grad_attended, vec_one = inner_grad(
         outer_run.sent(), outer_low, grad_two, slope, unit_one, inverse_one,
         w_attn_out, w_in, w_out, rows,
@@ -823,41 +947,40 @@
     outer_run.land(inner_away)
     inner_here = weight_half(60, [inner_away] + outer_run.sent(), core_bit, *inner_args)
     outer_run.land(inner_here)
-    inner_run = Reduction(begin_sum(inner_away), inner_here)
+    inner_run = Reduction(bits, 3, inner_away, inner_here)
+    inner_run.land()
     early, vec_early = unattend(
         outer_run.sent() + inner_run.sent(), 0, 2, q, k, v, p, grad_attended
     )
-    outer_run.land(vec_early)
-    stack_low, vec_late = unattend([], 1, 2, q, k, v, p, grad_attended, early)
-    inner_run.land(vec_late)
+    stack_low, vec_grad = unattend(
+        [], 1, 2, q, k, v, p, grad_attended, early, (vec_one, vec_two, vec_early)
+    )
+    inner_run.land(vec_grad)
     project_args = (tokens, stack_low, 3, False)
-    project_away = weight_half(8, inner_run.sent(), 1 - core_bit, *project_args)
+    project_away = weight_half(
+        8, inner_run.sent() + outer_run.landing(), 1 - core_bit, *project_args
+    )
     project_here = weight_half(60, [project_away], core_bit, *project_args)
     inner_run.land(project_here)
-    vec_heads = vec_early + vec_late
-    grad_vector = jnp.concatenate(
+    project_run = Reduction(bits, 3, project_away, project_here, vec_grad)
+    project_run.land()
+    inner_run.land()
+    project_run.land()
+    for run in (outer_run, inner_run, project_run):
+        run.finish()
+    slots_away, slots_here, vec_grad = to_slots(
+        bits, (project_run, inner_run, outer_run), (0, 1, 2, 7, 3, 4, 5, 6, 8, 9, 10, 11), owner_list
+    )
+    vec_grad = vec_grad.reshape(-1)
+    gathered, (low_left, grad_tokens) = spread(
+        bits,
+        slots_away,
+        slots_here,
         [
-            jnp.stack([vec_one[0], vec_two[0], vec_one[1], vec_two[1]]),
-            vec_heads,
-            jnp.stack([vec_one[2], vec_two[2]]),
-            vec_one[3:],
-        ]
-    )
-    project_run = Reduction(begin_sum(project_away), project_here, grad_vector)
-    grad_tokens = input_grad(
-        inner_run.sent() + project_run.sent(), grad_one, stack_low, w_qkv
-    )
-    project_run.land(grad_tokens)
-    inner_run.land(grad_tokens)
-    outer_sum, inner_sum, project_sum = (
-        run.finish() for run in (outer_run, inner_run, project_run)
-    )
-    vec_grad = project_run.rider
-    parts = (project_sum, inner_sum[-1:], inner_sum[:-1], outer_sum)
-    gathered, (low_left,) = spread(
-        to_slots([], parts, owner_list), [lambda after: ready(after, left_basis, LOW)]
-    )
-    vec_grad = vec_grad.reshape(-1)
+            lambda after: ready(after, left_basis, LOW),
+            lambda after: input_grad(after, grad_one, stack_low, w_qkv),
+        ],
+    )
     new_master, new_first, new_second, master_copy = rotated_adam(
         row_place(), gathered, turn(master), turn(first_moment), turn(second_moment),
         low_left, right_basis,

time: 237 us -> 219 us (0.924)
  waiting for transfers between devices: 59 us -> 46.9 us
  other arithmetic: 10.5 us -> 0.68 us
  starting transfers between devices: 37.5 us -> 45.2 us
  Pallas kernels: 113 us -> 120 us
  between operations: 6.97 us -> 1.15 us
  local copies, waits for them, and re-layouts: 9.92 us -> 4.46 us
    ppermute x32 -> x44, waiting for transfers between devices: 59 us -> 46.9 us  [swap(): return lax.ppermute(send, step[0], [(i, i ^ step[1]) for i in range(size)])]
    convert_element_type x26 -> x0, other arithmetic: 8.31 us -> none  [the longest x20 8.26 us: landed(): return total.astype(LOW)]
    ppermute x32 -> x44, starting transfers between devices: 37.5 us -> 45.2 us  [swap(): return lax.ppermute(send, step[0], [(i, i ^ step[1]) for i in range(size)])]
    slice x21 -> x0, local copies, waits for them, and re-layouts: 7.51 us -> none  [the longest x7 4.27 us: landed(): total += 0.0 * tied[(0,) * tied.ndim].astype(F32)]
    pallas_call x5 -> x19, Pallas kernels: 33.3 us -> 40.4 us  [the longest x1 14.9 us: rotated_adam(): pl.pallas_call(partial(adam_kernel, packed, len(gathered)), grid_spec=plt...]
    unnamed x53 -> x54, local copies, waits for them, and re-layouts: 0.23 us -> 4.35 us
  transfers between devices with their start and end apart: 32 -> 44, of which waited for: 22 -> 25; matrix products, arithmetic and copies ran while one was open for 7% -> 0% of each run, Pallas kernels for 25% -> 29%
where the time goes in v1:
time: 219 us
  Pallas kernels  120 us (55%)
  waiting for transfers between devices  46.9 us (21%)
  starting transfers between devices  45.2 us (21%)
  local copies, waits for them, and re-layouts  4.46 us (2%)
    ppermute x44, waiting for transfers between devices, swap(): return lax.ppermute(send, step[0], [(i, i ^ step[1]) for i in range(size)])  46.9 us
    ppermute x44, starting transfers between devices, swap(): return lax.ppermute(send, step[0], [(i, i ^ step[1]) for i in range(size)])  45.2 us
    pallas_call x1, Pallas kernels, feed(): pl.pallas_call(feed_kernel, grid=(FF // D,), in_specs=[SMEM, SMEM, tall(D...  19.4 us
    pallas_call x6, Pallas kernels, weight_half(): pl.pallas_call(partial(weight_kernel, panels, len(after)), grid_spec=pltp...  19.1 us
    pallas_call x1, Pallas kernels, inner_grad(): pl.pallas_call(partial(inner_kernel, len(after)), grid=(bands,), in_specs...  15.6 us
    pallas_call x1, Pallas kernels, rotated_adam(): pl.pallas_call(partial(adam_kernel, packed, len(gathered)), grid_spec=plt...  14.9 us
    pallas_call x2, Pallas kernels, unattend(): pl.pallas_call(partial(unattend_kernel, len(after), bool(sums)), grid=(co...  13.8 us
    pallas_call x1, Pallas kernels, attend(): pl.pallas_call(attend_kernel, grid=(total // TALL,), in_specs=[tall, whol...  10.4 us
  transfers between devices with their start and end apart: 44, of which 25 were waited for; matrix products, arithmetic and copies ran while one was open for 0% of the time, Pallas kernels for 29%

profile of v1, /device:TPU:0, one launch (start us, length us, event | category | flops | bytes accessed | tf_op | source)
XLA Modules:
  0.0 218.8 jit_solution(9757313207291673800)
XLA Ops:
  0.7 10.4 %attend.1 = (bf16[768,768]{1,0:T(8,128)(2,1)}, bf16[768,768]{1,0:T(8,128)(2,1)}, bf16[768,768]{1,0:T(8,128)(2,1)}, bf16[6,6,128,256]{3,2,1,0:T(8,128)(2,1)}, bf16[768,768]{1,0:T(8,128)(2,1)S(1)}) custom-call(bf16[768,768]{1,0:T(8,128)(2,1)} %refs_1_.2, bf16[3,768,768]{2,1,0:T(8,128)(2,1)} %refs_4_.3, f32[1,9216]{1,0:T(1,128)} %bitcast.26), custom_call_target="tpu_custom_call" | custom-call | flops 11000000512 | tf_op jit(solution)/shard_map/attend/pallas_call | solution.py:103
  11.1 19.4 %feed.1 = (bf16[768,768]{1,0:T(8,128)(2,1)}, bf16[768,3072]{1,0:T(8,128)(2,1)}, bf16[768,3072]{1,0:T(8,128)(2,1)}, bf16[768,768]{1,0:T(8,128)(2,1)}, bf16[768,76...) custom-call(s32[1]{0:T(128)} %bitcast.place, ...), custom_call_target="tpu_custom_call" | custom-call | flops 22000001024 | tf_op jit(solution)/shard_map/feed/pallas_call | solution.py:190
  30.5 4.1 %collective-permute-start = (bf16[8,768]{1,0:T(8,128)(2,1)S(1)}, bf16[8,768]{1,0:T(8,128)(2,1)S(1)}, u32[]{:S(2)}, u32[]{:S(2)}) collective-permute-start(bf16[8,768]{1,0:T(8,128)(2,1)S(1)} %get-tuple-element.108), channel_id=1, source_target_pairs={{0,4},{1,5},{2,6},{3,7},{4,0},{5,1},{6,2},{7,3},{8,12},{9,13},{10,... | collective-permute-start | bytes 36872 | tf_op jit(solution)/shard_map/ppermute | solution.py:650
  36.3 1.9 collective-permute-start.1
  38.2 1.9 collective-permute-done.1
  40.1 1.9 collective-permute-start.2
  42.0 2.2 %collective-permute-done.2 = bf16[32,768]{1,0:T(8,128)(2,1)S(1)} collective-permute-done((bf16[32,768]{1,0:T(8,128)(2,1)S(1)}, bf16[32,768]{1,0:T(8,128)(2,1)S(1)}, u32[]{:S(2)}, u32[]{:S(2)}) %collective-permute-start.2) | collective-permute-done | bytes 49184 | tf_op jit(solution)/shard_map/ppermute | solution.py:650
  44.2 1.9 collective-permute-start.3
  46.1 2.8 %collective-permute-done.3 = bf16[64,768]{1,0:T(8,128)(2,1)S(1)} collective-permute-done((bf16[64,768]{1,0:T(8,128)(2,1)S(1)}, bf16[64,768]{1,0:T(8,128)(2,1)S(1)}, u32[]{:S(2)}, u32[]{:S(2)}) %collective-permute-start.3) | collective-permute-done | bytes 98336 | tf_op jit(solution)/shard_map/ppermute | solution.py:650
  51.8 2.2 %outer.1 = (f32[768,768]{1,0:T(8,128)S(1)}, bf16[768,768]{1,0:T(8,128)(2,1)S(1)}, f32[3,768]{1,0:T(4,128)S(1)}) custom-call(s32[1]{0:T(128)} %bitcast.place, s32[32]{0:T(128)S(1)} %copy-done.5, bf16[768,768]{1,0:T(8,128)(2,1)S(1)} %copy-done.3, f32[8,768]{1,0:T(8,128)S(1)} %get-tuple-element.109.grad_cls, bf16[768,768]{1,0:T(8,128)(2,1)S(1)} %get-tuple-element.110.unit_two, ...), custom_call_target="tpu_custom_call" | custom-call | flops 5500000256 | tf_op jit(solution)/shard_map/outer/pallas_call | solution.py:251
  54.0 3.1 %weight.6.refs_0_ = bf16[4,384,768]{2,1,0:T(8,128)(2,1)S(1)} custom-call(s32[1]{0:T(128)} %bitcast.7.side, bf16[768,3072]{1,0:T(8,128)(2,1)S(1)} %bitcast.39, bf16[768,768]{1,0:T(8,128)(2,1)S(1)} %get-tuple-element.112.refs_1_.refs_2_), custom_call_target="tpu_custom_call" | custom-call | flops 8800000000 | tf_op jit(solution)/shard_map/weight/pallas_call | solution.py:288
  57.4 3.3 %weight.7 = bf16[4,384,768]{2,1,0:T(8,128)(2,1)S(1)} custom-call(s32[1]{0:T(128)} %bitcast.2.side, bf16[4,384,768]{2,1,0:T(8,128)(2,1)S(1)} %weight.6.refs_0_, bf16[768,3072]{1,0:T(8,128)(2,1)S(1)} %bitcast.39, bf16[768,768]{1,0:T(8,128)(2,1)S(1)} %get-tuple-element.112.refs_1_.refs_2_), custom_call_target="tpu_custom_call" | custom-call | flops 65999998976 | tf_op jit(solution)/shard_map/weight/pallas_call | solution.py:288
  62.7 1.9 collective-permute-start.6
  66.1 15.6 %inner.1 = (bf16[768,3072]{1,0:T(8,128)(2,1)S(1)}, f32[768,768]{1,0:T(8,128)}, bf16[768,768]{1,0:T(8,128)(2,1)S(1)}, bf16[768,768]{1,0:T(8,128)(2,1)S(1)}, f32[7,768]{1,0:T(8,128)S(1)}) custom-call(bf16[32,24,384]{2,1,0:T(8,128)(2,1)S(1)} %get-tuple-element.113.refs_0_, bf16[32,24,384]{2,1,0:T(8,128)(2,1)S(1)} %get-tuple-element.114.refs_1_, ...), custom_call_target="tpu_custom_call" | custom-call | flops 17600000000 | tf_op jit(solution)/shard_map/inner/pallas_call | solution.py:348
  85.1 4.0 %weight.8.refs_0_ = bf16[5,384,768]{2,1,0:T(8,128)(2,1)S(1)} custom-call(s32[1]{0:T(128)} %bitcast.7.side, bf16[16,24,384]{2,1,0:T(8,128)(2,1)S(1)} %get-tuple-element.122.refs_0_, bf16[16,24,384]{2,1,0:T(8,128)(2,1)S(1)} %get-tuple-element.123.refs_1_, bf16[768,768]{1,0:T(8,128)(2,1)S(1)} %copy-done.14, bf16[768,3072]{1,0:T(8,128)(2,1)S(1)} %get-tuple-element.125.refs_3_, ...), custom_call_target="tpu_custom_call" | custom-call | flops 8800000000 | tf_op jit(solution)/shard_map/weight/pallas_call | solution.py:288
  89.2 2.0 collective-permute-done.8.refs_2_
  93.7 3.9 %weight.9.refs_0_ = bf16[5,384,768]{2,1,0:T(8,128)(2,1)S(1)} custom-call(s32[1]{0:T(128)} %bitcast.2.side, bf16[5,384,768]{2,1,0:T(8,128)(2,1)S(1)} %weight.8.refs_0_, bf16[8,24,768]{2,1,0:T(8,128)(2,1)S(1)} %get-tuple-element.129.refs_1_, bf16[768,768]{1,0:T(8,128)(2,1)S(1)} %copy-done.14, bf16[768,3072]{1,0:T(8,128)(2,1)S(1)} %copy-done.10, ...), custom_call_target="tpu_custom_call" | custom-call | flops 65999998976 | tf_op jit(solution)/shard_map/weight/pallas_call | solution.py:288
  100.0 2.6 %collective-permute-start.15 = (bf16[4,24,768]{2,1,0:T(8,128)(2,1)S(1)}, bf16[4,24,768]{2,1,0:T(8,128)(2,1)S(1)}, u32[]{:S(2)}, u32[]{:S(2)}) collective-permute-start(bf16[4,24,768]{2,1,0:T(8,128)(2,1)S(1)} %get-tuple-element.131.refs_0_), channel_id=1, source_target_pairs={{0,4},{1,5},{2,6},{3,7},{4,0},{5,1},{6,2},{7,3},{8,12},{9,13},{10,... | collective-permute-start | bytes 442376 | tf_op jit(solution)/shard_map/ppermute | solution.py:650
  107.2 6.9 %unattend.2 = (bf16[768,2304]{1,0:T(8,128)(2,1)}, f32[2,768]{1,0:T(2,128)S(1)}) custom-call(bf16[4,24,768]{2,1,0:T(8,128)(2,1)S(1)} %get-tuple-element.131.refs_0_, bf16[40,24,256]{2,1,0:T(8,128)(2,1)S(1)} %get-tuple-element.132.refs_1_, bf16[40,24,256]{2,1,0:T(8,128)(2,1)S(1)} %get-tuple-element.133.refs_2_, ...), custom_call_target="tpu_custom_call" | custom-call | flops 8800000000 | tf_op jit(solution)/shard_map/unattend/pallas_call | solution.py:427
  114.1 6.9 %unattend.3 = (bf16[768,2304]{1,0:T(8,128)(2,1)}, f32[12,768]{1,0:T(8,128)S(1)}) custom-call(bf16[768,2304]{1,0:T(8,128)(2,1)} %get-tuple-element.140.refs_0_, bf16[768,768]{1,0:T(8,128)(2,1)S(1)} %copy-done.15, bf16[768,768]{1,0:T(8,128)(2,1)S(1)} %copy-done.16, bf16[768,768]{1,0:T(8,128)(2,1)S(1)} %copy-done.17, ...), custom_call_target="tpu_custom_call", output_to_operand_aliasing={{0}: (0, {})} | custom-call | flops 8800000000 | tf_op jit(solution)/shard_map/unattend/pallas_call | solution.py:427
  123.4 2.4 %weight.10.refs_0_ = bf16[3,384,768]{2,1,0:T(8,128)(2,1)S(1)} custom-call(s32[1]{0:T(128)} %bitcast.7.side, bf16[20,24,256]{2,1,0:T(8,128)(2,1)S(1)} %get-tuple-element.147.refs_0_, bf16[20,24,256]{2,1,0:T(8,128)(2,1)S(1)} %get-tuple-element.148.refs_1_, bf16[20,24,256]{2,1,0:T(8,128)(2,1)S(1)} %get-tuple-element.149.refs_2_, ...), custom_call_target="tpu_custom_call" | custom-call | flops 8800000000 | tf_op jit(solution)/shard_map/weight/pallas_call | solution.py:288
  126.3 2.4 %weight.11.refs_0_ = bf16[3,384,768]{2,1,0:T(8,128)(2,1)S(1)} custom-call(s32[1]{0:T(128)} %bitcast.2.side, bf16[3,384,768]{2,1,0:T(8,128)(2,1)S(1)} %weight.10.refs_0_, bf16[768,768]{1,0:T(8,128)(2,1)S(1)} %copy-done.4, bf16[768,2304]{1,0:T(8,128)(2,1)S(1)} %copy-done.7), custom_call_target="tpu_custom_call" | custom-call | flops 65999998976 | tf_op jit(solution)/shard_map/weight/pallas_call | solution.py:288
  136.0 4.3 %collective-permute-done.19.refs_3_ = bf16[24,24,256]{2,1,0:T(8,128)(2,1)S(1)} collective-permute-done((bf16[24,24,256]{2,1,0:T(8,128)(2,1)S(1)}, bf16[24,24,256]{2,1,0:T(8,128)(2,1)S(1)}, u32[]{:S(2)}, u32[]{:S(2)}) %collective-permute-start.19) | collective-permute-done | bytes 294944 | tf_op jit(solution)/shard_map/ppermute | solution.py:650
  145.6 2.1 collective-permute-done.29.refs_4_
  158.1 2.0 collective-permute-done.24.refs_1_
  161.2 7.8 %collective-permute-done.34.refs_3_ = bf16[5,24,768]{2,1,0:T(8,128)(2,1)S(1)} collective-permute-done((bf16[5,24,768]{2,1,0:T(8,128)(2,1)S(1)}, bf16[5,24,768]{2,1,0:T(8,128)(2,1)S(1)}, u32[]{:S(2)}, u32[]{:S(2)}) %collective-permute-start.34) | collective-permute-done | bytes 184352 | tf_op jit(solution)/shard_map/ppermute | solution.py:650
  171.8 9.0 %ready.1.refs_0_.refs_1_.refs_11_ = bf16[6,768,768]{2,1,0:T(8,128)(2,1)} custom-call(bf16[4,72,384]{2,1,0:T(8,128)(2,1)S(1)} %get-tuple-element.187.refs_0_, f32[6,768,768]{2,1,0:T(8,128)} %refs_1_.3), custom_call_target="tpu_custom_call" | custom-call | flops 4400000000 | tf_op jit(solution)/shard_map/ready/pallas_call | solution.py:586
  183.7 4.3 %input.1.refs_0_ = f32[768,768]{1,0:T(8,128)} custom-call(bf16[4,72,384]{2,1,0:T(8,128)(2,1)S(1)} %get-tuple-element.189.refs_0_, bf16[6,768,768]{2,1,0:T(8,128)(2,1)} %ready.1.refs_0_.refs_1_.refs_11_, f32[768,768]{1,0:T(8,128)S(1)} %copy-done.8, bf16[768,2304]{1,0:T(8,128)(2,1)S(1)} %copy-done.7, bf16[3,768,768]{2,1,0:T(8,128)(2,1)S(1)} %copy-done.2), custom_call_target="tpu_custom_call" | custom-call | flops 8800000000 | tf_op jit(solution)/shard_map/input/pallas_call | solution.py:457
  189.2 2.2 %collective-permute-start.37 = (bf16[4,72,384]{2,1,0:T(8,128)(2,1)S(1)}, bf16[4,72,384]{2,1,0:T(8,128)(2,1)S(1)}, u32[]{:S(2)}, u32[]{:S(2)}) collective-permute-start(bf16[4,72,384]{2,1,0:T(8,128)(2,1)S(1)} %get-tuple-element.194), channel_id=1, source_target_pairs={{0,1},{1,0},{2,3},{3,2},{4,5},{5,4},{6,7},{7,6},{8,9},{9,8},{10,11... | collective-permute-start | bytes 663560 | tf_op jit(solution)/shard_map/ppermute | solution.py:650
  192.5 3.7 %collective-permute-done.37.refs_1_ = bf16[4,72,384]{2,1,0:T(8,128)(2,1)S(1)} collective-permute-done((bf16[4,72,384]{2,1,0:T(8,128)(2,1)S(1)}, bf16[4,72,384]{2,1,0:T(8,128)(2,1)S(1)}, u32[]{:S(2)}, u32[]{:S(2)}) %collective-permute-start.37) | collective-permute-done | bytes 221216 | tf_op jit(solution)/shard_map/ppermute | solution.py:650
  197.9 4.5 %collective-permute-done.39.refs_3_ = bf16[4,72,384]{2,1,0:T(8,128)(2,1)S(1)} collective-permute-done((bf16[4,72,384]{2,1,0:T(8,128)(2,1)S(1)}, bf16[4,72,384]{2,1,0:T(8,128)(2,1)S(1)}, u32[]{:S(2)}, u32[]{:S(2)}) %collective-permute-start.39) | collective-permute-done | bytes 221216 | tf_op jit(solution)/shard_map/ppermute | solution.py:650
  203.9 14.9 %adam.1 = (f32[6,192,768]{2,1,0:T(8,128)}, f32[6,192,768]{2,1,0:T(8,128)}, f32[6,192,768]{2,1,0:T(8,128)}, bf16[6,192,768]{2,1,0:T(8,128)(2,1)}) custom-call(s32[1]{0:T(128)} %bitcast.17.position, bf16[4,72,384]{2,1,0:T(8,128)(2,1)S(1)} %get-tuple-element.193.refs_0_, bf16[4,72,384]{2,1,0:T(8,128)(2,1)S(1)} %collective-permute-done.37.refs_1_, ...), custom_call_target="tpu_custom_call" | custom-call | flops 22000001024 | tf_op jit(solution)/shard_map/adam/pallas_call | solution.py:621
  (152 shorter events, 59.1 us)
Async XLA Ops:
  30.5 5.8 %collective-permute-start = (bf16[8,768]{1,0:T(8,128)(2,1)S(1)}, bf16[8,768]{1,0:T(8,128)(2,1)S(1)}, u32[]{:S(2)}, u32[]{:S(2)}) collective-permute-start(bf16[8,768]{1,0:T(8,128)(2,1)S(1)} %get-tuple-element.108), channel_id=1, source_target_pairs={{0,4},{1,5},{2,6},{3,7},{4,0},{5,1},{6,2},{7,3},{8,12},{9,13},{10,... | collective-permute-start | bytes 36872 | tf_op jit(solution)/shard_map/ppermute | solution.py:650
  62.7 19.1 %collective-permute-start.6 = (bf16[32,24,384]{2,1,0:T(8,128)(2,1)S(1)}, bf16[32,24,384]{2,1,0:T(8,128)(2,1)S(1)}, u32[]{:S(2)}, u32[]{:S(2)}) collective-permute-start(bf16[32,24,384]{2,1,0:T(8,128)(2,1)S(1)} %get-tuple-element.113.refs_0_), channel_id=1, source_target_pairs={{0,16},{8,24},{16,0},{24,8},{1,17},{9,25},{17,1},{25,9},{2,18},{10... | collective-permute-start | bytes 1769480 | tf_op jit(solution)/shard_map/ppermute | solution.py:650
  64.6 17.2 %collective-permute-start.7 = (bf16[32,24,384]{2,1,0:T(8,128)(2,1)S(1)}, bf16[32,24,384]{2,1,0:T(8,128)(2,1)S(1)}, u32[]{:S(2)}, u32[]{:S(2)}) collective-permute-start(bf16[32,24,384]{2,1,0:T(8,128)(2,1)S(1)} %get-tuple-element.114.refs_1_), channel_id=1, source_target_pairs={{0,1},{1,0},{2,3},{3,2},{4,5},{5,4},{6,7},{7,6},{8,9},{9,8},{10,11... | collective-permute-start | bytes 1769480 | tf_op jit(solution)/shard_map/ppermute | solution.py:650
  82.6 8.6 %collective-permute-start.8 = (bf16[16,24,384]{2,1,0:T(8,128)(2,1)S(1)}, bf16[16,24,384]{2,1,0:T(8,128)(2,1)S(1)}, u32[]{:S(2)}, u32[]{:S(2)}) collective-permute-start(bf16[16,24,384]{2,1,0:T(8,128)(2,1)S(1)} %get-tuple-element.122.refs_0_), channel_id=1, source_target_pairs={{0,1},{1,0},{2,3},{3,2},{4,5},{5,4},{6,7},{7,6},{8,9},{9,8},{10,11... | collective-permute-start | bytes 884744 | tf_op jit(solution)/shard_map/ppermute | solution.py:650
  83.2 8.2 %collective-permute-start.9 = (bf16[16,24,384]{2,1,0:T(8,128)(2,1)S(1)}, bf16[16,24,384]{2,1,0:T(8,128)(2,1)S(1)}, u32[]{:S(2)}, u32[]{:S(2)}) collective-permute-start(bf16[16,24,384]{2,1,0:T(8,128)(2,1)S(1)} %get-tuple-element.123.refs_1_), channel_id=1, source_target_pairs={{0,16},{8,24},{16,0},{24,8},{1,17},{9,25},{17,1},{25,9},{2,18},{10... | collective-permute-start | bytes 884744 | tf_op jit(solution)/shard_map/ppermute | solution.py:650
  89.1 13.6 %collective-permute-start.11 = (bf16[5,384,768]{2,1,0:T(8,128)(2,1)S(1)}, bf16[5,384,768]{2,1,0:T(8,128)(2,1)S(1)}, u32[]{:S(2)}, u32[]{:S(2)}) collective-permute-start(bf16[5,384,768]{2,1,0:T(8,128)(2,1)S(1)} %weight.8.refs_0_), channel_id=1, source_target_pairs={{0,8},{8,0},{16,24},{24,16},{1,9},{9,1},{17,25},{25,17},{2,10},{10... | collective-permute-start | bytes 8847368 | tf_op jit(solution)/shard_map/ppermute | solution.py:650
  92.0 7.4 %collective-permute-start.10 = (bf16[8,24,768]{2,1,0:T(8,128)(2,1)S(1)}, bf16[8,24,768]{2,1,0:T(8,128)(2,1)S(1)}, u32[]{:S(2)}, u32[]{:S(2)}) collective-permute-start(bf16[8,24,768]{2,1,0:T(8,128)(2,1)S(1)} %get-tuple-element.129.refs_1_), channel_id=1, source_target_pairs={{0,2},{1,3},{2,0},{3,1},{4,6},{5,7},{6,4},{7,5},{8,10},{9,11},{10,... | collective-permute-start | bytes 884744 | tf_op jit(solution)/shard_map/ppermute | solution.py:650
  100.0 21.7 %collective-permute-start.15 = (bf16[4,24,768]{2,1,0:T(8,128)(2,1)S(1)}, bf16[4,24,768]{2,1,0:T(8,128)(2,1)S(1)}, u32[]{:S(2)}, u32[]{:S(2)}) collective-permute-start(bf16[4,24,768]{2,1,0:T(8,128)(2,1)S(1)} %get-tuple-element.131.refs_0_), channel_id=1, source_target_pairs={{0,4},{1,5},{2,6},{3,7},{4,0},{5,1},{6,2},{7,3},{8,12},{9,13},{10,... | collective-permute-start | bytes 442376 | tf_op jit(solution)/shard_map/ppermute | solution.py:650
  103.5 17.5 %collective-permute-start.12 = (bf16[40,24,256]{2,1,0:T(8,128)(2,1)S(1)}, bf16[40,24,256]{2,1,0:T(8,128)(2,1)S(1)}, u32[]{:S(2)}, u32[]{:S(2)}) collective-permute-start(bf16[40,24,256]{2,1,0:T(8,128)(2,1)S(1)} %get-tuple-element.132.refs_1_), channel_id=1, source_target_pairs={{0,16},{8,24},{16,0},{24,8},{1,17},{9,25},{17,1},{25,9},{2,18},{10... | collective-permute-start | bytes 1474568 | tf_op jit(solution)/shard_map/ppermute | solution.py:650
  104.1 16.8 %collective-permute-start.13 = (bf16[40,24,256]{2,1,0:T(8,128)(2,1)S(1)}, bf16[40,24,256]{2,1,0:T(8,128)(2,1)S(1)}, u32[]{:S(2)}, u32[]{:S(2)}) collective-permute-start(bf16[40,24,256]{2,1,0:T(8,128)(2,1)S(1)} %get-tuple-element.133.refs_2_), channel_id=1, source_target_pairs={{0,1},{1,0},{2,3},{3,2},{4,5},{5,4},{6,7},{7,6},{8,9},{9,8},{10,11... | collective-permute-start | bytes 1474568 | tf_op jit(solution)/shard_map/ppermute | solution.py:650
  105.6 15.4 %collective-permute-start.14 = (bf16[40,24,256]{2,1,0:T(8,128)(2,1)S(1)}, bf16[40,24,256]{2,1,0:T(8,128)(2,1)S(1)}, u32[]{:S(2)}, u32[]{:S(2)}) collective-permute-start(bf16[40,24,256]{2,1,0:T(8,128)(2,1)S(1)} %get-tuple-element.134.refs_3_), channel_id=1, source_target_pairs={{0,2},{1,3},{2,0},{3,1},{4,6},{5,7},{6,4},{7,5},{8,10},{9,11},{10,... | collective-permute-start | bytes 1474568 | tf_op jit(solution)/shard_map/ppermute | solution.py:650
  121.0 7.7 %collective-permute-start.17 = (f32[12,768]{1,0:T(8,128)S(1)}, f32[12,768]{1,0:T(8,128)S(1)}, u32[]{:S(2)}, u32[]{:S(2)}) collective-permute-start(f32[12,768]{1,0:T(8,128)S(1)} %get-tuple-element.143.refs_0_.refs_2_), channel_id=1, source_target_pairs={{0,8},{8,0},{16,24},{24,16},{1,9},{9,1},{17,25},{25,17},{2,10},{10... | collective-permute-start | bytes 110600 | tf_op jit(solution)/shard_map/ppermute | solution.py:650
  130.4 9.9 %collective-permute-start.19 = (bf16[24,24,256]{2,1,0:T(8,128)(2,1)S(1)}, bf16[24,24,256]{2,1,0:T(8,128)(2,1)S(1)}, u32[]{:S(2)}, u32[]{:S(2)}) collective-permute-start(bf16[24,24,256]{2,1,0:T(8,128)(2,1)S(1)} %get-tuple-element.154), channel_id=1, source_target_pairs={{0,1},{1,0},{2,3},{3,2},{4,5},{5,4},{6,7},{7,6},{8,9},{9,8},{10,11... | collective-permute-start | bytes 884744 | tf_op jit(solution)/shard_map/ppermute | solution.py:650
  131.0 11.4 %collective-permute-start.18 = (bf16[26,24,256]{2,1,0:T(8,128)(2,1)S(1)}, bf16[26,24,256]{2,1,0:T(8,128)(2,1)S(1)}, u32[]{:S(2)}, u32[]{:S(2)}) collective-permute-start(bf16[26,24,256]{2,1,0:T(8,128)(2,1)S(1)} %get-tuple-element.152), channel_id=1, source_target_pairs={{0,16},{8,24},{16,0},{24,8},{1,17},{9,25},{17,1},{25,9},{2,18},{10... | collective-permute-start | bytes 958472 | tf_op jit(solution)/shard_map/ppermute | solution.py:650
  132.5 9.9 %collective-permute-start.20 = (bf16[24,24,256]{2,1,0:T(8,128)(2,1)S(1)}, bf16[24,24,256]{2,1,0:T(8,128)(2,1)S(1)}, u32[]{:S(2)}, u32[]{:S(2)}) collective-permute-start(bf16[24,24,256]{2,1,0:T(8,128)(2,1)S(1)} %get-tuple-element.156), channel_id=1, source_target_pairs={{0,2},{1,3},{2,0},{3,1},{4,6},{5,7},{6,4},{7,5},{8,10},{9,11},{10,... | collective-permute-start | bytes 884744 | tf_op jit(solution)/shard_map/ppermute | solution.py:650
  132.9 12.1 %collective-permute-start.28 = (bf16[20,24,256]{2,1,0:T(8,128)(2,1)S(1)}, bf16[20,24,256]{2,1,0:T(8,128)(2,1)S(1)}, u32[]{:S(2)}, u32[]{:S(2)}) collective-permute-start(bf16[20,24,256]{2,1,0:T(8,128)(2,1)S(1)} %get-tuple-element.147.refs_0_), channel_id=1, source_target_pairs={{0,1},{1,0},{2,3},{3,2},{4,5},{5,4},{6,7},{7,6},{8,9},{9,8},{10,11... | collective-permute-start | bytes 737288 | tf_op jit(solution)/shard_map/ppermute | solution.py:650
  134.4 13.3 %collective-permute-start.29 = (bf16[20,24,256]{2,1,0:T(8,128)(2,1)S(1)}, bf16[20,24,256]{2,1,0:T(8,128)(2,1)S(1)}, u32[]{:S(2)}, u32[]{:S(2)}) collective-permute-start(bf16[20,24,256]{2,1,0:T(8,128)(2,1)S(1)} %get-tuple-element.148.refs_1_), channel_id=1, source_target_pairs={{0,2},{1,3},{2,0},{3,1},{4,6},{5,7},{6,4},{7,5},{8,10},{9,11},{10,... | collective-permute-start | bytes 737288 | tf_op jit(solution)/shard_map/ppermute | solution.py:650
  140.3 8.4 %collective-permute-start.30 = (bf16[20,24,256]{2,1,0:T(8,128)(2,1)S(1)}, bf16[20,24,256]{2,1,0:T(8,128)(2,1)S(1)}, u32[]{:S(2)}, u32[]{:S(2)}) collective-permute-start(bf16[20,24,256]{2,1,0:T(8,128)(2,1)S(1)} %get-tuple-element.149.refs_2_), channel_id=1, source_target_pairs={{0,16},{8,24},{16,0},{24,8},{1,17},{9,25},{17,1},{25,9},{2,18},{10... | collective-permute-start | bytes 737288 | tf_op jit(solution)/shard_map/ppermute | solution.py:650
  143.1 8.3 %collective-permute-start.22 = (bf16[12,24,256]{2,1,0:T(8,128)(2,1)S(1)}, bf16[12,24,256]{2,1,0:T(8,128)(2,1)S(1)}, u32[]{:S(2)}, u32[]{:S(2)}) collective-permute-start(bf16[12,24,256]{2,1,0:T(8,128)(2,1)S(1)} %get-tuple-element.161), channel_id=1, source_target_pairs={{0,2},{1,3},{2,0},{3,1},{4,6},{5,7},{6,4},{7,5},{8,10},{9,11},{10,... | collective-permute-start | bytes 442376 | tf_op jit(solution)/shard_map/ppermute | solution.py:650
  143.6 8.4 %collective-permute-start.23 = (bf16[12,24,256]{2,1,0:T(8,128)(2,1)S(1)}, bf16[12,24,256]{2,1,0:T(8,128)(2,1)S(1)}, u32[]{:S(2)}, u32[]{:S(2)}) collective-permute-start(bf16[12,24,256]{2,1,0:T(8,128)(2,1)S(1)} %get-tuple-element.163), channel_id=1, source_target_pairs={{0,16},{8,24},{16,0},{24,8},{1,17},{9,25},{17,1},{25,9},{2,18},{10... | collective-permute-start | bytes 442376 | tf_op jit(solution)/shard_map/ppermute | solution.py:650
  145.0 7.0 %collective-permute-start.21 = (bf16[14,24,256]{2,1,0:T(8,128)(2,1)S(1)}, bf16[14,24,256]{2,1,0:T(8,128)(2,1)S(1)}, u32[]{:S(2)}, u32[]{:S(2)}) collective-permute-start(bf16[14,24,256]{2,1,0:T(8,128)(2,1)S(1)} %get-tuple-element.159), channel_id=1, source_target_pairs={{0,1},{1,0},{2,3},{3,2},{4,5},{5,4},{6,7},{7,6},{8,9},{9,8},{10,11... | collective-permute-start | bytes 516104 | tf_op jit(solution)/shard_map/ppermute | solution.py:650
  149.9 6.3 %collective-permute-start.32 = (bf16[10,24,256]{2,1,0:T(8,128)(2,1)S(1)}, bf16[10,24,256]{2,1,0:T(8,128)(2,1)S(1)}, u32[]{:S(2)}, u32[]{:S(2)}) collective-permute-start(bf16[10,24,256]{2,1,0:T(8,128)(2,1)S(1)} %get-tuple-element.180), channel_id=1, source_target_pairs={{0,16},{8,24},{16,0},{24,8},{1,17},{9,25},{17,1},{25,9},{2,18},{10... | collective-permute-start | bytes 368648 | tf_op jit(solution)/shard_map/ppermute | solution.py:650
  154.6 5.6 %collective-permute-start.24 = (bf16[8,24,256]{2,1,0:T(8,128)(2,1)S(1)}, bf16[8,24,256]{2,1,0:T(8,128)(2,1)S(1)}, u32[]{:S(2)}, u32[]{:S(2)}) collective-permute-start(bf16[8,24,256]{2,1,0:T(8,128)(2,1)S(1)} %get-tuple-element.166), channel_id=1, source_target_pairs={{0,2},{1,3},{2,0},{3,1},{4,6},{5,7},{6,4},{7,5},{8,10},{9,11},{10,... | collective-permute-start | bytes 294920 | tf_op jit(solution)/shard_map/ppermute | solution.py:650
  156.8 12.3 %collective-permute-start.34 = (bf16[5,24,768]{2,1,0:T(8,128)(2,1)S(1)}, bf16[5,24,768]{2,1,0:T(8,128)(2,1)S(1)}, u32[]{:S(2)}, u32[]{:S(2)}) collective-permute-start(bf16[5,24,768]{2,1,0:T(8,128)(2,1)S(1)} %get-tuple-element.184), channel_id=1, source_target_pairs={{0,4},{1,5},{2,6},{3,7},{4,0},{5,1},{6,2},{7,3},{8,12},{9,13},{10,... | collective-permute-start | bytes 552968 | tf_op jit(solution)/shard_map/ppermute | solution.py:650
  160.7 9.9 %collective-permute-start.27 = (bf16[4,24,768]{2,1,0:T(8,128)(2,1)S(1)}, bf16[4,24,768]{2,1,0:T(8,128)(2,1)S(1)}, u32[]{:S(2)}, u32[]{:S(2)}) collective-permute-start(bf16[4,24,768]{2,1,0:T(8,128)(2,1)S(1)} %get-tuple-element.173), channel_id=1, source_target_pairs={{0,4},{1,5},{2,6},{3,7},{4,0},{5,1},{6,2},{7,3},{8,12},{9,13},{10,... | collective-permute-start | bytes 442376 | tf_op jit(solution)/shard_map/ppermute | solution.py:650
  171.7 9.2 %collective-permute-start.35 = (bf16[4,72,384]{2,1,0:T(8,128)(2,1)S(1)}, bf16[4,72,384]{2,1,0:T(8,128)(2,1)S(1)}, u32[]{:S(2)}, u32[]{:S(2)}) collective-permute-start(bf16[4,72,384]{2,1,0:T(8,128)(2,1)S(1)} %get-tuple-element.187.refs_0_), channel_id=1, source_target_pairs={{0,4},{1,5},{2,6},{3,7},{4,0},{5,1},{6,2},{7,3},{8,12},{9,13},{10,... | collective-permute-start | bytes 663560 | tf_op jit(solution)/shard_map/ppermute | solution.py:650
  181.5 7.1 %collective-permute-start.36 = (bf16[4,72,384]{2,1,0:T(8,128)(2,1)S(1)}, bf16[4,72,384]{2,1,0:T(8,128)(2,1)S(1)}, u32[]{:S(2)}, u32[]{:S(2)}) collective-permute-start(bf16[4,72,384]{2,1,0:T(8,128)(2,1)S(1)} %get-tuple-element.189.refs_0_), channel_id=1, source_target_pairs={{0,2},{1,3},{2,0},{3,1},{4,6},{5,7},{6,4},{7,5},{8,10},{9,11},{10,... | collective-permute-start | bytes 663560 | tf_op jit(solution)/shard_map/ppermute | solution.py:650
  189.2 7.0 %collective-permute-start.37 = (bf16[4,72,384]{2,1,0:T(8,128)(2,1)S(1)}, bf16[4,72,384]{2,1,0:T(8,128)(2,1)S(1)}, u32[]{:S(2)}, u32[]{:S(2)}) collective-permute-start(bf16[4,72,384]{2,1,0:T(8,128)(2,1)S(1)} %get-tuple-element.194), channel_id=1, source_target_pairs={{0,1},{1,0},{2,3},{3,2},{4,5},{5,4},{6,7},{7,6},{8,9},{9,8},{10,11... | collective-permute-start | bytes 663560 | tf_op jit(solution)/shard_map/ppermute | solution.py:650
  191.4 6.5 %collective-permute-start.38 = (bf16[4,72,384]{2,1,0:T(8,128)(2,1)S(1)}, bf16[4,72,384]{2,1,0:T(8,128)(2,1)S(1)}, u32[]{:S(2)}, u32[]{:S(2)}) collective-permute-start(bf16[4,72,384]{2,1,0:T(8,128)(2,1)S(1)} %get-tuple-element.193.refs_0_), channel_id=1, source_target_pairs={{0,16},{8,24},{16,0},{24,8},{1,17},{9,25},{17,1},{25,9},{2,18},{10... | collective-permute-start | bytes 663560 | tf_op jit(solution)/shard_map/ppermute | solution.py:650
  196.2 6.2 %collective-permute-start.39 = (bf16[4,72,384]{2,1,0:T(8,128)(2,1)S(1)}, bf16[4,72,384]{2,1,0:T(8,128)(2,1)S(1)}, u32[]{:S(2)}, u32[]{:S(2)}) collective-permute-start(bf16[4,72,384]{2,1,0:T(8,128)(2,1)S(1)} %collective-permute-done.37.refs_1_), channel_id=1, source_target_pairs={{0,16},{8,24},{16,0},{24,8},{1,17},{9,25},{17,1},{25,9},{2,18},{10... | collective-permute-start | bytes 663560 | tf_op jit(solution)/shard_map/ppermute | solution.py:650
  197.3 5.8 %collective-permute-start.40 = (bf16[4,72,384]{2,1,0:T(8,128)(2,1)S(1)}, bf16[4,72,384]{2,1,0:T(8,128)(2,1)S(1)}, u32[]{:S(2)}, u32[]{:S(2)}) collective-permute-start(bf16[4,72,384]{2,1,0:T(8,128)(2,1)S(1)} %get-tuple-element.193.refs_0_), channel_id=1, source_target_pairs={{0,8},{8,0},{16,24},{24,16},{1,9},{9,1},{17,25},{25,17},{2,10},{10... | collective-permute-start | bytes 663560 | tf_op jit(solution)/shard_map/ppermute | solution.py:650
  197.3 5.8 %collective-permute-start.41 = (bf16[4,72,384]{2,1,0:T(8,128)(2,1)S(1)}, bf16[4,72,384]{2,1,0:T(8,128)(2,1)S(1)}, u32[]{:S(2)}, u32[]{:S(2)}) collective-permute-start(bf16[4,72,384]{2,1,0:T(8,128)(2,1)S(1)} %collective-permute-done.37.refs_1_), channel_id=1, source_target_pairs={{0,8},{8,0},{16,24},{24,16},{1,9},{9,1},{17,25},{25,17},{2,10},{10... | collective-permute-start | bytes 663560 | tf_op jit(solution)/shard_map/ppermute | solution.py:650
  (37 other events, 207.8 us)

commit v2 on v1

--- a/solution.py
+++ b/solution.py
@@ -370,8 +370,8 @@
 
 
 def unattend_kernel(after, sums, *refs):
-    q, k, v, p, ga = refs[after : after + 5]
-    vec_one, vec_two, vec_early = refs[after + 5 : -2] if sums else (None, None, None)
+    q, k, v, p, ga, attended = refs[after : after + 6]
+    vec_one, vec_two, vec_early = refs[after + 6 : -2] if sums else (None, None, None)
     stack_out, vec_out = refs[-2:]
     scaling = HEAD ** (-0.5)
     first = pl.program_id(0) == 0
@@ -390,6 +390,9 @@
         vec_out[8:] = vec_one[3:]
 
     place = 4 if sums else 0
+    head_of_row = lax.broadcasted_iota(jnp.int32, (2 * HEAD, 2 * SPAN), 0) // HEAD
+    head_of_lane = lax.broadcasted_iota(jnp.int32, (2 * HEAD, 2 * SPAN), 1) // SPAN
+    by_head = jnp.where(head_of_row == head_of_lane, 1.0, 0.0).astype(LOW)
     for span in range(p.shape[0]):
         at = slice(span * SPAN, (span + 1) * SPAN)
         for pair in range(HEADS // 2):
@@ -398,13 +401,9 @@
             weights = p[span, pair]
             grad = ga[at, lanes]
             spread_out = dot(grad, split_heads(v[at, lanes]), (1, 1))
-            wide = weights.astype(F32)
-            parts = []
-            for half in range(2):
-                cols = slice(half * SPAN, (half + 1) * SPAN)
-                wgt, gw = wide[:, cols], spread_out[:, cols]
-                parts.append((wgt * (gw - jnp.sum(gw * wgt, axis=-1, keepdims=True))).astype(LOW))
-            grad_scores = jnp.concatenate(parts, axis=1)
+            along = (grad.astype(F32) * attended[at, lanes].astype(F32)).astype(LOW)
+            grad_scores = (weights.astype(F32) * (spread_out - dot(along, by_head))).astype(LOW)
+            parts = [grad_scores[:, :SPAN], grad_scores[:, SPAN:]]
             grad_q = dot(grad_scores, split_heads(k[at, lanes])) * scaling
             tall_scores = jnp.concatenate(parts, axis=0)
             tall_weights = jnp.concatenate([weights[:, :SPAN], weights[:, SPAN:]], axis=0)
@@ -417,7 +416,7 @@
             vec_out[place + 1 : place + 2, lanes] += jnp.sum(grad_v, axis=0, keepdims=True)
 
 
-def unattend(after, part, parts, q, k, v, p, ga, stack=None, sums=()):
+def unattend(after, part, parts, q, k, v, p, ga, attended, stack=None, sums=()):
     total = q.shape[0]
     count = total // SPAN // parts
     first = part * count
@@ -432,6 +431,7 @@
         + [
             pl.BlockSpec((1, HEADS // 2, SPAN, 2 * SPAN), lambda i: (first + i, 0, 0, 0)),
             tall(D),
+            tall(D),
         ]
         + [whole(a.shape) for a in sums],
         out_specs=[tall(3 * D), whole(vec_shape)],
@@ -440,7 +440,7 @@
         compiler_params=params(),
         cost_estimate=cost(8),
         name="unattend",
-    )(*after, q, k, v, p, ga, *sums)
+    )(*after, q, k, v, p, ga, attended, *sums)
 
 
 def input_kernel(*refs):
@@ -512,7 +512,7 @@
 def contrast(cls_rows, span_count, pair_index, device, slots):
     total = cls_rows.shape[0]
     scale = {"row": lax.axis_size("col"), "col": 1}
-    masks = [scale[name] * bit for name, bit in gather_steps()]
+    masks = [scale[name] * bit for phase in gather_steps() for name, bit in phase]
     return pl.pallas_call(
         partial(contrast_kernel, slots, masks),
         in_specs=[pl.BlockSpec(memory_space=pltpu.SMEM)]
@@ -557,23 +557,25 @@
                         piece = block[lo : lo + rows, side * quarter : (side + 1) * quarter]
                         owned[index, pl.ds(at, rows), :] = piece
 
-        gradient = owned[slot].astype(LOW)
-    else:
-        gradient = gathered[0][0]
-    low_left, low_right = left[0], right[0].astype(LOW)
-    turned = dot(gradient, low_left, (0, 0))
-    turned = dot(low_right, turned.astype(LOW), (0, 0))
-    new_first = 0.9 * first[0] + 0.1 * turned
-    new_second = 0.999 * second[0] + 0.001 * turned * turned
-    first_out[0] = new_first
-    second_out[0] = new_second
-    spread_by = jnp.sqrt(new_second * (1.0 / (1.0 - 0.999**STEP))) + 1e-08
-    update = new_first * (1.0 / (1.0 - 0.9**STEP)) / spread_by
-    update = dot(update.astype(LOW), low_left, (1, 1))
-    update = dot(low_right, update.astype(LOW))
-    new_master = master[0] - RATE * (update + DECAY * master[0])
-    master_out[0] = new_master
-    low_out[0] = new_master.astype(LOW)
+    for here in range(master.shape[0]):
+        if packed:
+            gradient = owned[slot * master.shape[0] + here].astype(LOW)
+        else:
+            gradient = gathered[0][here]
+        low_left, low_right = left[here], right[here].astype(LOW)
+        turned = dot(gradient, low_left, (0, 0))
+        turned = dot(low_right, turned.astype(LOW), (0, 0))
+        new_first = 0.9 * first[here] + 0.1 * turned
+        new_second = 0.999 * second[here] + 0.001 * turned * turned
+        first_out[here] = new_first
+        second_out[here] = new_second
+        spread_by = jnp.sqrt(new_second * (1.0 / (1.0 - 0.999**STEP))) + 1e-08
+        update = new_first * (1.0 / (1.0 - 0.9**STEP)) / spread_by
+        update = dot(update.astype(LOW), low_left, (1, 1))
+        update = dot(low_right, update.astype(LOW))
+        new_master = master[here] - RATE * (update + DECAY * master[here])
+        master_out[here] = new_master
+        low_out[here] = new_master.astype(LOW)
 
 
 def ready_kernel(*refs):
@@ -614,7 +616,8 @@
     packed = rows % 8 == 0 and per_owner % 2 == 0
     if not packed:
         gathered = [to_owned(jnp.concatenate(gathered), position, per_owner)]
-    block = lambda a: pl.BlockSpec((1,) + a.shape[1:], lambda s, p: (s, 0, 0))
+    at_once = max(n for n in (1, 2, 3) if per_owner % n == 0)
+    block = lambda a: pl.BlockSpec((at_once,) + a.shape[1:], lambda s, p: (s, 0, 0))
     operands = streamed(master, first_moment, second_moment, left_basis, right_basis)
     like = jax.ShapeDtypeStruct(operands[0].shape, F32)
     fixed = pl.BlockSpec(gathered[0].shape, lambda s, p: (0, 0, 0))
@@ -622,14 +625,14 @@
         partial(adam_kernel, packed, len(gathered)),
         grid_spec=pltpu.PrefetchScalarGridSpec(
             num_scalar_prefetch=1,
-            grid=(per_owner,),
+            grid=(per_owner // at_once,),
             in_specs=[fixed if packed else block(part) for part in gathered]
             + [block(a) for a in operands],
             out_specs=[block(operands[0])] * 4,
             scratch_shapes=[pltpu.VMEM((per_owner, D, quarter), F32)] if packed else [],
         ),
         out_shape=[like, like, like, jax.ShapeDtypeStruct(like.shape, LOW)],
-        compiler_params=params(28),
+        compiler_params=params(48),
         cost_estimate=cost(20),
         name="adam",
     )(position.reshape(1), *gathered, *operands)
@@ -652,12 +655,20 @@
 
 def gather_steps():
     core, across, y_bits, z_bits = row_steps()
-    return z_bits[::-1] + y_bits + across + core
+    return [z_bits[::-1], y_bits + across, core]
 
 
 def gather_all(rows):
-    for step in gather_steps():
-        rows = jnp.concatenate([rows, swap(rows, step)])
+    columns = lax.axis_size("col")
+    every = lax.axis_size("row") * columns
+    scale = {"row": columns, "col": 1}
+    for phase in gather_steps():
+        arrived = []
+        for number in range(1, 1 << len(phase)):
+            mask = sum(scale[name] * bit for j, (name, bit) in enumerate(phase) if number >> j & 1)
+            pairs = [(i, i ^ mask) for i in range(every)]
+            arrived.append(lax.ppermute(rows, ("row", "col"), pairs))
+        rows = jnp.concatenate([rows] + arrived)
     return rows
 
 
@@ -950,10 +961,10 @@
     inner_run = Reduction(bits, 3, inner_away, inner_here)
     inner_run.land()
     early, vec_early = unattend(
-        outer_run.sent() + inner_run.sent(), 0, 2, q, k, v, p, grad_attended
+        outer_run.sent() + inner_run.sent(), 0, 2, q, k, v, p, grad_attended, attended
     )
     stack_low, vec_grad = unattend(
-        [], 1, 2, q, k, v, p, grad_attended, early, (vec_one, vec_two, vec_early)
+        [], 1, 2, q, k, v, p, grad_attended, attended, early, (vec_one, vec_two, vec_early)
     )
     inner_run.land(vec_grad)
     project_args = (tokens, stack_low, 3, False)
@@ -961,8 +972,9 @@
         8, inner_run.sent() + outer_run.landing(), 1 - core_bit, *project_args
     )
     project_here = weight_half(60, [project_away], core_bit, *project_args)
-    inner_run.land(project_here)
     project_run = Reduction(bits, 3, project_away, project_here, vec_grad)
+    project_run.land(*inner_run.landing())
+    inner_run.land()
     project_run.land()
     inner_run.land()
     project_run.land()

time: 219 us -> 213 us (0.973)
  starting transfers between devices: 45.2 us -> 50.5 us
  waiting for transfers between devices: 46.9 us -> 42.2 us
  local copies, waits for them, and re-layouts: 4.46 us -> 0.86 us
    ppermute x44 -> x39, waiting for transfers between devices: 46.9 us -> 33.3 us  [swap(): return lax.ppermute(send, step[0], [(i, i ^ step[1]) for i in range(size)])]
    ppermute x0 -> x7, starting transfers between devices: none -> 9.39 us  [gather_all(): arrived.append(lax.ppermute(rows, ('row', 'col'), pairs))]
    ppermute x0 -> x7, waiting for transfers between devices: none -> 8.92 us  [gather_all(): arrived.append(lax.ppermute(rows, ('row', 'col'), pairs))]
    ppermute x44 -> x39, starting transfers between devices: 45.2 us -> 41.1 us  [swap(): return lax.ppermute(send, step[0], [(i, i ^ step[1]) for i in range(size)])]
    unnamed x54 -> x60, local copies, waits for them, and re-layouts: 4.35 us -> 0.75 us
    pallas_call x2, Pallas kernels: 13.8 us -> 11.5 us  [unattend(): pl.pallas_call(partial(unattend_kernel, len(after), bool(sums)), grid=(co...]
  transfers between devices with their start and end apart: 44 -> 46, of which waited for: 25 -> 23; matrix products, arithmetic and copies ran while one was open for 0% -> 0% of each run, Pallas kernels for 29% -> 29%
where the time goes in v2:
time: 213 us
  Pallas kernels  118 us (55%)
  starting transfers between devices  50.5 us (24%)
  waiting for transfers between devices  42.2 us (20%)
    ppermute x39, starting transfers between devices, swap(): return lax.ppermute(send, step[0], [(i, i ^ step[1]) for i in range(size)])  41.1 us
    ppermute x39, waiting for transfers between devices, swap(): return lax.ppermute(send, step[0], [(i, i ^ step[1]) for i in range(size)])  33.3 us
    pallas_call x1, Pallas kernels, feed(): pl.pallas_call(feed_kernel, grid=(FF // D,), in_specs=[SMEM, SMEM, tall(D...  19.4 us
    pallas_call x6, Pallas kernels, weight_half(): pl.pallas_call(partial(weight_kernel, panels, len(after)), grid_spec=pltp...  19 us
    pallas_call x1, Pallas kernels, inner_grad(): pl.pallas_call(partial(inner_kernel, len(after)), grid=(bands,), in_specs...  15.6 us
    pallas_call x1, Pallas kernels, rotated_adam(): pl.pallas_call(partial(adam_kernel, packed, len(gathered)), grid_spec=plt...  14.3 us
    pallas_call x2, Pallas kernels, unattend(): pl.pallas_call(partial(unattend_kernel, len(after), bool(sums)), grid=(co...  11.5 us
    pallas_call x1, Pallas kernels, attend(): pl.pallas_call(attend_kernel, grid=(total // TALL,), in_specs=[tall, whol...  10.4 us
  transfers between devices with their start and end apart: 46, of which 23 were waited for; matrix products, arithmetic and copies ran while one was open for 0% of the time, Pallas kernels for 29%

profile of v2, /device:TPU:0, one launch (start us, length us, event | category | flops | bytes accessed | tf_op | source)
XLA Modules:
  0.0 213.0 jit_solution(14908143450861562310)
XLA Ops:
  0.7 10.4 %attend.1 = (bf16[768,768]{1,0:T(8,128)(2,1)}, bf16[768,768]{1,0:T(8,128)(2,1)}, bf16[768,768]{1,0:T(8,128)(2,1)}, bf16[6,6,128,256]{3,2,1,0:T(8,128)(2,1)}, bf16[768,768]{1,0:T(8,128)(2,1)S(1)}) custom-call(bf16[768,768]{1,0:T(8,128)(2,1)} %refs_1_.2, bf16[3,768,768]{2,1,0:T(8,128)(2,1)} %refs_4_.3, f32[1,9216]{1,0:T(1,128)} %bitcast.26), custom_call_target="tpu_custom_call" | custom-call | flops 11000000512 | tf_op jit(solution)/shard_map/attend/pallas_call | solution.py:103
  11.1 19.4 %feed.1 = (bf16[768,768]{1,0:T(8,128)(2,1)}, bf16[768,3072]{1,0:T(8,128)(2,1)}, bf16[768,3072]{1,0:T(8,128)(2,1)}, bf16[768,768]{1,0:T(8,128)(2,1)}, bf16[768,76...) custom-call(s32[1]{0:T(128)} %bitcast.place, ...), custom_call_target="tpu_custom_call" | custom-call | flops 22000001024 | tf_op jit(solution)/shard_map/feed/pallas_call | solution.py:190
  30.5 5.1 %collective-permute-start.2 = (bf16[8,768]{1,0:T(8,128)(2,1)S(1)}, bf16[8,768]{1,0:T(8,128)(2,1)S(1)}, u32[]{:S(2)}, u32[]{:S(2)}) collective-permute-start(bf16[8,768]{1,0:T(8,128)(2,1)S(1)} %get-tuple-element.108), channel_id=1, source_target_pairs={{0,6},{1,7},{2,4},{3,5},{4,2},{5,3},{6,0},{7,1},{8,14},{9,15},{10,... | collective-permute-start | bytes 36872 | tf_op jit(solution)/shard_map/ppermute | solution.py:670
  36.2 4.0 %collective-permute-done = bf16[8,768]{1,0:T(8,128)(2,1)S(1)} collective-permute-done((bf16[8,768]{1,0:T(8,128)(2,1)S(1)}, bf16[8,768]{1,0:T(8,128)(2,1)S(1)}, u32[]{:S(2)}, u32[]{:S(2)}) %collective-permute-start) | collective-permute-done | bytes 12320 | tf_op jit(solution)/shard_map/ppermute | solution.py:670
  44.6 2.8 %collective-permute-done.4 = bf16[32,768]{1,0:T(8,128)(2,1)S(1)} collective-permute-done((bf16[32,768]{1,0:T(8,128)(2,1)S(1)}, bf16[32,768]{1,0:T(8,128)(2,1)S(1)}, u32[]{:S(2)}, u32[]{:S(2)}) %collective-permute-start.4) | collective-permute-done | bytes 49184 | tf_op jit(solution)/shard_map/ppermute | solution.py:670
  50.3 2.2 %outer.1 = (f32[768,768]{1,0:T(8,128)S(1)}, bf16[768,768]{1,0:T(8,128)(2,1)S(1)}, f32[3,768]{1,0:T(4,128)S(1)}) custom-call(s32[1]{0:T(128)} %bitcast.place, s32[32]{0:T(128)S(1)} %copy-done.5, bf16[768,768]{1,0:T(8,128)(2,1)S(1)} %copy-done.3, f32[8,768]{1,0:T(8,128)S(1)} %get-tuple-element.109.grad_cls, bf16[768,768]{1,0:T(8,128)(2,1)S(1)} %get-tuple-element.110.unit_two, ...), custom_call_target="tpu_custom_call" | custom-call | flops 5500000256 | tf_op jit(solution)/shard_map/outer/pallas_call | solution.py:251
  52.6 3.1 %weight.6.refs_0_ = bf16[4,384,768]{2,1,0:T(8,128)(2,1)S(1)} custom-call(s32[1]{0:T(128)} %bitcast.7.side, bf16[768,3072]{1,0:T(8,128)(2,1)S(1)} %bitcast.39, bf16[768,768]{1,0:T(8,128)(2,1)S(1)} %get-tuple-element.112.refs_1_.refs_2_), custom_call_target="tpu_custom_call" | custom-call | flops 8800000000 | tf_op jit(solution)/shard_map/weight/pallas_call | solution.py:288
  55.9 3.2 %weight.7 = bf16[4,384,768]{2,1,0:T(8,128)(2,1)S(1)} custom-call(s32[1]{0:T(128)} %bitcast.2.side, bf16[4,384,768]{2,1,0:T(8,128)(2,1)S(1)} %weight.6.refs_0_, bf16[768,3072]{1,0:T(8,128)(2,1)S(1)} %bitcast.39, bf16[768,768]{1,0:T(8,128)(2,1)S(1)} %get-tuple-element.112.refs_1_.refs_2_), custom_call_target="tpu_custom_call" | custom-call | flops 65999998976 | tf_op jit(solution)/shard_map/weight/pallas_call | solution.py:288
  63.4 15.6 %inner.1 = (bf16[768,3072]{1,0:T(8,128)(2,1)S(1)}, f32[768,768]{1,0:T(8,128)}, bf16[768,768]{1,0:T(8,128)(2,1)S(1)}, bf16[768,768]{1,0:T(8,128)(2,1)S(1)}, f32[7,768]{1,0:T(8,128)S(1)}) custom-call(bf16[32,24,384]{2,1,0:T(8,128)(2,1)S(1)} %get-tuple-element.113.refs_0_, bf16[32,24,384]{2,1,0:T(8,128)(2,1)S(1)} %get-tuple-element.114.refs_1_, ...), custom_call_target="tpu_custom_call" | custom-call | flops 17600000000 | tf_op jit(solution)/shard_map/inner/pallas_call | solution.py:348
  82.5 3.9 %weight.8.refs_0_ = bf16[5,384,768]{2,1,0:T(8,128)(2,1)S(1)} custom-call(s32[1]{0:T(128)} %bitcast.7.side, bf16[16,24,384]{2,1,0:T(8,128)(2,1)S(1)} %get-tuple-element.122.refs_0_, bf16[16,24,384]{2,1,0:T(8,128)(2,1)S(1)} %get-tuple-element.123.refs_1_, bf16[768,768]{1,0:T(8,128)(2,1)S(1)} %copy-done.19, bf16[768,3072]{1,0:T(8,128)(2,1)S(1)} %get-tuple-element.125.refs_3_, ...), custom_call_target="tpu_custom_call" | custom-call | flops 8800000000 | tf_op jit(solution)/shard_map/weight/pallas_call | solution.py:288
  86.5 2.1 collective-permute-done.10.refs_2_
  89.8 2.1 collective-permute-start.12
  91.9 3.9 %weight.9.refs_0_ = bf16[5,384,768]{2,1,0:T(8,128)(2,1)S(1)} custom-call(s32[1]{0:T(128)} %bitcast.2.side, bf16[5,384,768]{2,1,0:T(8,128)(2,1)S(1)} %weight.8.refs_0_, bf16[8,24,768]{2,1,0:T(8,128)(2,1)S(1)} %get-tuple-element.129.refs_1_, bf16[768,768]{1,0:T(8,128)(2,1)S(1)} %copy-done.19, bf16[768,3072]{1,0:T(8,128)(2,1)S(1)} %copy-done.10, ...), custom_call_target="tpu_custom_call" | custom-call | flops 65999998976 | tf_op jit(solution)/shard_map/weight/pallas_call | solution.py:288
  103.9 5.7 %unattend.2 = (bf16[768,2304]{1,0:T(8,128)(2,1)}, f32[2,768]{1,0:T(2,128)S(1)}) custom-call(bf16[4,24,768]{2,1,0:T(8,128)(2,1)S(1)} %get-tuple-element.131.refs_0_, bf16[40,24,256]{2,1,0:T(8,128)(2,1)S(1)} %get-tuple-element.132.refs_1_, bf16[40,24,256]{2,1,0:T(8,128)(2,1)S(1)} %get-tuple-element.133.refs_2_, ...), custom_call_target="tpu_custom_call" | custom-call | flops 8800000000 | tf_op jit(solution)/shard_map/unattend/pallas_call | solution.py:426
  109.7 5.7 %unattend.3 = (bf16[768,2304]{1,0:T(8,128)(2,1)}, f32[12,768]{1,0:T(8,128)S(1)}) custom-call(bf16[768,2304]{1,0:T(8,128)(2,1)} %get-tuple-element.140.refs_0_, bf16[768,768]{1,0:T(8,128)(2,1)S(1)} %copy-done.12, bf16[768,768]{1,0:T(8,128)(2,1)S(1)} %copy-done.13, bf16[768,768]{1,0:T(8,128)(2,1)S(1)} %copy-done.14, ...), custom_call_target="tpu_custom_call", output_to_operand_aliasing={{0}: (0, {})} | custom-call | flops 8800000000 | tf_op jit(solution)/shard_map/unattend/pallas_call | solution.py:426
  118.3 2.4 %weight.10.refs_0_ = bf16[3,384,768]{2,1,0:T(8,128)(2,1)S(1)} custom-call(s32[1]{0:T(128)} %bitcast.7.side, bf16[20,24,256]{2,1,0:T(8,128)(2,1)S(1)} %get-tuple-element.147.refs_0_, bf16[20,24,256]{2,1,0:T(8,128)(2,1)S(1)} %get-tuple-element.148.refs_1_, bf16[20,24,256]{2,1,0:T(8,128)(2,1)S(1)} %get-tuple-element.149.refs_2_, ...), custom_call_target="tpu_custom_call" | custom-call | flops 8800000000 | tf_op jit(solution)/shard_map/weight/pallas_call | solution.py:288
  120.7 2.4 %weight.11 = bf16[3,384,768]{2,1,0:T(8,128)(2,1)S(1)} custom-call(s32[1]{0:T(128)} %bitcast.2.side, bf16[3,384,768]{2,1,0:T(8,128)(2,1)S(1)} %weight.10.refs_0_, bf16[768,768]{1,0:T(8,128)(2,1)S(1)} %copy-done.4, bf16[768,2304]{1,0:T(8,128)(2,1)S(1)} %copy-done.7), custom_call_target="tpu_custom_call" | custom-call | flops 65999998976 | tf_op jit(solution)/shard_map/weight/pallas_call | solution.py:288
  127.7 1.7 collective-permute-start.25
  129.4 5.5 %collective-permute-done.24.refs_3_ = bf16[24,24,256]{2,1,0:T(8,128)(2,1)S(1)} collective-permute-done((bf16[24,24,256]{2,1,0:T(8,128)(2,1)S(1)}, bf16[24,24,256]{2,1,0:T(8,128)(2,1)S(1)}, u32[]{:S(2)}, u32[]{:S(2)}) %collective-permute-start.24) | collective-permute-done | bytes 294944 | tf_op jit(solution)/shard_map/ppermute | solution.py:653
  136.8 1.7 collective-permute-start.27
  149.5 2.8 %collective-permute-start.36 = (bf16[5,24,768]{2,1,0:T(8,128)(2,1)S(1)}, bf16[5,24,768]{2,1,0:T(8,128)(2,1)S(1)}, u32[]{:S(2)}, u32[]{:S(2)}) collective-permute-start(bf16[5,24,768]{2,1,0:T(8,128)(2,1)S(1)} %get-tuple-element.184), channel_id=1, source_target_pairs={{0,4},{1,5},{2,6},{3,7},{4,0},{5,1},{6,2},{7,3},{8,12},{9,13},{10,... | collective-permute-start | bytes 552968 | tf_op jit(solution)/shard_map/ppermute | solution.py:653
  152.9 3.9 %collective-permute-start.32 = (bf16[4,24,768]{2,1,0:T(8,128)(2,1)S(1)}, bf16[4,24,768]{2,1,0:T(8,128)(2,1)S(1)}, u32[]{:S(2)}, u32[]{:S(2)}) collective-permute-start(bf16[4,24,768]{2,1,0:T(8,128)(2,1)S(1)} %get-tuple-element.173), channel_id=1, source_target_pairs={{0,4},{1,5},{2,6},{3,7},{4,0},{5,1},{6,2},{7,3},{8,12},{9,13},{10,... | collective-permute-start | bytes 442376 | tf_op jit(solution)/shard_map/ppermute | solution.py:653
  156.8 4.3 %collective-permute-done.36.refs_3_ = bf16[5,24,768]{2,1,0:T(8,128)(2,1)S(1)} collective-permute-done((bf16[5,24,768]{2,1,0:T(8,128)(2,1)S(1)}, bf16[5,24,768]{2,1,0:T(8,128)(2,1)S(1)}, u32[]{:S(2)}, u32[]{:S(2)}) %collective-permute-start.36) | collective-permute-done | bytes 184352 | tf_op jit(solution)/shard_map/ppermute | solution.py:653
  164.0 9.0 %ready.1.refs_0_.refs_1_.refs_11_ = bf16[6,768,768]{2,1,0:T(8,128)(2,1)} custom-call(bf16[4,72,384]{2,1,0:T(8,128)(2,1)S(1)} %get-tuple-element.187.refs_0_, f32[6,768,768]{2,1,0:T(8,128)} %refs_1_.3), custom_call_target="tpu_custom_call" | custom-call | flops 4400000000 | tf_op jit(solution)/shard_map/ready/pallas_call | solution.py:588
  173.0 2.2 %collective-permute-done.37.refs_2_ = bf16[4,72,384]{2,1,0:T(8,128)(2,1)S(1)} collective-permute-done((bf16[4,72,384]{2,1,0:T(8,128)(2,1)S(1)}, bf16[4,72,384]{2,1,0:T(8,128)(2,1)S(1)}, u32[]{:S(2)}, u32[]{:S(2)}) %collective-permute-start.37) | collective-permute-done | bytes 221216 | tf_op jit(solution)/shard_map/ppermute | solution.py:653
  175.9 4.0 %collective-permute-start.38 = (bf16[4,72,384]{2,1,0:T(8,128)(2,1)S(1)}, bf16[4,72,384]{2,1,0:T(8,128)(2,1)S(1)}, u32[]{:S(2)}, u32[]{:S(2)}) collective-permute-start(bf16[4,72,384]{2,1,0:T(8,128)(2,1)S(1)} %get-tuple-element.189.refs_0_), channel_id=1, source_target_pairs={{0,2},{1,3},{2,0},{3,1},{4,6},{5,7},{6,4},{7,5},{8,10},{9,11},{10,... | collective-permute-start | bytes 663560 | tf_op jit(solution)/shard_map/ppermute | solution.py:653
  179.9 4.3 %input.1.refs_0_ = f32[768,768]{1,0:T(8,128)} custom-call(bf16[4,72,384]{2,1,0:T(8,128)(2,1)S(1)} %get-tuple-element.189.refs_0_, bf16[6,768,768]{2,1,0:T(8,128)(2,1)} %ready.1.refs_0_.refs_1_.refs_11_, f32[768,768]{1,0:T(8,128)S(1)} %copy-done.8, bf16[768,2304]{1,0:T(8,128)(2,1)S(1)} %copy-done.7, bf16[3,768,768]{2,1,0:T(8,128)(2,1)S(1)} %copy-done.2), custom_call_target="tpu_custom_call" | custom-call | flops 8800000000 | tf_op jit(solution)/shard_map/input/pallas_call | solution.py:457
  184.8 2.0 collective-permute-start.39
  187.3 3.5 %collective-permute-done.39.refs_1_ = bf16[4,72,384]{2,1,0:T(8,128)(2,1)S(1)} collective-permute-done((bf16[4,72,384]{2,1,0:T(8,128)(2,1)S(1)}, bf16[4,72,384]{2,1,0:T(8,128)(2,1)S(1)}, u32[]{:S(2)}, u32[]{:S(2)}) %collective-permute-start.39) | collective-permute-done | bytes 221216 | tf_op jit(solution)/shard_map/ppermute | solution.py:653
  192.3 2.5 %collective-permute-done.40.refs_2_ = bf16[4,72,384]{2,1,0:T(8,128)(2,1)S(1)} collective-permute-done((bf16[4,72,384]{2,1,0:T(8,128)(2,1)S(1)}, bf16[4,72,384]{2,1,0:T(8,128)(2,1)S(1)}, u32[]{:S(2)}, u32[]{:S(2)}) %collective-permute-start.40) | collective-permute-done | bytes 221216 | tf_op jit(solution)/shard_map/ppermute | solution.py:653
  194.8 2.4 %collective-permute-done.41.refs_3_ = bf16[4,72,384]{2,1,0:T(8,128)(2,1)S(1)} collective-permute-done((bf16[4,72,384]{2,1,0:T(8,128)(2,1)S(1)}, bf16[4,72,384]{2,1,0:T(8,128)(2,1)S(1)}, u32[]{:S(2)}, u32[]{:S(2)}) %collective-permute-start.41) | collective-permute-done | bytes 221216 | tf_op jit(solution)/shard_map/ppermute | solution.py:653
  198.6 14.3 %adam.1 = (f32[6,192,768]{2,1,0:T(8,128)}, f32[6,192,768]{2,1,0:T(8,128)}, f32[6,192,768]{2,1,0:T(8,128)}, bf16[6,192,768]{2,1,0:T(8,128)(2,1)}) custom-call(s32[1]{0:T(128)} %bitcast.17.position, bf16[4,72,384]{2,1,0:T(8,128)(2,1)S(1)} %get-tuple-element.193.refs_0_, bf16[4,72,384]{2,1,0:T(8,128)(2,1)S(1)} %collective-permute-done.39.refs_1_, ...), custom_call_target="tpu_custom_call" | custom-call | flops 22000001024 | tf_op jit(solution)/shard_map/adam/pallas_call | solution.py:624
  (159 shorter events, 53.4 us)
Async XLA Ops:
  30.5 9.7 %collective-permute-start.2 = (bf16[8,768]{1,0:T(8,128)(2,1)S(1)}, bf16[8,768]{1,0:T(8,128)(2,1)S(1)}, u32[]{:S(2)}, u32[]{:S(2)}) collective-permute-start(bf16[8,768]{1,0:T(8,128)(2,1)S(1)} %get-tuple-element.108), channel_id=1, source_target_pairs={{0,6},{1,7},{2,4},{3,5},{4,2},{5,3},{6,0},{7,1},{8,14},{9,15},{10,... | collective-permute-start | bytes 36872 | tf_op jit(solution)/shard_map/ppermute | solution.py:670
  61.3 17.8 %collective-permute-start.8 = (bf16[32,24,384]{2,1,0:T(8,128)(2,1)S(1)}, bf16[32,24,384]{2,1,0:T(8,128)(2,1)S(1)}, u32[]{:S(2)}, u32[]{:S(2)}) collective-permute-start(bf16[32,24,384]{2,1,0:T(8,128)(2,1)S(1)} %get-tuple-element.113.refs_0_), channel_id=1, source_target_pairs={{0,16},{8,24},{16,0},{24,8},{1,17},{9,25},{17,1},{25,9},{2,18},{10... | collective-permute-start | bytes 1769480 | tf_op jit(solution)/shard_map/ppermute | solution.py:653
  62.3 16.8 %collective-permute-start.9 = (bf16[32,24,384]{2,1,0:T(8,128)(2,1)S(1)}, bf16[32,24,384]{2,1,0:T(8,128)(2,1)S(1)}, u32[]{:S(2)}, u32[]{:S(2)}) collective-permute-start(bf16[32,24,384]{2,1,0:T(8,128)(2,1)S(1)} %get-tuple-element.114.refs_1_), channel_id=1, source_target_pairs={{0,1},{1,0},{2,3},{3,2},{4,5},{5,4},{6,7},{7,6},{8,9},{9,8},{10,11... | collective-permute-start | bytes 1769480 | tf_op jit(solution)/shard_map/ppermute | solution.py:653
  80.1 8.5 %collective-permute-start.10 = (bf16[16,24,384]{2,1,0:T(8,128)(2,1)S(1)}, bf16[16,24,384]{2,1,0:T(8,128)(2,1)S(1)}, u32[]{:S(2)}, u32[]{:S(2)}) collective-permute-start(bf16[16,24,384]{2,1,0:T(8,128)(2,1)S(1)} %get-tuple-element.122.refs_0_), channel_id=1, source_target_pairs={{0,1},{1,0},{2,3},{3,2},{4,5},{5,4},{6,7},{7,6},{8,9},{9,8},{10,11... | collective-permute-start | bytes 884744 | tf_op jit(solution)/shard_map/ppermute | solution.py:653
  81.0 8.2 %collective-permute-start.11 = (bf16[16,24,384]{2,1,0:T(8,128)(2,1)S(1)}, bf16[16,24,384]{2,1,0:T(8,128)(2,1)S(1)}, u32[]{:S(2)}, u32[]{:S(2)}) collective-permute-start(bf16[16,24,384]{2,1,0:T(8,128)(2,1)S(1)} %get-tuple-element.123.refs_1_), channel_id=1, source_target_pairs={{0,16},{8,24},{16,0},{24,8},{1,17},{9,25},{17,1},{25,9},{2,18},{10... | collective-permute-start | bytes 884744 | tf_op jit(solution)/shard_map/ppermute | solution.py:653
  86.4 12.2 %collective-permute-start.13 = (bf16[5,384,768]{2,1,0:T(8,128)(2,1)S(1)}, bf16[5,384,768]{2,1,0:T(8,128)(2,1)S(1)}, u32[]{:S(2)}, u32[]{:S(2)}) collective-permute-start(bf16[5,384,768]{2,1,0:T(8,128)(2,1)S(1)} %weight.8.refs_0_), channel_id=1, source_target_pairs={{0,8},{8,0},{16,24},{24,16},{1,9},{9,1},{17,25},{25,17},{2,10},{10... | collective-permute-start | bytes 8847368 | tf_op jit(solution)/shard_map/ppermute | solution.py:653
  89.8 7.6 %collective-permute-start.12 = (bf16[8,24,768]{2,1,0:T(8,128)(2,1)S(1)}, bf16[8,24,768]{2,1,0:T(8,128)(2,1)S(1)}, u32[]{:S(2)}, u32[]{:S(2)}) collective-permute-start(bf16[8,24,768]{2,1,0:T(8,128)(2,1)S(1)} %get-tuple-element.129.refs_1_), channel_id=1, source_target_pairs={{0,2},{1,3},{2,0},{3,1},{4,6},{5,7},{6,4},{7,5},{8,10},{9,11},{10,... | collective-permute-start | bytes 884744 | tf_op jit(solution)/shard_map/ppermute | solution.py:653
  98.1 20.2 %collective-permute-start.20 = (bf16[4,24,768]{2,1,0:T(8,128)(2,1)S(1)}, bf16[4,24,768]{2,1,0:T(8,128)(2,1)S(1)}, u32[]{:S(2)}, u32[]{:S(2)}) collective-permute-start(bf16[4,24,768]{2,1,0:T(8,128)(2,1)S(1)} %get-tuple-element.131.refs_0_), channel_id=1, source_target_pairs={{0,4},{1,5},{2,6},{3,7},{4,0},{5,1},{6,2},{7,3},{8,12},{9,13},{10,... | collective-permute-start | bytes 442376 | tf_op jit(solution)/shard_map/ppermute | solution.py:653
  99.5 15.9 %collective-permute-start.14 = (bf16[40,24,256]{2,1,0:T(8,128)(2,1)S(1)}, bf16[40,24,256]{2,1,0:T(8,128)(2,1)S(1)}, u32[]{:S(2)}, u32[]{:S(2)}) collective-permute-start(bf16[40,24,256]{2,1,0:T(8,128)(2,1)S(1)} %get-tuple-element.132.refs_1_), channel_id=1, source_target_pairs={{0,16},{8,24},{16,0},{24,8},{1,17},{9,25},{17,1},{25,9},{2,18},{10... | collective-permute-start | bytes 1474568 | tf_op jit(solution)/shard_map/ppermute | solution.py:653
  100.8 14.6 %collective-permute-start.15 = (bf16[40,24,256]{2,1,0:T(8,128)(2,1)S(1)}, bf16[40,24,256]{2,1,0:T(8,128)(2,1)S(1)}, u32[]{:S(2)}, u32[]{:S(2)}) collective-permute-start(bf16[40,24,256]{2,1,0:T(8,128)(2,1)S(1)} %get-tuple-element.133.refs_2_), channel_id=1, source_target_pairs={{0,1},{1,0},{2,3},{3,2},{4,5},{5,4},{6,7},{7,6},{8,9},{9,8},{10,11... | collective-permute-start | bytes 1474568 | tf_op jit(solution)/shard_map/ppermute | solution.py:653
  102.2 13.2 %collective-permute-start.16 = (bf16[40,24,256]{2,1,0:T(8,128)(2,1)S(1)}, bf16[40,24,256]{2,1,0:T(8,128)(2,1)S(1)}, u32[]{:S(2)}, u32[]{:S(2)}) collective-permute-start(bf16[40,24,256]{2,1,0:T(8,128)(2,1)S(1)} %get-tuple-element.134.refs_3_), channel_id=1, source_target_pairs={{0,2},{1,3},{2,0},{3,1},{4,6},{5,7},{6,4},{7,5},{8,10},{9,11},{10,... | collective-permute-start | bytes 1474568 | tf_op jit(solution)/shard_map/ppermute | solution.py:653
  115.4 7.8 %collective-permute-start.22 = (f32[12,768]{1,0:T(8,128)S(1)}, f32[12,768]{1,0:T(8,128)S(1)}, u32[]{:S(2)}, u32[]{:S(2)}) collective-permute-start(f32[12,768]{1,0:T(8,128)S(1)} %get-tuple-element.143.refs_0_.refs_5_), channel_id=1, source_target_pairs={{0,8},{8,0},{16,24},{24,16},{1,9},{9,1},{17,25},{25,17},{2,10},{10... | collective-permute-start | bytes 110600 | tf_op jit(solution)/shard_map/ppermute | solution.py:653
  116.2 8.4 %collective-permute-start.17 = (bf16[20,24,256]{2,1,0:T(8,128)(2,1)S(1)}, bf16[20,24,256]{2,1,0:T(8,128)(2,1)S(1)}, u32[]{:S(2)}, u32[]{:S(2)}) collective-permute-start(bf16[20,24,256]{2,1,0:T(8,128)(2,1)S(1)} %get-tuple-element.147.refs_0_), channel_id=1, source_target_pairs={{0,1},{1,0},{2,3},{3,2},{4,5},{5,4},{6,7},{7,6},{8,9},{9,8},{10,11... | collective-permute-start | bytes 737288 | tf_op jit(solution)/shard_map/ppermute | solution.py:653
  116.8 8.1 %collective-permute-start.18 = (bf16[20,24,256]{2,1,0:T(8,128)(2,1)S(1)}, bf16[20,24,256]{2,1,0:T(8,128)(2,1)S(1)}, u32[]{:S(2)}, u32[]{:S(2)}) collective-permute-start(bf16[20,24,256]{2,1,0:T(8,128)(2,1)S(1)} %get-tuple-element.148.refs_1_), channel_id=1, source_target_pairs={{0,2},{1,3},{2,0},{3,1},{4,6},{5,7},{6,4},{7,5},{8,10},{9,11},{10,... | collective-permute-start | bytes 737288 | tf_op jit(solution)/shard_map/ppermute | solution.py:653
  117.2 7.8 %collective-permute-start.19 = (bf16[20,24,256]{2,1,0:T(8,128)(2,1)S(1)}, bf16[20,24,256]{2,1,0:T(8,128)(2,1)S(1)}, u32[]{:S(2)}, u32[]{:S(2)}) collective-permute-start(bf16[20,24,256]{2,1,0:T(8,128)(2,1)S(1)} %get-tuple-element.149.refs_2_), channel_id=1, source_target_pairs={{0,16},{8,24},{16,0},{24,8},{1,17},{9,25},{17,1},{25,9},{2,18},{10... | collective-permute-start | bytes 737288 | tf_op jit(solution)/shard_map/ppermute | solution.py:653
  125.7 10.4 %collective-permute-start.23 = (bf16[26,24,256]{2,1,0:T(8,128)(2,1)S(1)}, bf16[26,24,256]{2,1,0:T(8,128)(2,1)S(1)}, u32[]{:S(2)}, u32[]{:S(2)}) collective-permute-start(bf16[26,24,256]{2,1,0:T(8,128)(2,1)S(1)} %get-tuple-element.152), channel_id=1, source_target_pairs={{0,16},{8,24},{16,0},{24,8},{1,17},{9,25},{17,1},{25,9},{2,18},{10... | collective-permute-start | bytes 958472 | tf_op jit(solution)/shard_map/ppermute | solution.py:653
  126.8 8.1 %collective-permute-start.24 = (bf16[24,24,256]{2,1,0:T(8,128)(2,1)S(1)}, bf16[24,24,256]{2,1,0:T(8,128)(2,1)S(1)}, u32[]{:S(2)}, u32[]{:S(2)}) collective-permute-start(bf16[24,24,256]{2,1,0:T(8,128)(2,1)S(1)} %get-tuple-element.154), channel_id=1, source_target_pairs={{0,1},{1,0},{2,3},{3,2},{4,5},{5,4},{6,7},{7,6},{8,9},{9,8},{10,11... | collective-permute-start | bytes 884744 | tf_op jit(solution)/shard_map/ppermute | solution.py:653
  127.7 8.4 %collective-permute-start.25 = (bf16[24,24,256]{2,1,0:T(8,128)(2,1)S(1)}, bf16[24,24,256]{2,1,0:T(8,128)(2,1)S(1)}, u32[]{:S(2)}, u32[]{:S(2)}) collective-permute-start(bf16[24,24,256]{2,1,0:T(8,128)(2,1)S(1)} %get-tuple-element.156), channel_id=1, source_target_pairs={{0,2},{1,3},{2,0},{3,1},{4,6},{5,7},{6,4},{7,5},{8,10},{9,11},{10,... | collective-permute-start | bytes 884744 | tf_op jit(solution)/shard_map/ppermute | solution.py:653
  136.8 6.0 %collective-permute-start.27 = (bf16[12,24,256]{2,1,0:T(8,128)(2,1)S(1)}, bf16[12,24,256]{2,1,0:T(8,128)(2,1)S(1)}, u32[]{:S(2)}, u32[]{:S(2)}) collective-permute-start(bf16[12,24,256]{2,1,0:T(8,128)(2,1)S(1)} %get-tuple-element.161), channel_id=1, source_target_pairs={{0,2},{1,3},{2,0},{3,1},{4,6},{5,7},{6,4},{7,5},{8,10},{9,11},{10,... | collective-permute-start | bytes 442376 | tf_op jit(solution)/shard_map/ppermute | solution.py:653
  139.1 6.0 %collective-permute-start.26 = (bf16[14,24,256]{2,1,0:T(8,128)(2,1)S(1)}, bf16[14,24,256]{2,1,0:T(8,128)(2,1)S(1)}, u32[]{:S(2)}, u32[]{:S(2)}) collective-permute-start(bf16[14,24,256]{2,1,0:T(8,128)(2,1)S(1)} %get-tuple-element.159), channel_id=1, source_target_pairs={{0,1},{1,0},{2,3},{3,2},{4,5},{5,4},{6,7},{7,6},{8,9},{9,8},{10,11... | collective-permute-start | bytes 516104 | tf_op jit(solution)/shard_map/ppermute | solution.py:653
  140.6 6.9 %collective-permute-start.33 = (bf16[10,24,256]{2,1,0:T(8,128)(2,1)S(1)}, bf16[10,24,256]{2,1,0:T(8,128)(2,1)S(1)}, u32[]{:S(2)}, u32[]{:S(2)}) collective-permute-start(bf16[10,24,256]{2,1,0:T(8,128)(2,1)S(1)} %get-tuple-element.178), channel_id=1, source_target_pairs={{0,2},{1,3},{2,0},{3,1},{4,6},{5,7},{6,4},{7,5},{8,10},{9,11},{10,... | collective-permute-start | bytes 368648 | tf_op jit(solution)/shard_map/ppermute | solution.py:653
  141.2 7.7 %collective-permute-start.34 = (bf16[10,24,256]{2,1,0:T(8,128)(2,1)S(1)}, bf16[10,24,256]{2,1,0:T(8,128)(2,1)S(1)}, u32[]{:S(2)}, u32[]{:S(2)}) collective-permute-start(bf16[10,24,256]{2,1,0:T(8,128)(2,1)S(1)} %get-tuple-element.180), channel_id=1, source_target_pairs={{0,16},{8,24},{16,0},{24,8},{1,17},{9,25},{17,1},{25,9},{2,18},{10... | collective-permute-start | bytes 368648 | tf_op jit(solution)/shard_map/ppermute | solution.py:653
  142.8 6.1 %collective-permute-start.35 = (bf16[10,24,256]{2,1,0:T(8,128)(2,1)S(1)}, bf16[10,24,256]{2,1,0:T(8,128)(2,1)S(1)}, u32[]{:S(2)}, u32[]{:S(2)}) collective-permute-start(bf16[10,24,256]{2,1,0:T(8,128)(2,1)S(1)} %get-tuple-element.182), channel_id=1, source_target_pairs={{0,1},{1,0},{2,3},{3,2},{4,5},{5,4},{6,7},{7,6},{8,9},{9,8},{10,11... | collective-permute-start | bytes 368648 | tf_op jit(solution)/shard_map/ppermute | solution.py:653
  145.7 6.6 %collective-permute-start.30 = (bf16[6,24,256]{2,1,0:T(8,128)(2,1)S(1)}, bf16[6,24,256]{2,1,0:T(8,128)(2,1)S(1)}, u32[]{:S(2)}, u32[]{:S(2)}) collective-permute-start(bf16[6,24,256]{2,1,0:T(8,128)(2,1)S(1)} %get-tuple-element.168), channel_id=1, source_target_pairs={{0,16},{8,24},{16,0},{24,8},{1,17},{9,25},{17,1},{25,9},{2,18},{10... | collective-permute-start | bytes 221192 | tf_op jit(solution)/shard_map/ppermute | solution.py:653
  149.5 11.5 %collective-permute-start.36 = (bf16[5,24,768]{2,1,0:T(8,128)(2,1)S(1)}, bf16[5,24,768]{2,1,0:T(8,128)(2,1)S(1)}, u32[]{:S(2)}, u32[]{:S(2)}) collective-permute-start(bf16[5,24,768]{2,1,0:T(8,128)(2,1)S(1)} %get-tuple-element.184), channel_id=1, source_target_pairs={{0,4},{1,5},{2,6},{3,7},{4,0},{5,1},{6,2},{7,3},{8,12},{9,13},{10,... | collective-permute-start | bytes 552968 | tf_op jit(solution)/shard_map/ppermute | solution.py:653
  152.9 9.7 %collective-permute-start.32 = (bf16[4,24,768]{2,1,0:T(8,128)(2,1)S(1)}, bf16[4,24,768]{2,1,0:T(8,128)(2,1)S(1)}, u32[]{:S(2)}, u32[]{:S(2)}) collective-permute-start(bf16[4,24,768]{2,1,0:T(8,128)(2,1)S(1)} %get-tuple-element.173), channel_id=1, source_target_pairs={{0,4},{1,5},{2,6},{3,7},{4,0},{5,1},{6,2},{7,3},{8,12},{9,13},{10,... | collective-permute-start | bytes 442376 | tf_op jit(solution)/shard_map/ppermute | solution.py:653
  163.6 11.6 %collective-permute-start.37 = (bf16[4,72,384]{2,1,0:T(8,128)(2,1)S(1)}, bf16[4,72,384]{2,1,0:T(8,128)(2,1)S(1)}, u32[]{:S(2)}, u32[]{:S(2)}) collective-permute-start(bf16[4,72,384]{2,1,0:T(8,128)(2,1)S(1)} %get-tuple-element.187.refs_0_), channel_id=1, source_target_pairs={{0,4},{1,5},{2,6},{3,7},{4,0},{5,1},{6,2},{7,3},{8,12},{9,13},{10,... | collective-permute-start | bytes 663560 | tf_op jit(solution)/shard_map/ppermute | solution.py:653
  175.9 8.3 %collective-permute-start.38 = (bf16[4,72,384]{2,1,0:T(8,128)(2,1)S(1)}, bf16[4,72,384]{2,1,0:T(8,128)(2,1)S(1)}, u32[]{:S(2)}, u32[]{:S(2)}) collective-permute-start(bf16[4,72,384]{2,1,0:T(8,128)(2,1)S(1)} %get-tuple-element.189.refs_0_), channel_id=1, source_target_pairs={{0,2},{1,3},{2,0},{3,1},{4,6},{5,7},{6,4},{7,5},{8,10},{9,11},{10,... | collective-permute-start | bytes 663560 | tf_op jit(solution)/shard_map/ppermute | solution.py:653
  186.8 8.0 %collective-permute-start.40 = (bf16[4,72,384]{2,1,0:T(8,128)(2,1)S(1)}, bf16[4,72,384]{2,1,0:T(8,128)(2,1)S(1)}, u32[]{:S(2)}, u32[]{:S(2)}) collective-permute-start(bf16[4,72,384]{2,1,0:T(8,128)(2,1)S(1)} %get-tuple-element.193.refs_0_), channel_id=1, source_target_pairs={{0,16},{8,24},{16,0},{24,8},{1,17},{9,25},{17,1},{25,9},{2,18},{10... | collective-permute-start | bytes 663560 | tf_op jit(solution)/shard_map/ppermute | solution.py:653
  190.8 6.4 %collective-permute-start.41 = (bf16[4,72,384]{2,1,0:T(8,128)(2,1)S(1)}, bf16[4,72,384]{2,1,0:T(8,128)(2,1)S(1)}, u32[]{:S(2)}, u32[]{:S(2)}) collective-permute-start(bf16[4,72,384]{2,1,0:T(8,128)(2,1)S(1)} %collective-permute-done.39.refs_1_), channel_id=1, source_target_pairs={{0,16},{8,24},{16,0},{24,8},{1,17},{9,25},{17,1},{25,9},{2,18},{10... | collective-permute-start | bytes 663560 | tf_op jit(solution)/shard_map/ppermute | solution.py:653
  191.8 6.1 %collective-permute-start.42 = (bf16[4,72,384]{2,1,0:T(8,128)(2,1)S(1)}, bf16[4,72,384]{2,1,0:T(8,128)(2,1)S(1)}, u32[]{:S(2)}, u32[]{:S(2)}) collective-permute-start(bf16[4,72,384]{2,1,0:T(8,128)(2,1)S(1)} %get-tuple-element.193.refs_0_), channel_id=1, source_target_pairs={{0,8},{8,0},{16,24},{24,16},{1,9},{9,1},{17,25},{25,17},{2,10},{10... | collective-permute-start | bytes 663560 | tf_op jit(solution)/shard_map/ppermute | solution.py:653
  191.8 6.0 %collective-permute-start.43 = (bf16[4,72,384]{2,1,0:T(8,128)(2,1)S(1)}, bf16[4,72,384]{2,1,0:T(8,128)(2,1)S(1)}, u32[]{:S(2)}, u32[]{:S(2)}) collective-permute-start(bf16[4,72,384]{2,1,0:T(8,128)(2,1)S(1)} %collective-permute-done.39.refs_1_), channel_id=1, source_target_pairs={{0,8},{8,0},{16,24},{24,16},{1,9},{9,1},{17,25},{25,17},{2,10},{10... | collective-permute-start | bytes 663560 | tf_op jit(solution)/shard_map/ppermute | solution.py:653
  (41 other events, 238.6 us)

commit v3 on v2

--- a/solution.py
+++ b/solution.py
@@ -533,32 +533,30 @@
 
 
 def adam_kernel(
-    packed, parts, position, *refs,
+    masks, parts, position, *refs,
 ):
     gathered = refs[:parts]
     master, first, second, left, right, master_out, first_out, second_out, low_out, *scratch = refs[parts:]
     quarter = D // 4
     slot = pl.program_id(0)
-    if packed:
+    if masks:
         owned = scratch[0]
         shares, tall, _ = gathered[0].shape
-        rows = D // (shares * parts)
+        rows = D // len(masks)
 
         @pl.when(slot == 0)
         def _():
-            for part in range(parts):
-                for share in range(shares):
-                    block = gathered[part][share].astype(F32)
-                    number = part * shares + share
-                    at = pl.multiple_of((number ^ position[0]) * rows, rows)
-                    for index in range(owned.shape[0]):
-                        lo = index * rows % tall
-                        side = index * rows // tall
-                        piece = block[lo : lo + rows, side * quarter : (side + 1) * quarter]
-                        owned[index, pl.ds(at, rows), :] = piece
+            for number, mask in enumerate(masks):
+                block = gathered[number // shares][number % shares].astype(F32)
+                at = pl.multiple_of((mask ^ position[0]) * rows, rows)
+                for index in range(owned.shape[0]):
+                    lo = index * rows % tall
+                    side = index * rows // tall
+                    piece = block[lo : lo + rows, side * quarter : (side + 1) * quarter]
+                    owned[index, pl.ds(at, rows), :] = piece
 
     for here in range(master.shape[0]):
-        if packed:
+        if masks:
             gradient = owned[slot * master.shape[0] + here].astype(LOW)
         else:
             gradient = gathered[0][here]
@@ -597,9 +595,10 @@
     )(*after, *streamed(array))
 
 
-def to_owned(gathered, position, per_owner):
+def to_owned(gathered, masks, position, per_owner):
     quarter = D // 4
-    gathered = jnp.take(gathered, jnp.arange(gathered.shape[0]) ^ position, axis=0)
+    places = jnp.array(masks, jnp.int32) ^ position
+    gathered = jnp.zeros_like(gathered).at[places].set(gathered)
     flat = jnp.concatenate([gathered[..., :quarter], gathered[..., quarter:]], axis=1)
     rows = flat.shape[1] // per_owner
     flat = flat.reshape(flat.shape[0], per_owner, rows, quarter).transpose(1, 0, 2, 3)
@@ -610,26 +609,25 @@
     return array.transpose(0, 2, 1)
 
 
-def rotated_adam(position, gathered, master, first_moment, second_moment, left_basis, right_basis):
+def rotated_adam(position, gathered, masks, master, first_moment, second_moment, left_basis, right_basis):
     per_owner, quarter, _ = master.shape
-    rows = D // sum(part.shape[0] for part in gathered)
-    packed = rows % 8 == 0 and per_owner % 2 == 0
-    if not packed:
-        gathered = [to_owned(jnp.concatenate(gathered), position, per_owner)]
+    if D // len(masks) % 8 or per_owner % 2:
+        gathered = [to_owned(jnp.concatenate(gathered), masks, position, per_owner)]
+        masks = []
     at_once = max(n for n in (1, 2, 3) if per_owner % n == 0)
     block = lambda a: pl.BlockSpec((at_once,) + a.shape[1:], lambda s, p: (s, 0, 0))
     operands = streamed(master, first_moment, second_moment, left_basis, right_basis)
     like = jax.ShapeDtypeStruct(operands[0].shape, F32)
     fixed = pl.BlockSpec(gathered[0].shape, lambda s, p: (0, 0, 0))
     outputs = pl.pallas_call(
-        partial(adam_kernel, packed, len(gathered)),
+        partial(adam_kernel, masks, len(gathered)),
         grid_spec=pltpu.PrefetchScalarGridSpec(
             num_scalar_prefetch=1,
             grid=(per_owner // at_once,),
-            in_specs=[fixed if packed else block(part) for part in gathered]
+            in_specs=[fixed if masks else block(part) for part in gathered]
             + [block(a) for a in operands],
             out_specs=[block(operands[0])] * 4,
-            scratch_shapes=[pltpu.VMEM((per_owner, D, quarter), F32)] if packed else [],
+            scratch_shapes=[pltpu.VMEM((per_owner, D, quarter), F32)] if masks else [],
         ),
         out_shape=[like, like, like, jax.ShapeDtypeStruct(like.shape, LOW)],
         compiler_params=params(48),
@@ -808,9 +806,10 @@
             self.land()
 
 
-def slots_kernel(cols, panels, bits, owners, *refs):
-    sums, rider = refs[:6], refs[6]
-    away, here, rider_out, blocks, packed = refs[7:]
+def slots_kernel(after, cols, panels, column, owners, *refs):
+    refs = refs[after:]
+    sums, rider, rider_out = refs[:6], refs[6], refs[7]
+    targets, blocks, packed = refs[8:-2], refs[-2], refs[-1]
     quarter = D // 4
     found = [(sums[2 * run], sums[2 * run + 1], i) for run in range(3) for i in range(sums[2 * run].shape[0])]
     at = 0
@@ -832,74 +831,65 @@
             if lo < hi:
                 lanes = slice(side * quarter, (side + 1) * quarter)
                 packed[col, lo - side * half : hi - side * half, lanes] = value[lo - first : hi - first]
-    bit = bits[bits.shape[0] - 1]
-    count = cols // 2
-    away[...] = packed[pl.ds((1 - bit) * count, count)].astype(LOW)
-    here[...] = packed[pl.ds(bit * count, count)].astype(LOW)
-
-
-def to_slots(bits, runs, panels, owner_list):
+    for number, target in enumerate(targets):
+        target[...] = packed[column[0] ^ number].astype(LOW)
+
+
+def to_slots(after, runs, panels, owner_list):
     quarter, cols = D // 4, lax.axis_size("col")
     arrays = [a for run in runs for a in run.sides[0][:2]]
     rows = runs[0].rows
-    shape = (cols, len(panels) * 4 // cols * rows // 2, 2 * quarter)
-    like = jax.ShapeDtypeStruct((cols // 2,) + shape[1:], LOW)
+    shape = (len(panels) * 4 // cols * rows // 2, 2 * quarter)
     rider = runs[0].rider[0]
     return pl.pallas_call(
-        partial(slots_kernel, cols, panels),
-        in_specs=[SMEM, SMEM] + [pl.BlockSpec(memory_space=pltpu.VMEM)] * 7,
-        out_shape=[like, like, jax.ShapeDtypeStruct(rider.shape, F32)],
-        scratch_shapes=[pltpu.VMEM((len(panels) * 4, rows, quarter), F32), pltpu.VMEM(shape, F32)],
+        partial(slots_kernel, len(after), cols, panels),
+        in_specs=[SMEM, SMEM] + [ANY] * len(after) + [pl.BlockSpec(memory_space=pltpu.VMEM)] * 7,
+        out_shape=[jax.ShapeDtypeStruct(rider.shape, F32)] + [jax.ShapeDtypeStruct(shape, LOW)] * cols,
+        scratch_shapes=[
+            pltpu.VMEM((len(panels) * 4, rows, quarter), F32),
+            pltpu.VMEM((cols,) + shape, F32),
+        ],
         compiler_params=params(24),
         cost_estimate=cost(4),
         name="slots",
-    )(bits, owner_list, *arrays, rider)
-
-
-def regroup_kernel(after, at_bit, before, behind, bits, *refs):
-    parts, (away, here) = refs[after:-2], refs[-2:]
-    bit = bits[at_bit]
-    for which, target in ((1 - bit, away), (bit, here)):
-        to = 0
-        for part in parts:
-            for at in range(before):
-                target[to : to + behind] = part[pl.ds((2 * at + which) * behind, behind)]
-                to += behind
-
-
-def regroup(bits, at_bit, after, parts, before, behind):
-    count, tall, width = parts[0].shape
-    like = jax.ShapeDtypeStruct((count * len(parts) // 2, tall, width), LOW)
+    )(lax.axis_index("col").reshape(1), owner_list, *after, *arrays, rider)
+
+
+def merge_kernel(after, *refs):
+    *sources, target = refs[after:]
+    for number, source in enumerate(sources):
+        target[number] = source[...]
+
+
+def merge(after, arrays):
     return pl.pallas_call(
-        partial(regroup_kernel, len(after), at_bit, before, behind),
-        in_specs=[SMEM] + [ANY] * len(after) + [pl.BlockSpec(memory_space=pltpu.VMEM)] * len(parts),
-        out_shape=[like, like],
+        partial(merge_kernel, len(after)),
+        in_specs=[ANY] * len(after) + [pl.BlockSpec(memory_space=pltpu.VMEM)] * len(arrays),
+        out_shape=jax.ShapeDtypeStruct((len(arrays),) + arrays[0].shape, arrays[0].dtype),
         compiler_params=params(24),
-        cost_estimate=cost(2),
-        name="regroup",
-    )(bits, *after, *parts)
-
-
-def spread(bits, away, here, beside):
+        cost_estimate=cost(1),
+        name="merge",
+    )(*after, *arrays)
+
+
+def spread(parts):
     core, across, y_bits, z_bits = row_steps()
     order = core + across + y_bits + z_bits
-    left = axis_bits("col")[::-1]
-    made, shares = [], 1
-    for step in (y_bits + z_bits)[::-1]:
-        dim = left.index(step)
-        if shares > 1:
-            after = streamed(*made[-1:]) if len(made) == shares.bit_length() - 1 else []
-            behind = 1 << (len(left) - dim - 1)
-            before = shares // 2 << dim
-            away, here = regroup(bits, order.index(step), after, parts, before, behind)
-        left.remove(step)
-        parts = [here, swap(away, step)]
-        if len(made) < len(beside):
-            made.append(beside[len(made)]([away] + streamed(*made[-1:])))
-        shares *= 2
-    for step in (core + across)[::-1]:
-        parts = parts + [swap(part, step) for part in parts]
-    return parts, made
+    weight = lambda step: 1 << (len(order) - 1 - order.index(step))
+    cols, bits = len(parts), axis_bits("col")
+    sent = lambda number: lax.ppermute(parts[number], "col", [(i, i ^ number) for i in range(cols)])
+    arrived = [parts[0]] + [sent(number) for number in range(1, cols)]
+    masks = [sum(weight(step) for step in bits if number & step[1]) for number in range(cols)]
+    near = merge([], arrived[: cols // 2])
+    first, *rest = (core + across)[::-1]
+    moved = swap(near, first)
+    far = merge([], arrived[cols // 2 :])
+    shares = [near, far, moved, swap(far, first)]
+    masks = masks + [mask ^ weight(first) for mask in masks]
+    for step in rest:
+        shares = shares + [swap(share, step) for share in shares]
+        masks = masks + [mask ^ weight(step) for mask in masks]
+    return shares, masks
 
 
 def row_place():
@@ -974,27 +964,22 @@
     project_here = weight_half(60, [project_away], core_bit, *project_args)
     project_run = Reduction(bits, 3, project_away, project_here, vec_grad)
     project_run.land(*inner_run.landing())
+    grad_tokens = input_grad(project_run.sent(), grad_one, stack_low, w_qkv)
     inner_run.land()
-    project_run.land()
+    project_run.land(*streamed(grad_tokens))
     inner_run.land()
     project_run.land()
     for run in (outer_run, inner_run, project_run):
         run.finish()
-    slots_away, slots_here, vec_grad = to_slots(
-        bits, (project_run, inner_run, outer_run), (0, 1, 2, 7, 3, 4, 5, 6, 8, 9, 10, 11), owner_list
+    low_left = ready(project_run.sent(), left_basis, LOW)
+    vec_grad, *parts = to_slots(
+        streamed(low_left), (project_run, inner_run, outer_run),
+        (0, 1, 2, 7, 3, 4, 5, 6, 8, 9, 10, 11), owner_list,
     )
     vec_grad = vec_grad.reshape(-1)
-    gathered, (low_left, grad_tokens) = spread(
-        bits,
-        slots_away,
-        slots_here,
-        [
-            lambda after: ready(after, left_basis, LOW),
-            lambda after: input_grad(after, grad_one, stack_low, w_qkv),
-        ],
-    )
+    gathered, masks = spread(parts)
     new_master, new_first, new_second, master_copy = rotated_adam(
-        row_place(), gathered, turn(master), turn(first_moment), turn(second_moment),
+        row_place(), gathered, masks, turn(master), turn(first_moment), turn(second_moment),
         low_left, right_basis,
     )
     vec_first_new = 0.9 * vec_first + 0.1 * vec_grad

time: 213 us -> 203 us (0.953)
  waiting for transfers between devices: 42.2 us -> 27.6 us
  starting transfers between devices: 50.5 us -> 56.1 us
    ppermute x39 -> x36, waiting for transfers between devices: 33.3 us -> 16.7 us  [swap(): return lax.ppermute(send, step[0], [(i, i ^ step[1]) for i in range(size)])]
    ppermute x0 -> x7, starting transfers between devices: none -> 11.2 us  [spread(): lax.ppermute(parts[number], 'col', [(i, i ^ number) for i in range(cols)])]
    ppermute x39 -> x36, starting transfers between devices: 41.1 us -> 35.6 us  [swap(): return lax.ppermute(send, step[0], [(i, i ^ step[1]) for i in range(size)])]
  transfers between devices with their start and end apart: 46 -> 50, of which waited for: 23 -> 23; matrix products, arithmetic and copies ran while one was open for 0% -> 0% of each run, Pallas kernels for 29% -> 30%
where the time goes in v3:
time: 203 us
  Pallas kernels  116 us (57%)
  starting transfers between devices  56.1 us (28%)
  waiting for transfers between devices  27.6 us (14%)
    ppermute x36, starting transfers between devices, swap(): return lax.ppermute(send, step[0], [(i, i ^ step[1]) for i in range(size)])  35.6 us
    pallas_call x1, Pallas kernels, feed(): pl.pallas_call(feed_kernel, grid=(FF // D,), in_specs=[SMEM, SMEM, tall(D...  19.4 us
    pallas_call x6, Pallas kernels, weight_half(): pl.pallas_call(partial(weight_kernel, panels, len(after)), grid_spec=pltp...  19 us
    ppermute x36, waiting for transfers between devices, swap(): return lax.ppermute(send, step[0], [(i, i ^ step[1]) for i in range(size)])  16.7 us
    pallas_call x1, Pallas kernels, inner_grad(): pl.pallas_call(partial(inner_kernel, len(after)), grid=(bands,), in_specs...  15.6 us
    pallas_call x1, Pallas kernels, rotated_adam(): pl.pallas_call(partial(adam_kernel, masks, len(gathered)), grid_spec=pltp...  14.3 us
    pallas_call x2, Pallas kernels, unattend(): pl.pallas_call(partial(unattend_kernel, len(after), bool(sums)), grid=(co...  11.5 us
    ppermute x7, starting transfers between devices, spread(): lax.ppermute(parts[number], 'col', [(i, i ^ number) for i in range(cols)])  11.2 us
  transfers between devices with their start and end apart: 50, of which 23 were waited for; matrix products, arithmetic and copies ran while one was open for 0% of the time, Pallas kernels for 30%

profile of v3, /device:TPU:0, one launch (start us, length us, event | category | flops | bytes accessed | tf_op | source)
XLA Modules:
  0.0 202.8 jit_solution(8464529905981209099)
XLA Ops:
  0.7 10.4 %attend.1 = (bf16[768,768]{1,0:T(8,128)(2,1)}, bf16[768,768]{1,0:T(8,128)(2,1)}, bf16[768,768]{1,0:T(8,128)(2,1)}, bf16[6,6,128,256]{3,2,1,0:T(8,128)(2,1)}, bf16[768,768]{1,0:T(8,128)(2,1)S(1)}) custom-call(bf16[768,768]{1,0:T(8,128)(2,1)} %refs_1_.2, bf16[3,768,768]{2,1,0:T(8,128)(2,1)} %refs_5_.1, f32[1,9216]{1,0:T(1,128)} %bitcast.27), custom_call_target="tpu_custom_call" | custom-call | flops 11000000512 | tf_op jit(solution)/shard_map/attend/pallas_call | solution.py:103
  11.1 19.4 %feed.1 = (bf16[768,768]{1,0:T(8,128)(2,1)}, bf16[768,3072]{1,0:T(8,128)(2,1)}, bf16[768,3072]{1,0:T(8,128)(2,1)}, bf16[768,768]{1,0:T(8,128)(2,1)}, bf16[768,76...) custom-call(s32[1]{0:T(128)} %bitcast.place, ...), custom_call_target="tpu_custom_call" | custom-call | flops 22000001024 | tf_op jit(solution)/shard_map/feed/pallas_call | solution.py:190
  30.5 5.1 %collective-permute-start.2 = (bf16[8,768]{1,0:T(8,128)(2,1)S(1)}, bf16[8,768]{1,0:T(8,128)(2,1)S(1)}, u32[]{:S(2)}, u32[]{:S(2)}) collective-permute-start(bf16[8,768]{1,0:T(8,128)(2,1)S(1)} %get-tuple-element.110), channel_id=1, source_target_pairs={{0,6},{1,7},{2,4},{3,5},{4,2},{5,3},{6,0},{7,1},{8,14},{9,15},{10,... | collective-permute-start | bytes 36872 | tf_op jit(solution)/shard_map/ppermute | solution.py:668
  36.2 4.0 %collective-permute-done = bf16[8,768]{1,0:T(8,128)(2,1)S(1)} collective-permute-done((bf16[8,768]{1,0:T(8,128)(2,1)S(1)}, bf16[8,768]{1,0:T(8,128)(2,1)S(1)}, u32[]{:S(2)}, u32[]{:S(2)}) %collective-permute-start) | collective-permute-done | bytes 12320 | tf_op jit(solution)/shard_map/ppermute | solution.py:668
  44.6 2.8 %collective-permute-done.4 = bf16[32,768]{1,0:T(8,128)(2,1)S(1)} collective-permute-done((bf16[32,768]{1,0:T(8,128)(2,1)S(1)}, bf16[32,768]{1,0:T(8,128)(2,1)S(1)}, u32[]{:S(2)}, u32[]{:S(2)}) %collective-permute-start.4) | collective-permute-done | bytes 49184 | tf_op jit(solution)/shard_map/ppermute | solution.py:668
  50.3 2.2 %outer.1 = (f32[768,768]{1,0:T(8,128)S(1)}, bf16[768,768]{1,0:T(8,128)(2,1)S(1)}, f32[3,768]{1,0:T(4,128)S(1)}) custom-call(s32[1]{0:T(128)} %bitcast.place, s32[32]{0:T(128)S(1)} %copy-done.5, bf16[768,768]{1,0:T(8,128)(2,1)S(1)} %copy-done.3, f32[8,768]{1,0:T(8,128)S(1)} %get-tuple-element.111.grad_cls, bf16[768,768]{1,0:T(8,128)(2,1)S(1)} %get-tuple-element.112.unit_two, ...), custom_call_target="tpu_custom_call" | custom-call | flops 5500000256 | tf_op jit(solution)/shard_map/outer/pallas_call | solution.py:251
  52.6 3.1 %weight.6.refs_0_ = bf16[4,384,768]{2,1,0:T(8,128)(2,1)S(1)} custom-call(s32[1]{0:T(128)} %bitcast.7.side, bf16[768,3072]{1,0:T(8,128)(2,1)S(1)} %bitcast.40, bf16[768,768]{1,0:T(8,128)(2,1)S(1)} %get-tuple-element.114.refs_1_.refs_2_), custom_call_target="tpu_custom_call" | custom-call | flops 8800000000 | tf_op jit(solution)/shard_map/weight/pallas_call | solution.py:288
  55.9 3.2 %weight.7 = bf16[4,384,768]{2,1,0:T(8,128)(2,1)S(1)} custom-call(s32[1]{0:T(128)} %bitcast.2.side, bf16[4,384,768]{2,1,0:T(8,128)(2,1)S(1)} %weight.6.refs_0_, bf16[768,3072]{1,0:T(8,128)(2,1)S(1)} %bitcast.40, bf16[768,768]{1,0:T(8,128)(2,1)S(1)} %get-tuple-element.114.refs_1_.refs_2_), custom_call_target="tpu_custom_call" | custom-call | flops 65999998976 | tf_op jit(solution)/shard_map/weight/pallas_call | solution.py:288
  63.4 15.6 %inner.1 = (bf16[768,3072]{1,0:T(8,128)(2,1)S(1)}, f32[768,768]{1,0:T(8,128)}, bf16[768,768]{1,0:T(8,128)(2,1)S(1)}, bf16[768,768]{1,0:T(8,128)(2,1)S(1)}, f32[7,768]{1,0:T(8,128)S(1)}) custom-call(bf16[32,24,384]{2,1,0:T(8,128)(2,1)S(1)} %get-tuple-element.115.refs_0_, bf16[32,24,384]{2,1,0:T(8,128)(2,1)S(1)} %get-tuple-element.116.refs_1_, ...), custom_call_target="tpu_custom_call" | custom-call | flops 17600000000 | tf_op jit(solution)/shard_map/inner/pallas_call | solution.py:348
  82.4 4.0 %weight.8.refs_0_ = bf16[5,384,768]{2,1,0:T(8,128)(2,1)S(1)} custom-call(s32[1]{0:T(128)} %bitcast.7.side, bf16[16,24,384]{2,1,0:T(8,128)(2,1)S(1)} %get-tuple-element.124.refs_0_, bf16[16,24,384]{2,1,0:T(8,128)(2,1)S(1)} %get-tuple-element.125.refs_1_, bf16[768,768]{1,0:T(8,128)(2,1)S(1)} %copy-done.19, bf16[768,3072]{1,0:T(8,128)(2,1)S(1)} %get-tuple-element.127.refs_3_, ...), custom_call_target="tpu_custom_call" | custom-call | flops 8800000000 | tf_op jit(solution)/shard_map/weight/pallas_call | solution.py:288
  86.5 2.1 %collective-permute-done.10.refs_2_ = bf16[16,24,384]{2,1,0:T(8,128)(2,1)S(1)} collective-permute-done((bf16[16,24,384]{2,1,0:T(8,128)(2,1)S(1)}, bf16[16,24,384]{2,1,0:T(8,128)(2,1)S(1)}, u32[]{:S(2)}, u32[]{:S(2)}) %collective-permute-start.10) | collective-permute-done | bytes 294944 | tf_op jit(solution)/shard_map/ppermute | solution.py:651
  89.8 2.1 %collective-permute-start.12 = (bf16[8,24,768]{2,1,0:T(8,128)(2,1)S(1)}, bf16[8,24,768]{2,1,0:T(8,128)(2,1)S(1)}, u32[]{:S(2)}, u32[]{:S(2)}) collective-permute-start(bf16[8,24,768]{2,1,0:T(8,128)(2,1)S(1)} %get-tuple-element.131.refs_1_), channel_id=1, source_target_pairs={{0,2},{1,3},{2,0},{3,1},{4,6},{5,7},{6,4},{7,5},{8,10},{9,11},{10,... | collective-permute-start | bytes 884744 | tf_op jit(solution)/shard_map/ppermute | solution.py:651
  91.9 4.0 %weight.9.refs_0_ = bf16[5,384,768]{2,1,0:T(8,128)(2,1)S(1)} custom-call(s32[1]{0:T(128)} %bitcast.2.side, bf16[5,384,768]{2,1,0:T(8,128)(2,1)S(1)} %weight.8.refs_0_, bf16[8,24,768]{2,1,0:T(8,128)(2,1)S(1)} %get-tuple-element.131.refs_1_, bf16[768,768]{1,0:T(8,128)(2,1)S(1)} %copy-done.19, bf16[768,3072]{1,0:T(8,128)(2,1)S(1)} %copy-done.8, ...), custom_call_target="tpu_custom_call" | custom-call | flops 65999998976 | tf_op jit(solution)/shard_map/weight/pallas_call | solution.py:288
  102.2 1.7 collective-permute-start.16
  103.9 5.7 %unattend.2 = (bf16[768,2304]{1,0:T(8,128)(2,1)}, f32[2,768]{1,0:T(2,128)S(1)}) custom-call(bf16[4,24,768]{2,1,0:T(8,128)(2,1)S(1)} %get-tuple-element.133.refs_0_, bf16[40,24,256]{2,1,0:T(8,128)(2,1)S(1)} %get-tuple-element.134.refs_1_, bf16[40,24,256]{2,1,0:T(8,128)(2,1)S(1)} %get-tuple-element.135.refs_2_, ...), custom_call_target="tpu_custom_call" | custom-call | flops 8800000000 | tf_op jit(solution)/shard_map/unattend/pallas_call | solution.py:426
  109.6 5.7 %unattend.3 = (bf16[768,2304]{1,0:T(8,128)(2,1)}, f32[12,768]{1,0:T(8,128)S(1)}) custom-call(bf16[768,2304]{1,0:T(8,128)(2,1)} %get-tuple-element.142.refs_0_, bf16[768,768]{1,0:T(8,128)(2,1)S(1)} %copy-done.12, bf16[768,768]{1,0:T(8,128)(2,1)S(1)} %copy-done.13, bf16[768,768]{1,0:T(8,128)(2,1)S(1)} %copy-done.14, ...), custom_call_target="tpu_custom_call", output_to_operand_aliasing={{0}: (0, {})} | custom-call | flops 8800000000 | tf_op jit(solution)/shard_map/unattend/pallas_call | solution.py:426
  118.2 2.4 %weight.10.refs_0_ = bf16[3,384,768]{2,1,0:T(8,128)(2,1)S(1)} custom-call(s32[1]{0:T(128)} %bitcast.7.side, bf16[20,24,256]{2,1,0:T(8,128)(2,1)S(1)} %get-tuple-element.149.refs_0_, bf16[20,24,256]{2,1,0:T(8,128)(2,1)S(1)} %get-tuple-element.150.refs_1_, bf16[20,24,256]{2,1,0:T(8,128)(2,1)S(1)} %get-tuple-element.151.refs_2_, ...), custom_call_target="tpu_custom_call" | custom-call | flops 8800000000 | tf_op jit(solution)/shard_map/weight/pallas_call | solution.py:288
  120.7 2.4 %weight.11 = bf16[3,384,768]{2,1,0:T(8,128)(2,1)S(1)} custom-call(s32[1]{0:T(128)} %bitcast.2.side, bf16[3,384,768]{2,1,0:T(8,128)(2,1)S(1)} %weight.10.refs_0_, bf16[768,768]{1,0:T(8,128)(2,1)S(1)} %copy-done.4, bf16[768,2304]{1,0:T(8,128)(2,1)S(1)} %copy-done.9), custom_call_target="tpu_custom_call" | custom-call | flops 65999998976 | tf_op jit(solution)/shard_map/weight/pallas_call | solution.py:288
  127.1 1.7 collective-permute-start.25
  129.4 4.3 %input.1.refs_0_ = f32[768,768]{1,0:T(8,128)} custom-call(bf16[26,24,256]{2,1,0:T(8,128)(2,1)S(1)} %get-tuple-element.153.refs_0_, bf16[24,24,256]{2,1,0:T(8,128)(2,1)S(1)} %get-tuple-element.154.refs_1_, bf16[24,24,256]{2,1,0:T(8,128)(2,1)S(1)} %get-tuple-element.155.refs_2_, f32[768,768]{1,0:T(8,128)S(1)} %copy-done.10, bf16[768,2304]{1,0:T(8,128)(2,1)S(1)} %copy-done.9, ...), custom_call_target="tpu_custom_call" | custom-call | flops 8800000000 | tf_op jit(solution)/shard_map/input/pallas_call | solution.py:457
  135.2 1.7 collective-permute-done.23.refs_2_
  140.5 1.7 collective-permute-start.33
  148.0 1.8 collective-permute-start.29
  150.4 3.0 %collective-permute-start.36 = (bf16[5,24,768]{2,1,0:T(8,128)(2,1)S(1)}, bf16[5,24,768]{2,1,0:T(8,128)(2,1)S(1)}, u32[]{:S(2)}, u32[]{:S(2)}) collective-permute-start(bf16[5,24,768]{2,1,0:T(8,128)(2,1)S(1)} %get-tuple-element.188), channel_id=1, source_target_pairs={{0,4},{1,5},{2,6},{3,7},{4,0},{5,1},{6,2},{7,3},{8,12},{9,13},{10,... | collective-permute-start | bytes 552968 | tf_op jit(solution)/shard_map/ppermute | solution.py:651
  154.0 2.2 %collective-permute-start.32 = (bf16[4,24,768]{2,1,0:T(8,128)(2,1)S(1)}, bf16[4,24,768]{2,1,0:T(8,128)(2,1)S(1)}, u32[]{:S(2)}, u32[]{:S(2)}) collective-permute-start(bf16[4,24,768]{2,1,0:T(8,128)(2,1)S(1)} %get-tuple-element.176.refs_0_), channel_id=1, source_target_pairs={{0,4},{1,5},{2,6},{3,7},{4,0},{5,1},{6,2},{7,3},{8,12},{9,13},{10,... | collective-permute-start | bytes 442376 | tf_op jit(solution)/shard_map/ppermute | solution.py:651
  156.3 9.0 %ready.1.refs_0_.refs_11_ = bf16[6,768,768]{2,1,0:T(8,128)(2,1)} custom-call(bf16[4,24,768]{2,1,0:T(8,128)(2,1)S(1)} %get-tuple-element.176.refs_0_, f32[6,768,768]{2,1,0:T(8,128)} %refs_1_.3), custom_call_target="tpu_custom_call" | custom-call | flops 4400000000 | tf_op jit(solution)/shard_map/ready/pallas_call | solution.py:586
  167.2 3.1 %collective-permute-start.41 = (bf16[72,384]{1,0:T(8,128)(2,1)S(1)}, bf16[72,384]{1,0:T(8,128)(2,1)S(1)}, u32[]{:S(2)}, u32[]{:S(2)}) collective-permute-start(bf16[72,384]{1,0:T(8,128)(2,1)S(1)} %get-tuple-element.196), channel_id=1, source_target_pairs={{0,5},{1,4},{2,7},{3,6},{4,1},{5,0},{6,3},{7,2},{8,13},{9,12},{10,... | collective-permute-start | bytes 165896 | tf_op jit(solution)/shard_map/ppermute | solution.py:880
  171.6 2.5 %collective-permute-start.43 = (bf16[72,384]{1,0:T(8,128)(2,1)S(1)}, bf16[72,384]{1,0:T(8,128)(2,1)S(1)}, u32[]{:S(2)}, u32[]{:S(2)}) collective-permute-start(bf16[72,384]{1,0:T(8,128)(2,1)S(1)} %get-tuple-element.198), channel_id=1, source_target_pairs={{0,7},{1,6},{2,5},{3,4},{4,3},{5,2},{6,1},{7,0},{8,15},{9,14},{10,... | collective-permute-start | bytes 165896 | tf_op jit(solution)/shard_map/ppermute | solution.py:880
  175.6 2.0 collective-permute-start.39
  182.7 1.9 collective-permute-done.45.refs_3_
  184.6 2.4 %collective-permute-done.44.refs_2_ = bf16[4,72,384]{2,1,0:T(8,128)(2,1)S(1)} collective-permute-done((bf16[4,72,384]{2,1,0:T(8,128)(2,1)S(1)}, bf16[4,72,384]{2,1,0:T(8,128)(2,1)S(1)}, u32[]{:S(2)}, u32[]{:S(2)}) %collective-permute-start.44) | collective-permute-done | bytes 221216 | tf_op jit(solution)/shard_map/ppermute | solution.py:651
  188.4 14.3 %adam.1 = (f32[6,192,768]{2,1,0:T(8,128)}, f32[6,192,768]{2,1,0:T(8,128)}, f32[6,192,768]{2,1,0:T(8,128)}, bf16[6,192,768]{2,1,0:T(8,128)(2,1)}) custom-call(s32[1]{0:T(128)} %bitcast.17.position, bf16[4,72,384]{2,1,0:T(8,128)(2,1)S(1)} %merge.2.refs_0_, bf16[4,72,384]{2,1,0:T(8,128)(2,1)S(1)} %merge.3.refs_1_, ...), custom_call_target="tpu_custom_call" | custom-call | flops 22000001024 | tf_op jit(solution)/shard_map/adam/pallas_call | solution.py:622
  (167 shorter events, 54.2 us)
Async XLA Ops:
  30.5 9.7 %collective-permute-start.2 = (bf16[8,768]{1,0:T(8,128)(2,1)S(1)}, bf16[8,768]{1,0:T(8,128)(2,1)S(1)}, u32[]{:S(2)}, u32[]{:S(2)}) collective-permute-start(bf16[8,768]{1,0:T(8,128)(2,1)S(1)} %get-tuple-element.110), channel_id=1, source_target_pairs={{0,6},{1,7},{2,4},{3,5},{4,2},{5,3},{6,0},{7,1},{8,14},{9,15},{10,... | collective-permute-start | bytes 36872 | tf_op jit(solution)/shard_map/ppermute | solution.py:668
  61.3 17.8 %collective-permute-start.8 = (bf16[32,24,384]{2,1,0:T(8,128)(2,1)S(1)}, bf16[32,24,384]{2,1,0:T(8,128)(2,1)S(1)}, u32[]{:S(2)}, u32[]{:S(2)}) collective-permute-start(bf16[32,24,384]{2,1,0:T(8,128)(2,1)S(1)} %get-tuple-element.115.refs_0_), channel_id=1, source_target_pairs={{0,16},{8,24},{16,0},{24,8},{1,17},{9,25},{17,1},{25,9},{2,18},{10... | collective-permute-start | bytes 1769480 | tf_op jit(solution)/shard_map/ppermute | solution.py:651
  62.3 16.8 %collective-permute-start.9 = (bf16[32,24,384]{2,1,0:T(8,128)(2,1)S(1)}, bf16[32,24,384]{2,1,0:T(8,128)(2,1)S(1)}, u32[]{:S(2)}, u32[]{:S(2)}) collective-permute-start(bf16[32,24,384]{2,1,0:T(8,128)(2,1)S(1)} %get-tuple-element.116.refs_1_), channel_id=1, source_target_pairs={{0,1},{1,0},{2,3},{3,2},{4,5},{5,4},{6,7},{7,6},{8,9},{9,8},{10,11... | collective-permute-start | bytes 1769480 | tf_op jit(solution)/shard_map/ppermute | solution.py:651
  80.0 8.5 %collective-permute-start.10 = (bf16[16,24,384]{2,1,0:T(8,128)(2,1)S(1)}, bf16[16,24,384]{2,1,0:T(8,128)(2,1)S(1)}, u32[]{:S(2)}, u32[]{:S(2)}) collective-permute-start(bf16[16,24,384]{2,1,0:T(8,128)(2,1)S(1)} %get-tuple-element.124.refs_0_), channel_id=1, source_target_pairs={{0,1},{1,0},{2,3},{3,2},{4,5},{5,4},{6,7},{7,6},{8,9},{9,8},{10,11... | collective-permute-start | bytes 884744 | tf_op jit(solution)/shard_map/ppermute | solution.py:651
  80.9 8.2 %collective-permute-start.11 = (bf16[16,24,384]{2,1,0:T(8,128)(2,1)S(1)}, bf16[16,24,384]{2,1,0:T(8,128)(2,1)S(1)}, u32[]{:S(2)}, u32[]{:S(2)}) collective-permute-start(bf16[16,24,384]{2,1,0:T(8,128)(2,1)S(1)} %get-tuple-element.125.refs_1_), channel_id=1, source_target_pairs={{0,16},{8,24},{16,0},{24,8},{1,17},{9,25},{17,1},{25,9},{2,18},{10... | collective-permute-start | bytes 884744 | tf_op jit(solution)/shard_map/ppermute | solution.py:651
  86.4 12.2 %collective-permute-start.13 = (bf16[5,384,768]{2,1,0:T(8,128)(2,1)S(1)}, bf16[5,384,768]{2,1,0:T(8,128)(2,1)S(1)}, u32[]{:S(2)}, u32[]{:S(2)}) collective-permute-start(bf16[5,384,768]{2,1,0:T(8,128)(2,1)S(1)} %weight.8.refs_0_), channel_id=1, source_target_pairs={{0,8},{8,0},{16,24},{24,16},{1,9},{9,1},{17,25},{25,17},{2,10},{10... | collective-permute-start | bytes 8847368 | tf_op jit(solution)/shard_map/ppermute | solution.py:651
  89.8 7.6 %collective-permute-start.12 = (bf16[8,24,768]{2,1,0:T(8,128)(2,1)S(1)}, bf16[8,24,768]{2,1,0:T(8,128)(2,1)S(1)}, u32[]{:S(2)}, u32[]{:S(2)}) collective-permute-start(bf16[8,24,768]{2,1,0:T(8,128)(2,1)S(1)} %get-tuple-element.131.refs_1_), channel_id=1, source_target_pairs={{0,2},{1,3},{2,0},{3,1},{4,6},{5,7},{6,4},{7,5},{8,10},{9,11},{10,... | collective-permute-start | bytes 884744 | tf_op jit(solution)/shard_map/ppermute | solution.py:651
  98.0 20.2 %collective-permute-start.20 = (bf16[4,24,768]{2,1,0:T(8,128)(2,1)S(1)}, bf16[4,24,768]{2,1,0:T(8,128)(2,1)S(1)}, u32[]{:S(2)}, u32[]{:S(2)}) collective-permute-start(bf16[4,24,768]{2,1,0:T(8,128)(2,1)S(1)} %get-tuple-element.133.refs_0_), channel_id=1, source_target_pairs={{0,4},{1,5},{2,6},{3,7},{4,0},{5,1},{6,2},{7,3},{8,12},{9,13},{10,... | collective-permute-start | bytes 442376 | tf_op jit(solution)/shard_map/ppermute | solution.py:651
  99.5 15.9 %collective-permute-start.14 = (bf16[40,24,256]{2,1,0:T(8,128)(2,1)S(1)}, bf16[40,24,256]{2,1,0:T(8,128)(2,1)S(1)}, u32[]{:S(2)}, u32[]{:S(2)}) collective-permute-start(bf16[40,24,256]{2,1,0:T(8,128)(2,1)S(1)} %get-tuple-element.134.refs_1_), channel_id=1, source_target_pairs={{0,16},{8,24},{16,0},{24,8},{1,17},{9,25},{17,1},{25,9},{2,18},{10... | collective-permute-start | bytes 1474568 | tf_op jit(solution)/shard_map/ppermute | solution.py:651
  100.7 14.7 %collective-permute-start.15 = (bf16[40,24,256]{2,1,0:T(8,128)(2,1)S(1)}, bf16[40,24,256]{2,1,0:T(8,128)(2,1)S(1)}, u32[]{:S(2)}, u32[]{:S(2)}) collective-permute-start(bf16[40,24,256]{2,1,0:T(8,128)(2,1)S(1)} %get-tuple-element.135.refs_2_), channel_id=1, source_target_pairs={{0,1},{1,0},{2,3},{3,2},{4,5},{5,4},{6,7},{7,6},{8,9},{9,8},{10,11... | collective-permute-start | bytes 1474568 | tf_op jit(solution)/shard_map/ppermute | solution.py:651
  102.2 13.2 %collective-permute-start.16 = (bf16[40,24,256]{2,1,0:T(8,128)(2,1)S(1)}, bf16[40,24,256]{2,1,0:T(8,128)(2,1)S(1)}, u32[]{:S(2)}, u32[]{:S(2)}) collective-permute-start(bf16[40,24,256]{2,1,0:T(8,128)(2,1)S(1)} %get-tuple-element.136.refs_3_), channel_id=1, source_target_pairs={{0,2},{1,3},{2,0},{3,1},{4,6},{5,7},{6,4},{7,5},{8,10},{9,11},{10,... | collective-permute-start | bytes 1474568 | tf_op jit(solution)/shard_map/ppermute | solution.py:651
  115.3 7.8 %collective-permute-start.22 = (f32[12,768]{1,0:T(8,128)S(1)}, f32[12,768]{1,0:T(8,128)S(1)}, u32[]{:S(2)}, u32[]{:S(2)}) collective-permute-start(f32[12,768]{1,0:T(8,128)S(1)} %get-tuple-element.145.refs_0_.refs_5_), channel_id=1, source_target_pairs={{0,8},{8,0},{16,24},{24,16},{1,9},{9,1},{17,25},{25,17},{2,10},{10... | collective-permute-start | bytes 110600 | tf_op jit(solution)/shard_map/ppermute | solution.py:651
  116.1 8.4 %collective-permute-start.17 = (bf16[20,24,256]{2,1,0:T(8,128)(2,1)S(1)}, bf16[20,24,256]{2,1,0:T(8,128)(2,1)S(1)}, u32[]{:S(2)}, u32[]{:S(2)}) collective-permute-start(bf16[20,24,256]{2,1,0:T(8,128)(2,1)S(1)} %get-tuple-element.149.refs_0_), channel_id=1, source_target_pairs={{0,1},{1,0},{2,3},{3,2},{4,5},{5,4},{6,7},{7,6},{8,9},{9,8},{10,11... | collective-permute-start | bytes 737288 | tf_op jit(solution)/shard_map/ppermute | solution.py:651
  116.7 8.1 %collective-permute-start.18 = (bf16[20,24,256]{2,1,0:T(8,128)(2,1)S(1)}, bf16[20,24,256]{2,1,0:T(8,128)(2,1)S(1)}, u32[]{:S(2)}, u32[]{:S(2)}) collective-permute-start(bf16[20,24,256]{2,1,0:T(8,128)(2,1)S(1)} %get-tuple-element.150.refs_1_), channel_id=1, source_target_pairs={{0,2},{1,3},{2,0},{3,1},{4,6},{5,7},{6,4},{7,5},{8,10},{9,11},{10,... | collective-permute-start | bytes 737288 | tf_op jit(solution)/shard_map/ppermute | solution.py:651
  117.1 7.8 %collective-permute-start.19 = (bf16[20,24,256]{2,1,0:T(8,128)(2,1)S(1)}, bf16[20,24,256]{2,1,0:T(8,128)(2,1)S(1)}, u32[]{:S(2)}, u32[]{:S(2)}) collective-permute-start(bf16[20,24,256]{2,1,0:T(8,128)(2,1)S(1)} %get-tuple-element.151.refs_2_), channel_id=1, source_target_pairs={{0,16},{8,24},{16,0},{24,8},{1,17},{9,25},{17,1},{25,9},{2,18},{10... | collective-permute-start | bytes 737288 | tf_op jit(solution)/shard_map/ppermute | solution.py:651
  125.6 8.6 %collective-permute-start.24 = (bf16[24,24,256]{2,1,0:T(8,128)(2,1)S(1)}, bf16[24,24,256]{2,1,0:T(8,128)(2,1)S(1)}, u32[]{:S(2)}, u32[]{:S(2)}) collective-permute-start(bf16[24,24,256]{2,1,0:T(8,128)(2,1)S(1)} %get-tuple-element.154.refs_1_), channel_id=1, source_target_pairs={{0,1},{1,0},{2,3},{3,2},{4,5},{5,4},{6,7},{7,6},{8,9},{9,8},{10,11... | collective-permute-start | bytes 884744 | tf_op jit(solution)/shard_map/ppermute | solution.py:651
  127.1 8.0 %collective-permute-start.25 = (bf16[24,24,256]{2,1,0:T(8,128)(2,1)S(1)}, bf16[24,24,256]{2,1,0:T(8,128)(2,1)S(1)}, u32[]{:S(2)}, u32[]{:S(2)}) collective-permute-start(bf16[24,24,256]{2,1,0:T(8,128)(2,1)S(1)} %get-tuple-element.155.refs_2_), channel_id=1, source_target_pairs={{0,2},{1,3},{2,0},{3,1},{4,6},{5,7},{6,4},{7,5},{8,10},{9,11},{10,... | collective-permute-start | bytes 884744 | tf_op jit(solution)/shard_map/ppermute | solution.py:651
  128.8 8.0 %collective-permute-start.23 = (bf16[26,24,256]{2,1,0:T(8,128)(2,1)S(1)}, bf16[26,24,256]{2,1,0:T(8,128)(2,1)S(1)}, u32[]{:S(2)}, u32[]{:S(2)}) collective-permute-start(bf16[26,24,256]{2,1,0:T(8,128)(2,1)S(1)} %get-tuple-element.153.refs_0_), channel_id=1, source_target_pairs={{0,16},{8,24},{16,0},{24,8},{1,17},{9,25},{17,1},{25,9},{2,18},{10... | collective-permute-start | bytes 958472 | tf_op jit(solution)/shard_map/ppermute | solution.py:651
  137.5 6.1 %collective-permute-start.27 = (bf16[12,24,256]{2,1,0:T(8,128)(2,1)S(1)}, bf16[12,24,256]{2,1,0:T(8,128)(2,1)S(1)}, u32[]{:S(2)}, u32[]{:S(2)}) collective-permute-start(bf16[12,24,256]{2,1,0:T(8,128)(2,1)S(1)} %get-tuple-element.165), channel_id=1, source_target_pairs={{0,2},{1,3},{2,0},{3,1},{4,6},{5,7},{6,4},{7,5},{8,10},{9,11},{10,... | collective-permute-start | bytes 442376 | tf_op jit(solution)/shard_map/ppermute | solution.py:651
  138.1 6.6 %collective-permute-start.28 = (bf16[12,24,256]{2,1,0:T(8,128)(2,1)S(1)}, bf16[12,24,256]{2,1,0:T(8,128)(2,1)S(1)}, u32[]{:S(2)}, u32[]{:S(2)}) collective-permute-start(bf16[12,24,256]{2,1,0:T(8,128)(2,1)S(1)} %get-tuple-element.167), channel_id=1, source_target_pairs={{0,16},{8,24},{16,0},{24,8},{1,17},{9,25},{17,1},{25,9},{2,18},{10... | collective-permute-start | bytes 442376 | tf_op jit(solution)/shard_map/ppermute | solution.py:651
  139.3 6.1 %collective-permute-start.26 = (bf16[14,24,256]{2,1,0:T(8,128)(2,1)S(1)}, bf16[14,24,256]{2,1,0:T(8,128)(2,1)S(1)}, u32[]{:S(2)}, u32[]{:S(2)}) collective-permute-start(bf16[14,24,256]{2,1,0:T(8,128)(2,1)S(1)} %get-tuple-element.163), channel_id=1, source_target_pairs={{0,1},{1,0},{2,3},{3,2},{4,5},{5,4},{6,7},{7,6},{8,9},{9,8},{10,11... | collective-permute-start | bytes 516104 | tf_op jit(solution)/shard_map/ppermute | solution.py:651
  140.5 7.5 %collective-permute-start.33 = (bf16[10,24,256]{2,1,0:T(8,128)(2,1)S(1)}, bf16[10,24,256]{2,1,0:T(8,128)(2,1)S(1)}, u32[]{:S(2)}, u32[]{:S(2)}) collective-permute-start(bf16[10,24,256]{2,1,0:T(8,128)(2,1)S(1)} %get-tuple-element.182), channel_id=1, source_target_pairs={{0,2},{1,3},{2,0},{3,1},{4,6},{5,7},{6,4},{7,5},{8,10},{9,11},{10,... | collective-permute-start | bytes 368648 | tf_op jit(solution)/shard_map/ppermute | solution.py:651
  142.2 7.6 %collective-permute-start.34 = (bf16[10,24,256]{2,1,0:T(8,128)(2,1)S(1)}, bf16[10,24,256]{2,1,0:T(8,128)(2,1)S(1)}, u32[]{:S(2)}, u32[]{:S(2)}) collective-permute-start(bf16[10,24,256]{2,1,0:T(8,128)(2,1)S(1)} %get-tuple-element.184), channel_id=1, source_target_pairs={{0,16},{8,24},{16,0},{24,8},{1,17},{9,25},{17,1},{25,9},{2,18},{10... | collective-permute-start | bytes 368648 | tf_op jit(solution)/shard_map/ppermute | solution.py:651
  143.5 6.2 %collective-permute-start.35 = (bf16[10,24,256]{2,1,0:T(8,128)(2,1)S(1)}, bf16[10,24,256]{2,1,0:T(8,128)(2,1)S(1)}, u32[]{:S(2)}, u32[]{:S(2)}) collective-permute-start(bf16[10,24,256]{2,1,0:T(8,128)(2,1)S(1)} %get-tuple-element.186), channel_id=1, source_target_pairs={{0,1},{1,0},{2,3},{3,2},{4,5},{5,4},{6,7},{7,6},{8,9},{9,8},{10,11... | collective-permute-start | bytes 368648 | tf_op jit(solution)/shard_map/ppermute | solution.py:651
  146.0 7.3 %collective-permute-start.30 = (bf16[6,24,256]{2,1,0:T(8,128)(2,1)S(1)}, bf16[6,24,256]{2,1,0:T(8,128)(2,1)S(1)}, u32[]{:S(2)}, u32[]{:S(2)}) collective-permute-start(bf16[6,24,256]{2,1,0:T(8,128)(2,1)S(1)} %get-tuple-element.172), channel_id=1, source_target_pairs={{0,16},{8,24},{16,0},{24,8},{1,17},{9,25},{17,1},{25,9},{2,18},{10... | collective-permute-start | bytes 221192 | tf_op jit(solution)/shard_map/ppermute | solution.py:651
  150.4 15.0 %collective-permute-start.36 = (bf16[5,24,768]{2,1,0:T(8,128)(2,1)S(1)}, bf16[5,24,768]{2,1,0:T(8,128)(2,1)S(1)}, u32[]{:S(2)}, u32[]{:S(2)}) collective-permute-start(bf16[5,24,768]{2,1,0:T(8,128)(2,1)S(1)} %get-tuple-element.188), channel_id=1, source_target_pairs={{0,4},{1,5},{2,6},{3,7},{4,0},{5,1},{6,2},{7,3},{8,12},{9,13},{10,... | collective-permute-start | bytes 552968 | tf_op jit(solution)/shard_map/ppermute | solution.py:651
  154.0 11.3 %collective-permute-start.32 = (bf16[4,24,768]{2,1,0:T(8,128)(2,1)S(1)}, bf16[4,24,768]{2,1,0:T(8,128)(2,1)S(1)}, u32[]{:S(2)}, u32[]{:S(2)}) collective-permute-start(bf16[4,24,768]{2,1,0:T(8,128)(2,1)S(1)} %get-tuple-element.176.refs_0_), channel_id=1, source_target_pairs={{0,4},{1,5},{2,6},{3,7},{4,0},{5,1},{6,2},{7,3},{8,12},{9,13},{10,... | collective-permute-start | bytes 442376 | tf_op jit(solution)/shard_map/ppermute | solution.py:651
  166.4 9.2 %collective-permute-start.40 = (bf16[72,384]{1,0:T(8,128)(2,1)S(1)}, bf16[72,384]{1,0:T(8,128)(2,1)S(1)}, u32[]{:S(2)}, u32[]{:S(2)}) collective-permute-start(bf16[72,384]{1,0:T(8,128)(2,1)S(1)} %get-tuple-element.195), channel_id=1, source_target_pairs={{0,4},{1,5},{2,6},{3,7},{4,0},{5,1},{6,2},{7,3},{8,12},{9,13},{10,... | collective-permute-start | bytes 165896 | tf_op jit(solution)/shard_map/ppermute | solution.py:880
  167.2 8.4 %collective-permute-start.41 = (bf16[72,384]{1,0:T(8,128)(2,1)S(1)}, bf16[72,384]{1,0:T(8,128)(2,1)S(1)}, u32[]{:S(2)}, u32[]{:S(2)}) collective-permute-start(bf16[72,384]{1,0:T(8,128)(2,1)S(1)} %get-tuple-element.196), channel_id=1, source_target_pairs={{0,5},{1,4},{2,7},{3,6},{4,1},{5,0},{6,3},{7,2},{8,13},{9,12},{10,... | collective-permute-start | bytes 165896 | tf_op jit(solution)/shard_map/ppermute | solution.py:880
  170.3 7.3 %collective-permute-start.42 = (bf16[72,384]{1,0:T(8,128)(2,1)S(1)}, bf16[72,384]{1,0:T(8,128)(2,1)S(1)}, u32[]{:S(2)}, u32[]{:S(2)}) collective-permute-start(bf16[72,384]{1,0:T(8,128)(2,1)S(1)} %get-tuple-element.197), channel_id=1, source_target_pairs={{0,6},{1,7},{2,4},{3,5},{4,2},{5,3},{6,0},{7,1},{8,14},{9,15},{10,... | collective-permute-start | bytes 165896 | tf_op jit(solution)/shard_map/ppermute | solution.py:880
  171.6 7.0 %collective-permute-start.43 = (bf16[72,384]{1,0:T(8,128)(2,1)S(1)}, bf16[72,384]{1,0:T(8,128)(2,1)S(1)}, u32[]{:S(2)}, u32[]{:S(2)}) collective-permute-start(bf16[72,384]{1,0:T(8,128)(2,1)S(1)} %get-tuple-element.198), channel_id=1, source_target_pairs={{0,7},{1,6},{2,5},{3,4},{4,3},{5,2},{6,1},{7,0},{8,15},{9,14},{10,... | collective-permute-start | bytes 165896 | tf_op jit(solution)/shard_map/ppermute | solution.py:880
  180.7 6.2 %collective-permute-start.44 = (bf16[4,72,384]{2,1,0:T(8,128)(2,1)S(1)}, bf16[4,72,384]{2,1,0:T(8,128)(2,1)S(1)}, u32[]{:S(2)}, u32[]{:S(2)}) collective-permute-start(bf16[4,72,384]{2,1,0:T(8,128)(2,1)S(1)} %merge.2.refs_0_), channel_id=1, source_target_pairs={{0,16},{8,24},{16,0},{24,8},{1,17},{9,25},{17,1},{25,9},{2,18},{10... | collective-permute-start | bytes 663560 | tf_op jit(solution)/shard_map/ppermute | solution.py:651
  (45 other events, 246.8 us)

commit v4 on v3

--- a/solution.py
+++ b/solution.py
@@ -581,18 +581,20 @@
     out[...] = source[...].astype(out.dtype)
 
 
-def ready(after, array, kind):
-    block = pl.BlockSpec((1,) + array.shape[1:], lambda s: (s, 0, 0))
+def ready(after, array, kind, first, count, before=()):
+    block = pl.BlockSpec((1,) + array.shape[1:], lambda s: (first + s, 0, 0))
+    first_in = list(before) + list(after)
     return pl.pallas_call(
         ready_kernel,
-        grid=(array.shape[0],),
-        in_specs=[ANY] * len(after) + [block],
+        grid=(count,),
+        in_specs=[ANY] * len(first_in) + [block],
         out_specs=block,
         out_shape=far(array.shape, kind),
+        input_output_aliases={0: 0} if before else {},
         compiler_params=params(16),
-        cost_estimate=cost(4),
+        cost_estimate=cost(1.5 * count),
         name="ready",
-    )(*after, *streamed(array))
+    )(*first_in, *streamed(array))
 
 
 def to_owned(gathered, masks, position, per_owner):
@@ -656,7 +658,7 @@
     return [z_bits[::-1], y_bits + across, core]
 
 
-def gather_all(rows):
+def gather_all(rows, beside):
     columns = lax.axis_size("col")
     every = lax.axis_size("row") * columns
     scale = {"row": columns, "col": 1}
@@ -666,7 +668,11 @@
             mask = sum(scale[name] * bit for j, (name, bit) in enumerate(phase) if number >> j & 1)
             pairs = [(i, i ^ mask) for i in range(every)]
             arrived.append(lax.ppermute(rows, ("row", "col"), pairs))
-        rows = jnp.concatenate([rows] + arrived)
+        if beside:
+            rows = merge(beside, [rows] + arrived).reshape(-1, D)
+            beside = []
+        else:
+            rows = jnp.concatenate([rows] + arrived)
     return rows
 
 
@@ -929,7 +935,11 @@
     encoded, hidden, slope, normed_low, unit_one, inverse_one, unit_two, inverse_two, cls_rows = (
         feed(device, span_count, tokens, attended, w_attn_out, w_in, w_out, rows)
     )
-    loss, grad_cls = contrast(gather_all(cls_rows), span_count, pair_index, device, slots)
+    per_owner = left_basis.shape[0]
+    head = per_owner // 3
+    low_left = ready([cls_rows], left_basis, LOW, 0, head)
+    every_cls = gather_all(cls_rows, streamed(low_left))
+    loss, grad_cls = contrast(every_cls, span_count, pair_index, device, slots)
     grad_two, outer_low, vec_two = outer_grad(
         device, span_count, out_grad, grad_cls, unit_two, inverse_two, rows
     )
@@ -965,13 +975,16 @@
     project_run = Reduction(bits, 3, project_away, project_here, vec_grad)
     project_run.land(*inner_run.landing())
     grad_tokens = input_grad(project_run.sent(), grad_one, stack_low, w_qkv)
-    inner_run.land()
+    inner_run.land(*streamed(grad_tokens))
     project_run.land(*streamed(grad_tokens))
     inner_run.land()
-    project_run.land()
+    project_run.land(*inner_run.sent())
+    project_run.land(*inner_run.landing())
     for run in (outer_run, inner_run, project_run):
         run.finish()
-    low_left = ready(project_run.sent(), left_basis, LOW)
+    low_left = ready(
+        project_run.sent(), left_basis, LOW, head, per_owner - head, [low_left]
+    )
     vec_grad, *parts = to_slots(
         streamed(low_left), (project_run, inner_run, outer_run),
         (0, 1, 2, 7, 3, 4, 5, 6, 8, 9, 10, 11), owner_list,

time: 203 us -> 200 us (0.985)
  starting transfers between devices: 56.1 us -> 53.3 us
    ppermute x7, waiting for transfers between devices: 8.92 us -> 5.32 us  [gather_all(): arrived.append(lax.ppermute(rows, ('row', 'col'), pairs))]
    ppermute x36, waiting for transfers between devices: 16.7 us -> 19.9 us  [swap(): return lax.ppermute(send, step[0], [(i, i ^ step[1]) for i in range(size)])]
    ppermute x36, starting transfers between devices: 35.6 us -> 32.7 us  [swap(): return lax.ppermute(send, step[0], [(i, i ^ step[1]) for i in range(size)])]
    pallas_call x1 -> x2, Pallas kernels: 9.05 us -> 9.72 us  [ready(): pl.pallas_call(ready_kernel, grid=(count,), in_specs=[ANY] * len(first_in...]
  transfers between devices with their start and end apart: 50 -> 50, of which waited for: 23 -> 24; matrix products, arithmetic and copies ran while one was open for 0% -> 0% of each run, Pallas kernels for 30% -> 31%
where the time goes in v4:
time: 200 us
  Pallas kernels  117 us (58%)
  starting transfers between devices  53.3 us (27%)
  waiting for transfers between devices  26.9 us (13%)
    ppermute x36, starting transfers between devices, swap(): return lax.ppermute(send, step[0], [(i, i ^ step[1]) for i in range(size)])  32.7 us
    ppermute x36, waiting for transfers between devices, swap(): return lax.ppermute(send, step[0], [(i, i ^ step[1]) for i in range(size)])  19.9 us
    pallas_call x1, Pallas kernels, feed(): pl.pallas_call(feed_kernel, grid=(FF // D,), in_specs=[SMEM, SMEM, tall(D...  19.4 us
    pallas_call x6, Pallas kernels, weight_half(): pl.pallas_call(partial(weight_kernel, panels, len(after)), grid_spec=pltp...  18.9 us
    pallas_call x1, Pallas kernels, inner_grad(): pl.pallas_call(partial(inner_kernel, len(after)), grid=(bands,), in_specs...  15.5 us
    pallas_call x1, Pallas kernels, rotated_adam(): pl.pallas_call(partial(adam_kernel, masks, len(gathered)), grid_spec=pltp...  14.3 us
    pallas_call x2, Pallas kernels, unattend(): pl.pallas_call(partial(unattend_kernel, len(after), bool(sums)), grid=(co...  11.5 us
    ppermute x7, starting transfers between devices, spread(): lax.ppermute(parts[number], 'col', [(i, i ^ number) for i in range(cols)])  11.2 us
  transfers between devices with their start and end apart: 50, of which 24 were waited for; matrix products, arithmetic and copies ran while one was open for 0% of the time, Pallas kernels for 31%

profile of v4, /device:TPU:0, one launch (start us, length us, event | category | flops | bytes accessed | tf_op | source)
XLA Modules:
  0.0 199.6 jit_solution(13381765484731781078)
XLA Ops:
  0.7 10.4 %attend.1 = (bf16[768,768]{1,0:T(8,128)(2,1)}, bf16[768,768]{1,0:T(8,128)(2,1)}, bf16[768,768]{1,0:T(8,128)(2,1)}, bf16[6,6,128,256]{3,2,1,0:T(8,128)(2,1)}, bf16[768,768]{1,0:T(8,128)(2,1)S(1)}) custom-call(bf16[768,768]{1,0:T(8,128)(2,1)} %refs_1_.3, bf16[3,768,768]{2,1,0:T(8,128)(2,1)} %refs_5_.1, f32[1,9216]{1,0:T(1,128)} %bitcast.33), custom_call_target="tpu_custom_call" | custom-call | flops 11000000512 | tf_op jit(solution)/shard_map/attend/pallas_call | solution.py:103
  11.0 19.4 %feed.1 = (bf16[768,768]{1,0:T(8,128)(2,1)}, bf16[768,3072]{1,0:T(8,128)(2,1)}, bf16[768,3072]{1,0:T(8,128)(2,1)}, bf16[768,768]{1,0:T(8,128)(2,1)}, bf16[768,76...) custom-call(s32[1]{0:T(128)} %bitcast.place, ...), custom_call_target="tpu_custom_call" | custom-call | flops 22000001024 | tf_op jit(solution)/shard_map/feed/pallas_call | solution.py:190
  30.5 5.1 %collective-permute-start.2 = (bf16[8,768]{1,0:T(8,128)(2,1)S(1)}, bf16[8,768]{1,0:T(8,128)(2,1)S(1)}, u32[]{:S(2)}, u32[]{:S(2)}) collective-permute-start(bf16[8,768]{1,0:T(8,128)(2,1)S(1)} %get-tuple-element.110.refs_0_.refs_1_), channel_id=1, source_target_pairs={{0,6},{1,7},{2,4},{3,5},{4,2},{5,3},{6,0},{7,1},{8,14},{9,15},{10,... | collective-permute-start | bytes 36872 | tf_op jit(solution)/shard_map/ppermute | solution.py:670
  36.3 3.5 %ready.2.refs_0_ = bf16[6,768,768]{2,1,0:T(8,128)(2,1)} custom-call(bf16[8,768]{1,0:T(8,128)(2,1)S(1)} %get-tuple-element.110.refs_0_.refs_1_, f32[6,768,768]{2,1,0:T(8,128)} %refs_2_.1), custom_call_target="tpu_custom_call" | custom-call | flops 3300000000 | tf_op jit(solution)/shard_map/ready/pallas_call | solution.py:587
  40.2 2.4 %collective-permute-start.5 = (bf16[32,768]{1,0:T(8,128)(2,1)S(1)}, bf16[32,768]{1,0:T(8,128)(2,1)S(1)}, u32[]{:S(2)}, u32[]{:S(2)}) collective-permute-start(bf16[32,768]{1,0:T(8,128)(2,1)S(1)} %bitcast.29), channel_id=1, source_target_pairs={{0,17},{1,16},{2,19},{3,18},{4,21},{5,20},{6,23},{7,22},{8,25},{9,... | collective-permute-start | bytes 147464 | tf_op jit(solution)/shard_map/ppermute | solution.py:670
  43.7 1.6 collective-permute-done.5
  50.1 2.2 %outer.1 = (f32[768,768]{1,0:T(8,128)S(1)}, bf16[768,768]{1,0:T(8,128)(2,1)S(1)}, f32[3,768]{1,0:T(4,128)S(1)}) custom-call(s32[1]{0:T(128)} %bitcast.place, s32[32]{0:T(128)S(1)} %copy-done.5, bf16[768,768]{1,0:T(8,128)(2,1)S(1)} %copy-done.3, f32[8,768]{1,0:T(8,128)S(1)} %get-tuple-element.111.grad_cls, bf16[768,768]{1,0:T(8,128)(2,1)S(1)} %get-tuple-element.112.unit_two, ...), custom_call_target="tpu_custom_call" | custom-call | flops 5500000256 | tf_op jit(solution)/shard_map/outer/pallas_call | solution.py:251
  52.4 3.1 %weight.6.refs_0_ = bf16[4,384,768]{2,1,0:T(8,128)(2,1)S(1)} custom-call(s32[1]{0:T(128)} %bitcast.7.side, bf16[768,3072]{1,0:T(8,128)(2,1)S(1)} %bitcast.46, bf16[768,768]{1,0:T(8,128)(2,1)S(1)} %get-tuple-element.114.refs_1_.refs_2_), custom_call_target="tpu_custom_call" | custom-call | flops 8800000000 | tf_op jit(solution)/shard_map/weight/pallas_call | solution.py:288
  55.6 3.1 %weight.7 = bf16[4,384,768]{2,1,0:T(8,128)(2,1)S(1)} custom-call(s32[1]{0:T(128)} %bitcast.2.side, bf16[4,384,768]{2,1,0:T(8,128)(2,1)S(1)} %weight.6.refs_0_, bf16[768,3072]{1,0:T(8,128)(2,1)S(1)} %bitcast.46, bf16[768,768]{1,0:T(8,128)(2,1)S(1)} %get-tuple-element.114.refs_1_.refs_2_), custom_call_target="tpu_custom_call" | custom-call | flops 65999998976 | tf_op jit(solution)/shard_map/weight/pallas_call | solution.py:288
  63.1 15.5 %inner.1 = (bf16[768,3072]{1,0:T(8,128)(2,1)S(1)}, f32[768,768]{1,0:T(8,128)}, bf16[768,768]{1,0:T(8,128)(2,1)S(1)}, bf16[768,768]{1,0:T(8,128)(2,1)S(1)}, f32[7,768]{1,0:T(8,128)S(1)}) custom-call(bf16[32,24,384]{2,1,0:T(8,128)(2,1)S(1)} %get-tuple-element.115.refs_0_, bf16[32,24,384]{2,1,0:T(8,128)(2,1)S(1)} %get-tuple-element.116.refs_1_, ...), custom_call_target="tpu_custom_call" | custom-call | flops 17600000000 | tf_op jit(solution)/shard_map/inner/pallas_call | solution.py:348
  82.0 3.9 %weight.8.refs_0_ = bf16[5,384,768]{2,1,0:T(8,128)(2,1)S(1)} custom-call(s32[1]{0:T(128)} %bitcast.7.side, bf16[16,24,384]{2,1,0:T(8,128)(2,1)S(1)} %get-tuple-element.124.refs_0_, bf16[16,24,384]{2,1,0:T(8,128)(2,1)S(1)} %get-tuple-element.125.refs_1_, bf16[768,768]{1,0:T(8,128)(2,1)S(1)} %copy-done.19, bf16[768,3072]{1,0:T(8,128)(2,1)S(1)} %get-tuple-element.127.refs_3_, ...), custom_call_target="tpu_custom_call" | custom-call | flops 8800000000 | tf_op jit(solution)/shard_map/weight/pallas_call | solution.py:288
  86.0 2.1 %collective-permute-done.10.refs_2_ = bf16[16,24,384]{2,1,0:T(8,128)(2,1)S(1)} collective-permute-done((bf16[16,24,384]{2,1,0:T(8,128)(2,1)S(1)}, bf16[16,24,384]{2,1,0:T(8,128)(2,1)S(1)}, u32[]{:S(2)}, u32[]{:S(2)}) %collective-permute-start.10) | collective-permute-done | bytes 294944 | tf_op jit(solution)/shard_map/ppermute | solution.py:653
  90.0 2.1 %collective-permute-start.12 = (bf16[8,24,768]{2,1,0:T(8,128)(2,1)S(1)}, bf16[8,24,768]{2,1,0:T(8,128)(2,1)S(1)}, u32[]{:S(2)}, u32[]{:S(2)}) collective-permute-start(bf16[8,24,768]{2,1,0:T(8,128)(2,1)S(1)} %get-tuple-element.131.refs_1_), channel_id=1, source_target_pairs={{0,2},{1,3},{2,0},{3,1},{4,6},{5,7},{6,4},{7,5},{8,10},{9,11},{10,... | collective-permute-start | bytes 884744 | tf_op jit(solution)/shard_map/ppermute | solution.py:653
  92.1 4.0 %weight.9.refs_0_ = bf16[5,384,768]{2,1,0:T(8,128)(2,1)S(1)} custom-call(s32[1]{0:T(128)} %bitcast.2.side, bf16[5,384,768]{2,1,0:T(8,128)(2,1)S(1)} %weight.8.refs_0_, bf16[8,24,768]{2,1,0:T(8,128)(2,1)S(1)} %get-tuple-element.131.refs_1_, bf16[768,768]{1,0:T(8,128)(2,1)S(1)} %copy-done.19, bf16[768,3072]{1,0:T(8,128)(2,1)S(1)} %copy-done.8, ...), custom_call_target="tpu_custom_call" | custom-call | flops 65999998976 | tf_op jit(solution)/shard_map/weight/pallas_call | solution.py:288
  96.0 1.6 collective-permute-done.12.refs_2_
  98.2 2.1 %collective-permute-start.20 = (bf16[4,24,768]{2,1,0:T(8,128)(2,1)S(1)}, bf16[4,24,768]{2,1,0:T(8,128)(2,1)S(1)}, u32[]{:S(2)}, u32[]{:S(2)}) collective-permute-start(bf16[4,24,768]{2,1,0:T(8,128)(2,1)S(1)} %get-tuple-element.133.refs_0_), channel_id=1, source_target_pairs={{0,4},{1,5},{2,6},{3,7},{4,0},{5,1},{6,2},{7,3},{8,12},{9,13},{10,... | collective-permute-start | bytes 442376 | tf_op jit(solution)/shard_map/ppermute | solution.py:653
  102.4 1.7 collective-permute-start.16
  104.1 5.7 %unattend.2 = (bf16[768,2304]{1,0:T(8,128)(2,1)}, f32[2,768]{1,0:T(2,128)S(1)}) custom-call(bf16[4,24,768]{2,1,0:T(8,128)(2,1)S(1)} %get-tuple-element.133.refs_0_, bf16[40,24,256]{2,1,0:T(8,128)(2,1)S(1)} %get-tuple-element.134.refs_1_, bf16[40,24,256]{2,1,0:T(8,128)(2,1)S(1)} %get-tuple-element.135.refs_2_, ...), custom_call_target="tpu_custom_call" | custom-call | flops 8800000000 | tf_op jit(solution)/shard_map/unattend/pallas_call | solution.py:426
  109.9 5.7 %unattend.3 = (bf16[768,2304]{1,0:T(8,128)(2,1)}, f32[12,768]{1,0:T(8,128)S(1)}) custom-call(bf16[768,2304]{1,0:T(8,128)(2,1)} %get-tuple-element.142.refs_0_, bf16[768,768]{1,0:T(8,128)(2,1)S(1)} %copy-done.12, bf16[768,768]{1,0:T(8,128)(2,1)S(1)} %copy-done.13, bf16[768,768]{1,0:T(8,128)(2,1)S(1)} %copy-done.14, ...), custom_call_target="tpu_custom_call", output_to_operand_aliasing={{0}: (0, {})} | custom-call | flops 8800000000 | tf_op jit(solution)/shard_map/unattend/pallas_call | solution.py:426
  119.7 2.4 %weight.10.refs_0_ = bf16[3,384,768]{2,1,0:T(8,128)(2,1)S(1)} custom-call(s32[1]{0:T(128)} %bitcast.7.side, bf16[20,24,256]{2,1,0:T(8,128)(2,1)S(1)} %get-tuple-element.149.refs_0_, bf16[20,24,256]{2,1,0:T(8,128)(2,1)S(1)} %get-tuple-element.150.refs_1_, bf16[20,24,256]{2,1,0:T(8,128)(2,1)S(1)} %get-tuple-element.151.refs_2_, ...), custom_call_target="tpu_custom_call" | custom-call | flops 8800000000 | tf_op jit(solution)/shard_map/weight/pallas_call | solution.py:288
  122.2 2.4 %weight.11 = bf16[3,384,768]{2,1,0:T(8,128)(2,1)S(1)} custom-call(s32[1]{0:T(128)} %bitcast.2.side, bf16[3,384,768]{2,1,0:T(8,128)(2,1)S(1)} %weight.10.refs_0_, bf16[768,768]{1,0:T(8,128)(2,1)S(1)} %copy-done.4, bf16[768,2304]{1,0:T(8,128)(2,1)S(1)} %copy-done.9), custom_call_target="tpu_custom_call" | custom-call | flops 65999998976 | tf_op jit(solution)/shard_map/weight/pallas_call | solution.py:288
  130.6 4.3 %input.1.refs_0_ = f32[768,768]{1,0:T(8,128)} custom-call(bf16[26,24,256]{2,1,0:T(8,128)(2,1)S(1)} %get-tuple-element.153.refs_0_, bf16[24,24,256]{2,1,0:T(8,128)(2,1)S(1)} %get-tuple-element.154.refs_1_, bf16[24,24,256]{2,1,0:T(8,128)(2,1)S(1)} %get-tuple-element.155.refs_2_, f32[768,768]{1,0:T(8,128)S(1)} %copy-done.10, bf16[768,2304]{1,0:T(8,128)(2,1)S(1)} %copy-done.9, ...), custom_call_target="tpu_custom_call" | custom-call | flops 8800000000 | tf_op jit(solution)/shard_map/input/pallas_call | solution.py:457
  145.5 1.7 collective-permute-done.30.refs_2_
  149.3 2.0 %collective-permute-start.35 = (bf16[6,24,256]{2,1,0:T(8,128)(2,1)S(1)}, bf16[6,24,256]{2,1,0:T(8,128)(2,1)S(1)}, u32[]{:S(2)}, u32[]{:S(2)}) collective-permute-start(bf16[6,24,256]{2,1,0:T(8,128)(2,1)S(1)} %get-tuple-element.184), channel_id=1, source_target_pairs={{0,1},{1,0},{2,3},{3,2},{4,5},{5,4},{6,7},{7,6},{8,9},{9,8},{10,11... | collective-permute-start | bytes 221192 | tf_op jit(solution)/shard_map/ppermute | solution.py:653
  155.1 6.2 %ready.3.refs_0_.refs_11_ = bf16[6,768,768]{2,1,0:T(8,128)(2,1)} custom-call(bf16[6,768,768]{2,1,0:T(8,128)(2,1)} %ready.2.refs_0_, bf16[4,24,768]{2,1,0:T(8,128)(2,1)S(1)} %get-tuple-element.186.refs_1_, f32[6,768,768]{2,1,0:T(8,128)} %refs_2_.1), custom_call_target="tpu_custom_call", output_to_operand_aliasing={{}: (0, {})} | custom-call | flops 6600000000 | tf_op jit(solution)/shard_map/ready/pallas_call | solution.py:587
  163.0 1.6 collective-permute-start.40
  164.5 2.4 %collective-permute-start.41 = (bf16[72,384]{1,0:T(8,128)(2,1)S(1)}, bf16[72,384]{1,0:T(8,128)(2,1)S(1)}, u32[]{:S(2)}, u32[]{:S(2)}) collective-permute-start(bf16[72,384]{1,0:T(8,128)(2,1)S(1)} %get-tuple-element.196), channel_id=1, source_target_pairs={{0,5},{1,4},{2,7},{3,6},{4,1},{5,0},{6,3},{7,2},{8,13},{9,12},{10,... | collective-permute-start | bytes 165896 | tf_op jit(solution)/shard_map/ppermute | solution.py:886
  168.4 2.2 %collective-permute-start.43 = (bf16[72,384]{1,0:T(8,128)(2,1)S(1)}, bf16[72,384]{1,0:T(8,128)(2,1)S(1)}, u32[]{:S(2)}, u32[]{:S(2)}) collective-permute-start(bf16[72,384]{1,0:T(8,128)(2,1)S(1)} %get-tuple-element.198), channel_id=1, source_target_pairs={{0,7},{1,6},{2,5},{3,4},{4,3},{5,2},{6,1},{7,0},{8,15},{9,14},{10,... | collective-permute-start | bytes 165896 | tf_op jit(solution)/shard_map/ppermute | solution.py:886
  172.2 1.9 collective-permute-start.39
  178.5 3.0 %collective-permute-done.45.refs_3_ = bf16[4,72,384]{2,1,0:T(8,128)(2,1)S(1)} collective-permute-done((bf16[4,72,384]{2,1,0:T(8,128)(2,1)S(1)}, bf16[4,72,384]{2,1,0:T(8,128)(2,1)S(1)}, u32[]{:S(2)}, u32[]{:S(2)}) %collective-permute-start.45) | collective-permute-done | bytes 221216 | tf_op jit(solution)/shard_map/ppermute | solution.py:653
  181.5 2.4 %collective-permute-done.44.refs_2_ = bf16[4,72,384]{2,1,0:T(8,128)(2,1)S(1)} collective-permute-done((bf16[4,72,384]{2,1,0:T(8,128)(2,1)S(1)}, bf16[4,72,384]{2,1,0:T(8,128)(2,1)S(1)}, u32[]{:S(2)}, u32[]{:S(2)}) %collective-permute-start.44) | collective-permute-done | bytes 221216 | tf_op jit(solution)/shard_map/ppermute | solution.py:653
  185.3 14.3 %adam.1 = (f32[6,192,768]{2,1,0:T(8,128)}, f32[6,192,768]{2,1,0:T(8,128)}, f32[6,192,768]{2,1,0:T(8,128)}, bf16[6,192,768]{2,1,0:T(8,128)(2,1)}) custom-call(s32[1]{0:T(128)} %bitcast.18.position, bf16[4,72,384]{2,1,0:T(8,128)(2,1)S(1)} %merge.4.refs_0_, bf16[4,72,384]{2,1,0:T(8,128)(2,1)S(1)} %merge.5.refs_1_, ...), custom_call_target="tpu_custom_call" | custom-call | flops 22000001024 | tf_op jit(solution)/shard_map/adam/pallas_call | solution.py:624
  (167 shorter events, 56.3 us)
Async XLA Ops:
  30.5 9.4 %collective-permute-start.2 = (bf16[8,768]{1,0:T(8,128)(2,1)S(1)}, bf16[8,768]{1,0:T(8,128)(2,1)S(1)}, u32[]{:S(2)}, u32[]{:S(2)}) collective-permute-start(bf16[8,768]{1,0:T(8,128)(2,1)S(1)} %get-tuple-element.110.refs_0_.refs_1_), channel_id=1, source_target_pairs={{0,6},{1,7},{2,4},{3,5},{4,2},{5,3},{6,0},{7,1},{8,14},{9,15},{10,... | collective-permute-start | bytes 36872 | tf_op jit(solution)/shard_map/ppermute | solution.py:670
  61.0 17.6 %collective-permute-start.8 = (bf16[32,24,384]{2,1,0:T(8,128)(2,1)S(1)}, bf16[32,24,384]{2,1,0:T(8,128)(2,1)S(1)}, u32[]{:S(2)}, u32[]{:S(2)}) collective-permute-start(bf16[32,24,384]{2,1,0:T(8,128)(2,1)S(1)} %get-tuple-element.115.refs_0_), channel_id=1, source_target_pairs={{0,16},{8,24},{16,0},{24,8},{1,17},{9,25},{17,1},{25,9},{2,18},{10... | collective-permute-start | bytes 1769480 | tf_op jit(solution)/shard_map/ppermute | solution.py:653
  62.6 16.1 %collective-permute-start.9 = (bf16[32,24,384]{2,1,0:T(8,128)(2,1)S(1)}, bf16[32,24,384]{2,1,0:T(8,128)(2,1)S(1)}, u32[]{:S(2)}, u32[]{:S(2)}) collective-permute-start(bf16[32,24,384]{2,1,0:T(8,128)(2,1)S(1)} %get-tuple-element.116.refs_1_), channel_id=1, source_target_pairs={{0,1},{1,0},{2,3},{3,2},{4,5},{5,4},{6,7},{7,6},{8,9},{9,8},{10,11... | collective-permute-start | bytes 1769480 | tf_op jit(solution)/shard_map/ppermute | solution.py:653
  79.6 8.5 %collective-permute-start.10 = (bf16[16,24,384]{2,1,0:T(8,128)(2,1)S(1)}, bf16[16,24,384]{2,1,0:T(8,128)(2,1)S(1)}, u32[]{:S(2)}, u32[]{:S(2)}) collective-permute-start(bf16[16,24,384]{2,1,0:T(8,128)(2,1)S(1)} %get-tuple-element.124.refs_0_), channel_id=1, source_target_pairs={{0,1},{1,0},{2,3},{3,2},{4,5},{5,4},{6,7},{7,6},{8,9},{9,8},{10,11... | collective-permute-start | bytes 884744 | tf_op jit(solution)/shard_map/ppermute | solution.py:653
  81.1 8.2 %collective-permute-start.11 = (bf16[16,24,384]{2,1,0:T(8,128)(2,1)S(1)}, bf16[16,24,384]{2,1,0:T(8,128)(2,1)S(1)}, u32[]{:S(2)}, u32[]{:S(2)}) collective-permute-start(bf16[16,24,384]{2,1,0:T(8,128)(2,1)S(1)} %get-tuple-element.125.refs_1_), channel_id=1, source_target_pairs={{0,16},{8,24},{16,0},{24,8},{1,17},{9,25},{17,1},{25,9},{2,18},{10... | collective-permute-start | bytes 884744 | tf_op jit(solution)/shard_map/ppermute | solution.py:653
  86.0 14.3 %collective-permute-start.13 = (bf16[5,384,768]{2,1,0:T(8,128)(2,1)S(1)}, bf16[5,384,768]{2,1,0:T(8,128)(2,1)S(1)}, u32[]{:S(2)}, u32[]{:S(2)}) collective-permute-start(bf16[5,384,768]{2,1,0:T(8,128)(2,1)S(1)} %weight.8.refs_0_), channel_id=1, source_target_pairs={{0,8},{8,0},{16,24},{24,16},{1,9},{9,1},{17,25},{25,17},{2,10},{10... | collective-permute-start | bytes 8847368 | tf_op jit(solution)/shard_map/ppermute | solution.py:653
  90.0 7.6 %collective-permute-start.12 = (bf16[8,24,768]{2,1,0:T(8,128)(2,1)S(1)}, bf16[8,24,768]{2,1,0:T(8,128)(2,1)S(1)}, u32[]{:S(2)}, u32[]{:S(2)}) collective-permute-start(bf16[8,24,768]{2,1,0:T(8,128)(2,1)S(1)} %get-tuple-element.131.refs_1_), channel_id=1, source_target_pairs={{0,2},{1,3},{2,0},{3,1},{4,6},{5,7},{6,4},{7,5},{8,10},{9,11},{10,... | collective-permute-start | bytes 884744 | tf_op jit(solution)/shard_map/ppermute | solution.py:653
  98.2 21.5 %collective-permute-start.20 = (bf16[4,24,768]{2,1,0:T(8,128)(2,1)S(1)}, bf16[4,24,768]{2,1,0:T(8,128)(2,1)S(1)}, u32[]{:S(2)}, u32[]{:S(2)}) collective-permute-start(bf16[4,24,768]{2,1,0:T(8,128)(2,1)S(1)} %get-tuple-element.133.refs_0_), channel_id=1, source_target_pairs={{0,4},{1,5},{2,6},{3,7},{4,0},{5,1},{6,2},{7,3},{8,12},{9,13},{10,... | collective-permute-start | bytes 442376 | tf_op jit(solution)/shard_map/ppermute | solution.py:653
  101.2 14.4 %collective-permute-start.14 = (bf16[40,24,256]{2,1,0:T(8,128)(2,1)S(1)}, bf16[40,24,256]{2,1,0:T(8,128)(2,1)S(1)}, u32[]{:S(2)}, u32[]{:S(2)}) collective-permute-start(bf16[40,24,256]{2,1,0:T(8,128)(2,1)S(1)} %get-tuple-element.134.refs_1_), channel_id=1, source_target_pairs={{0,16},{8,24},{16,0},{24,8},{1,17},{9,25},{17,1},{25,9},{2,18},{10... | collective-permute-start | bytes 1474568 | tf_op jit(solution)/shard_map/ppermute | solution.py:653
  101.8 13.8 %collective-permute-start.15 = (bf16[40,24,256]{2,1,0:T(8,128)(2,1)S(1)}, bf16[40,24,256]{2,1,0:T(8,128)(2,1)S(1)}, u32[]{:S(2)}, u32[]{:S(2)}) collective-permute-start(bf16[40,24,256]{2,1,0:T(8,128)(2,1)S(1)} %get-tuple-element.135.refs_2_), channel_id=1, source_target_pairs={{0,1},{1,0},{2,3},{3,2},{4,5},{5,4},{6,7},{7,6},{8,9},{9,8},{10,11... | collective-permute-start | bytes 1474568 | tf_op jit(solution)/shard_map/ppermute | solution.py:653
  102.4 13.3 %collective-permute-start.16 = (bf16[40,24,256]{2,1,0:T(8,128)(2,1)S(1)}, bf16[40,24,256]{2,1,0:T(8,128)(2,1)S(1)}, u32[]{:S(2)}, u32[]{:S(2)}) collective-permute-start(bf16[40,24,256]{2,1,0:T(8,128)(2,1)S(1)} %get-tuple-element.136.refs_3_), channel_id=1, source_target_pairs={{0,2},{1,3},{2,0},{3,1},{4,6},{5,7},{6,4},{7,5},{8,10},{9,11},{10,... | collective-permute-start | bytes 1474568 | tf_op jit(solution)/shard_map/ppermute | solution.py:653
  115.6 9.0 %collective-permute-start.22 = (f32[12,768]{1,0:T(8,128)S(1)}, f32[12,768]{1,0:T(8,128)S(1)}, u32[]{:S(2)}, u32[]{:S(2)}) collective-permute-start(f32[12,768]{1,0:T(8,128)S(1)} %get-tuple-element.145.refs_0_.refs_5_), channel_id=1, source_target_pairs={{0,8},{8,0},{16,24},{24,16},{1,9},{9,1},{17,25},{25,17},{2,10},{10... | collective-permute-start | bytes 110600 | tf_op jit(solution)/shard_map/ppermute | solution.py:653
  116.4 8.4 %collective-permute-start.17 = (bf16[20,24,256]{2,1,0:T(8,128)(2,1)S(1)}, bf16[20,24,256]{2,1,0:T(8,128)(2,1)S(1)}, u32[]{:S(2)}, u32[]{:S(2)}) collective-permute-start(bf16[20,24,256]{2,1,0:T(8,128)(2,1)S(1)} %get-tuple-element.149.refs_0_), channel_id=1, source_target_pairs={{0,1},{1,0},{2,3},{3,2},{4,5},{5,4},{6,7},{7,6},{8,9},{9,8},{10,11... | collective-permute-start | bytes 737288 | tf_op jit(solution)/shard_map/ppermute | solution.py:653
  117.9 8.1 %collective-permute-start.18 = (bf16[20,24,256]{2,1,0:T(8,128)(2,1)S(1)}, bf16[20,24,256]{2,1,0:T(8,128)(2,1)S(1)}, u32[]{:S(2)}, u32[]{:S(2)}) collective-permute-start(bf16[20,24,256]{2,1,0:T(8,128)(2,1)S(1)} %get-tuple-element.150.refs_1_), channel_id=1, source_target_pairs={{0,2},{1,3},{2,0},{3,1},{4,6},{5,7},{6,4},{7,5},{8,10},{9,11},{10,... | collective-permute-start | bytes 737288 | tf_op jit(solution)/shard_map/ppermute | solution.py:653
  118.2 7.8 %collective-permute-start.19 = (bf16[20,24,256]{2,1,0:T(8,128)(2,1)S(1)}, bf16[20,24,256]{2,1,0:T(8,128)(2,1)S(1)}, u32[]{:S(2)}, u32[]{:S(2)}) collective-permute-start(bf16[20,24,256]{2,1,0:T(8,128)(2,1)S(1)} %get-tuple-element.151.refs_2_), channel_id=1, source_target_pairs={{0,16},{8,24},{16,0},{24,8},{1,17},{9,25},{17,1},{25,9},{2,18},{10... | collective-permute-start | bytes 737288 | tf_op jit(solution)/shard_map/ppermute | solution.py:653
  126.8 10.3 %collective-permute-start.28 = (bf16[24,24,256]{2,1,0:T(8,128)(2,1)S(1)}, bf16[24,24,256]{2,1,0:T(8,128)(2,1)S(1)}, u32[]{:S(2)}, u32[]{:S(2)}) collective-permute-start(bf16[24,24,256]{2,1,0:T(8,128)(2,1)S(1)} %get-tuple-element.154.refs_1_), channel_id=1, source_target_pairs={{0,1},{1,0},{2,3},{3,2},{4,5},{5,4},{6,7},{7,6},{8,9},{9,8},{10,11... | collective-permute-start | bytes 884744 | tf_op jit(solution)/shard_map/ppermute | solution.py:653
  128.0 9.9 %collective-permute-start.29 = (bf16[24,24,256]{2,1,0:T(8,128)(2,1)S(1)}, bf16[24,24,256]{2,1,0:T(8,128)(2,1)S(1)}, u32[]{:S(2)}, u32[]{:S(2)}) collective-permute-start(bf16[24,24,256]{2,1,0:T(8,128)(2,1)S(1)} %get-tuple-element.155.refs_2_), channel_id=1, source_target_pairs={{0,2},{1,3},{2,0},{3,1},{4,6},{5,7},{6,4},{7,5},{8,10},{9,11},{10,... | collective-permute-start | bytes 884744 | tf_op jit(solution)/shard_map/ppermute | solution.py:653
  129.1 9.0 %collective-permute-start.27 = (bf16[26,24,256]{2,1,0:T(8,128)(2,1)S(1)}, bf16[26,24,256]{2,1,0:T(8,128)(2,1)S(1)}, u32[]{:S(2)}, u32[]{:S(2)}) collective-permute-start(bf16[26,24,256]{2,1,0:T(8,128)(2,1)S(1)} %get-tuple-element.153.refs_0_), channel_id=1, source_target_pairs={{0,16},{8,24},{16,0},{24,8},{1,17},{9,25},{17,1},{25,9},{2,18},{10... | collective-permute-start | bytes 958472 | tf_op jit(solution)/shard_map/ppermute | solution.py:653
  135.5 6.3 %collective-permute-start.23 = (bf16[10,24,256]{2,1,0:T(8,128)(2,1)S(1)}, bf16[10,24,256]{2,1,0:T(8,128)(2,1)S(1)}, u32[]{:S(2)}, u32[]{:S(2)}) collective-permute-start(bf16[10,24,256]{2,1,0:T(8,128)(2,1)S(1)} %get-tuple-element.162), channel_id=1, source_target_pairs={{0,2},{1,3},{2,0},{3,1},{4,6},{5,7},{6,4},{7,5},{8,10},{9,11},{10,... | collective-permute-start | bytes 368648 | tf_op jit(solution)/shard_map/ppermute | solution.py:653
  135.9 6.8 %collective-permute-start.24 = (bf16[10,24,256]{2,1,0:T(8,128)(2,1)S(1)}, bf16[10,24,256]{2,1,0:T(8,128)(2,1)S(1)}, u32[]{:S(2)}, u32[]{:S(2)}) collective-permute-start(bf16[10,24,256]{2,1,0:T(8,128)(2,1)S(1)} %get-tuple-element.164), channel_id=1, source_target_pairs={{0,16},{8,24},{16,0},{24,8},{1,17},{9,25},{17,1},{25,9},{2,18},{10... | collective-permute-start | bytes 368648 | tf_op jit(solution)/shard_map/ppermute | solution.py:653
  138.8 6.0 %collective-permute-start.31 = (bf16[12,24,256]{2,1,0:T(8,128)(2,1)S(1)}, bf16[12,24,256]{2,1,0:T(8,128)(2,1)S(1)}, u32[]{:S(2)}, u32[]{:S(2)}) collective-permute-start(bf16[12,24,256]{2,1,0:T(8,128)(2,1)S(1)} %get-tuple-element.175), channel_id=1, source_target_pairs={{0,2},{1,3},{2,0},{3,1},{4,6},{5,7},{6,4},{7,5},{8,10},{9,11},{10,... | collective-permute-start | bytes 442376 | tf_op jit(solution)/shard_map/ppermute | solution.py:653
  143.3 8.5 %collective-permute-start.26 = (bf16[5,24,768]{2,1,0:T(8,128)(2,1)S(1)}, bf16[5,24,768]{2,1,0:T(8,128)(2,1)S(1)}, u32[]{:S(2)}, u32[]{:S(2)}) collective-permute-start(bf16[5,24,768]{2,1,0:T(8,128)(2,1)S(1)} %get-tuple-element.167.refs_0_), channel_id=1, source_target_pairs={{0,4},{1,5},{2,6},{3,7},{4,0},{5,1},{6,2},{7,3},{8,12},{9,13},{10,... | collective-permute-start | bytes 552968 | tf_op jit(solution)/shard_map/ppermute | solution.py:653
  154.2 7.7 %collective-permute-start.36 = (bf16[4,24,768]{2,1,0:T(8,128)(2,1)S(1)}, bf16[4,24,768]{2,1,0:T(8,128)(2,1)S(1)}, u32[]{:S(2)}, u32[]{:S(2)}) collective-permute-start(bf16[4,24,768]{2,1,0:T(8,128)(2,1)S(1)} %get-tuple-element.186.refs_1_), channel_id=1, source_target_pairs={{0,4},{1,5},{2,6},{3,7},{4,0},{5,1},{6,2},{7,3},{8,12},{9,13},{10,... | collective-permute-start | bytes 442376 | tf_op jit(solution)/shard_map/ppermute | solution.py:653
  163.0 9.3 %collective-permute-start.40 = (bf16[72,384]{1,0:T(8,128)(2,1)S(1)}, bf16[72,384]{1,0:T(8,128)(2,1)S(1)}, u32[]{:S(2)}, u32[]{:S(2)}) collective-permute-start(bf16[72,384]{1,0:T(8,128)(2,1)S(1)} %get-tuple-element.195), channel_id=1, source_target_pairs={{0,4},{1,5},{2,6},{3,7},{4,0},{5,1},{6,2},{7,3},{8,12},{9,13},{10,... | collective-permute-start | bytes 165896 | tf_op jit(solution)/shard_map/ppermute | solution.py:886
  164.5 7.7 %collective-permute-start.41 = (bf16[72,384]{1,0:T(8,128)(2,1)S(1)}, bf16[72,384]{1,0:T(8,128)(2,1)S(1)}, u32[]{:S(2)}, u32[]{:S(2)}) collective-permute-start(bf16[72,384]{1,0:T(8,128)(2,1)S(1)} %get-tuple-element.196), channel_id=1, source_target_pairs={{0,5},{1,4},{2,7},{3,6},{4,1},{5,0},{6,3},{7,2},{8,13},{9,12},{10,... | collective-permute-start | bytes 165896 | tf_op jit(solution)/shard_map/ppermute | solution.py:886
  166.9 7.2 %collective-permute-start.42 = (bf16[72,384]{1,0:T(8,128)(2,1)S(1)}, bf16[72,384]{1,0:T(8,128)(2,1)S(1)}, u32[]{:S(2)}, u32[]{:S(2)}) collective-permute-start(bf16[72,384]{1,0:T(8,128)(2,1)S(1)} %get-tuple-element.197), channel_id=1, source_target_pairs={{0,6},{1,7},{2,4},{3,5},{4,2},{5,3},{6,0},{7,1},{8,14},{9,15},{10,... | collective-permute-start | bytes 165896 | tf_op jit(solution)/shard_map/ppermute | solution.py:886
  168.4 7.0 %collective-permute-start.43 = (bf16[72,384]{1,0:T(8,128)(2,1)S(1)}, bf16[72,384]{1,0:T(8,128)(2,1)S(1)}, u32[]{:S(2)}, u32[]{:S(2)}) collective-permute-start(bf16[72,384]{1,0:T(8,128)(2,1)S(1)} %get-tuple-element.198), channel_id=1, source_target_pairs={{0,7},{1,6},{2,5},{3,4},{4,3},{5,2},{6,1},{7,0},{8,15},{9,14},{10,... | collective-permute-start | bytes 165896 | tf_op jit(solution)/shard_map/ppermute | solution.py:886
  170.7 6.2 %collective-permute-start.37 = (bf16[72,384]{1,0:T(8,128)(2,1)S(1)}, bf16[72,384]{1,0:T(8,128)(2,1)S(1)}, u32[]{:S(2)}, u32[]{:S(2)}) collective-permute-start(bf16[72,384]{1,0:T(8,128)(2,1)S(1)} %get-tuple-element.192), channel_id=1, source_target_pairs={{0,1},{1,0},{2,3},{3,2},{4,5},{5,4},{6,7},{7,6},{8,9},{9,8},{10,11... | collective-permute-start | bytes 165896 | tf_op jit(solution)/shard_map/ppermute | solution.py:886
  175.5 6.0 %collective-permute-start.45 = (bf16[4,72,384]{2,1,0:T(8,128)(2,1)S(1)}, bf16[4,72,384]{2,1,0:T(8,128)(2,1)S(1)}, u32[]{:S(2)}, u32[]{:S(2)}) collective-permute-start(bf16[4,72,384]{2,1,0:T(8,128)(2,1)S(1)} %merge.5.refs_1_), channel_id=1, source_target_pairs={{0,16},{8,24},{16,0},{24,8},{1,17},{9,25},{17,1},{25,9},{2,18},{10... | collective-permute-start | bytes 663560 | tf_op jit(solution)/shard_map/ppermute | solution.py:653
  177.4 6.5 %collective-permute-start.44 = (bf16[4,72,384]{2,1,0:T(8,128)(2,1)S(1)}, bf16[4,72,384]{2,1,0:T(8,128)(2,1)S(1)}, u32[]{:S(2)}, u32[]{:S(2)}) collective-permute-start(bf16[4,72,384]{2,1,0:T(8,128)(2,1)S(1)} %merge.4.refs_0_), channel_id=1, source_target_pairs={{0,16},{8,24},{16,0},{24,8},{1,17},{9,25},{17,1},{25,9},{2,18},{10... | collective-permute-start | bytes 663560 | tf_op jit(solution)/shard_map/ppermute | solution.py:653
  178.0 6.5 %collective-permute-start.47 = (bf16[4,72,384]{2,1,0:T(8,128)(2,1)S(1)}, bf16[4,72,384]{2,1,0:T(8,128)(2,1)S(1)}, u32[]{:S(2)}, u32[]{:S(2)}) collective-permute-start(bf16[4,72,384]{2,1,0:T(8,128)(2,1)S(1)} %merge.5.refs_1_), channel_id=1, source_target_pairs={{0,8},{8,0},{16,24},{24,16},{1,9},{9,1},{17,25},{25,17},{2,10},{10... | collective-permute-start | bytes 663560 | tf_op jit(solution)/shard_map/ppermute | solution.py:653
  178.0 6.5 %collective-permute-start.46 = (bf16[4,72,384]{2,1,0:T(8,128)(2,1)S(1)}, bf16[4,72,384]{2,1,0:T(8,128)(2,1)S(1)}, u32[]{:S(2)}, u32[]{:S(2)}) collective-permute-start(bf16[4,72,384]{2,1,0:T(8,128)(2,1)S(1)} %merge.4.refs_0_), channel_id=1, source_target_pairs={{0,8},{8,0},{16,24},{24,16},{1,9},{9,1},{17,25},{25,17},{2,10},{10... | collective-permute-start | bytes 663560 | tf_op jit(solution)/shard_map/ppermute | solution.py:653
  (45 other events, 213.1 us)

commit v5 on v4

--- a/solution.py
+++ b/solution.py
@@ -132,7 +132,8 @@
 
 def gelu_pair(x):
     cdf = 0.5 + 0.5 * lax.erf(x * 0.7071067811865476)
-    return x * cdf, cdf + x * jnp.exp(-0.5 * x * x) * 0.3989422804014327
+    gauss = jnp.exp2(x * x * -0.7213475204444817)
+    return x * cdf, cdf + x * gauss * 0.3989422804014327
 
 
 def feed_kernel(

time: 200 us -> 199 us (level)
  no operation moved by 1% of the time
where the time goes in v5:
time: 199 us
  Pallas kernels  117 us (59%)
  starting transfers between devices  53.2 us (27%)
  waiting for transfers between devices  27 us (14%)
    ppermute x36, starting transfers between devices, swap(): return lax.ppermute(send, step[0], [(i, i ^ step[1]) for i in range(size)])  32.7 us
    ppermute x36, waiting for transfers between devices, swap(): return lax.ppermute(send, step[0], [(i, i ^ step[1]) for i in range(size)])  19.9 us
    pallas_call x1, Pallas kernels, feed(): pl.pallas_call(feed_kernel, grid=(FF // D,), in_specs=[SMEM, SMEM, tall(D...  19.1 us
    pallas_call x6, Pallas kernels, weight_half(): pl.pallas_call(partial(weight_kernel, panels, len(after)), grid_spec=pltp...  18.9 us
    pallas_call x1, Pallas kernels, inner_grad(): pl.pallas_call(partial(inner_kernel, len(after)), grid=(bands,), in_specs...  15.5 us
    pallas_call x1, Pallas kernels, rotated_adam(): pl.pallas_call(partial(adam_kernel, masks, len(gathered)), grid_spec=pltp...  14.3 us
    pallas_call x2, Pallas kernels, unattend(): pl.pallas_call(partial(unattend_kernel, len(after), bool(sums)), grid=(co...  11.5 us
    ppermute x7, starting transfers between devices, spread(): lax.ppermute(parts[number], 'col', [(i, i ^ number) for i in range(cols)])  11.2 us
  transfers between devices with their start and end apart: 50, of which 24 were waited for; matrix products, arithmetic and copies ran while one was open for 0% of the time, Pallas kernels for 31%

profile of v5, /device:TPU:0, one launch (start us, length us, event | category | flops | bytes accessed | tf_op | source)
XLA Modules:
  0.0 199.3 jit_solution(15353605603880101830)
XLA Ops:
  0.7 10.4 %attend.1 = (bf16[768,768]{1,0:T(8,128)(2,1)}, bf16[768,768]{1,0:T(8,128)(2,1)}, bf16[768,768]{1,0:T(8,128)(2,1)}, bf16[6,6,128,256]{3,2,1,0:T(8,128)(2,1)}, bf16[768,768]{1,0:T(8,128)(2,1)S(1)}) custom-call(bf16[768,768]{1,0:T(8,128)(2,1)} %refs_1_.3, bf16[3,768,768]{2,1,0:T(8,128)(2,1)} %refs_5_.1, f32[1,9216]{1,0:T(1,128)} %bitcast.33), custom_call_target="tpu_custom_call" | custom-call | flops 11000000512 | tf_op jit(solution)/shard_map/attend/pallas_call | solution.py:103
  11.0 19.1 %feed.1 = (bf16[768,768]{1,0:T(8,128)(2,1)}, bf16[768,3072]{1,0:T(8,128)(2,1)}, bf16[768,3072]{1,0:T(8,128)(2,1)}, bf16[768,768]{1,0:T(8,128)(2,1)}, bf16[768,76...) custom-call(s32[1]{0:T(128)} %bitcast.place, ...), custom_call_target="tpu_custom_call" | custom-call | flops 22000001024 | tf_op jit(solution)/shard_map/feed/pallas_call | solution.py:191
  30.1 5.1 %collective-permute-start.2 = (bf16[8,768]{1,0:T(8,128)(2,1)S(1)}, bf16[8,768]{1,0:T(8,128)(2,1)S(1)}, u32[]{:S(2)}, u32[]{:S(2)}) collective-permute-start(bf16[8,768]{1,0:T(8,128)(2,1)S(1)} %get-tuple-element.110.refs_0_.refs_1_), channel_id=1, source_target_pairs={{0,6},{1,7},{2,4},{3,5},{4,2},{5,3},{6,0},{7,1},{8,14},{9,15},{10,... | collective-permute-start | bytes 36872 | tf_op jit(solution)/shard_map/ppermute | solution.py:671
  35.9 3.5 %ready.2.refs_0_ = bf16[6,768,768]{2,1,0:T(8,128)(2,1)} custom-call(bf16[8,768]{1,0:T(8,128)(2,1)S(1)} %get-tuple-element.110.refs_0_.refs_1_, f32[6,768,768]{2,1,0:T(8,128)} %refs_2_.1), custom_call_target="tpu_custom_call" | custom-call | flops 3300000000 | tf_op jit(solution)/shard_map/ready/pallas_call | solution.py:588
  39.9 2.4 %collective-permute-start.5 = (bf16[32,768]{1,0:T(8,128)(2,1)S(1)}, bf16[32,768]{1,0:T(8,128)(2,1)S(1)}, u32[]{:S(2)}, u32[]{:S(2)}) collective-permute-start(bf16[32,768]{1,0:T(8,128)(2,1)S(1)} %bitcast.29), channel_id=1, source_target_pairs={{0,17},{1,16},{2,19},{3,18},{4,21},{5,20},{6,23},{7,22},{8,25},{9,... | collective-permute-start | bytes 147464 | tf_op jit(solution)/shard_map/ppermute | solution.py:671
  43.4 1.6 collective-permute-done.5
  49.8 2.2 %outer.1 = (f32[768,768]{1,0:T(8,128)S(1)}, bf16[768,768]{1,0:T(8,128)(2,1)S(1)}, f32[3,768]{1,0:T(4,128)S(1)}) custom-call(s32[1]{0:T(128)} %bitcast.place, s32[32]{0:T(128)S(1)} %copy-done.5, bf16[768,768]{1,0:T(8,128)(2,1)S(1)} %copy-done.3, f32[8,768]{1,0:T(8,128)S(1)} %get-tuple-element.111.grad_cls, bf16[768,768]{1,0:T(8,128)(2,1)S(1)} %get-tuple-element.112.unit_two, ...), custom_call_target="tpu_custom_call" | custom-call | flops 5500000256 | tf_op jit(solution)/shard_map/outer/pallas_call | solution.py:252
  52.0 3.1 %weight.6.refs_0_ = bf16[4,384,768]{2,1,0:T(8,128)(2,1)S(1)} custom-call(s32[1]{0:T(128)} %bitcast.7.side, bf16[768,3072]{1,0:T(8,128)(2,1)S(1)} %bitcast.46, bf16[768,768]{1,0:T(8,128)(2,1)S(1)} %get-tuple-element.114.refs_1_.refs_2_), custom_call_target="tpu_custom_call" | custom-call | flops 8800000000 | tf_op jit(solution)/shard_map/weight/pallas_call | solution.py:289
  55.3 3.1 %weight.7 = bf16[4,384,768]{2,1,0:T(8,128)(2,1)S(1)} custom-call(s32[1]{0:T(128)} %bitcast.2.side, bf16[4,384,768]{2,1,0:T(8,128)(2,1)S(1)} %weight.6.refs_0_, bf16[768,3072]{1,0:T(8,128)(2,1)S(1)} %bitcast.46, bf16[768,768]{1,0:T(8,128)(2,1)S(1)} %get-tuple-element.114.refs_1_.refs_2_), custom_call_target="tpu_custom_call" | custom-call | flops 65999998976 | tf_op jit(solution)/shard_map/weight/pallas_call | solution.py:289
  62.7 15.5 %inner.1 = (bf16[768,3072]{1,0:T(8,128)(2,1)S(1)}, f32[768,768]{1,0:T(8,128)}, bf16[768,768]{1,0:T(8,128)(2,1)S(1)}, bf16[768,768]{1,0:T(8,128)(2,1)S(1)}, f32[7,768]{1,0:T(8,128)S(1)}) custom-call(bf16[32,24,384]{2,1,0:T(8,128)(2,1)S(1)} %get-tuple-element.115.refs_0_, bf16[32,24,384]{2,1,0:T(8,128)(2,1)S(1)} %get-tuple-element.116.refs_1_, ...), custom_call_target="tpu_custom_call" | custom-call | flops 17600000000 | tf_op jit(solution)/shard_map/inner/pallas_call | solution.py:349
  81.7 3.9 %weight.8.refs_0_ = bf16[5,384,768]{2,1,0:T(8,128)(2,1)S(1)} custom-call(s32[1]{0:T(128)} %bitcast.7.side, bf16[16,24,384]{2,1,0:T(8,128)(2,1)S(1)} %get-tuple-element.124.refs_0_, bf16[16,24,384]{2,1,0:T(8,128)(2,1)S(1)} %get-tuple-element.125.refs_1_, bf16[768,768]{1,0:T(8,128)(2,1)S(1)} %copy-done.19, bf16[768,3072]{1,0:T(8,128)(2,1)S(1)} %get-tuple-element.127.refs_3_, ...), custom_call_target="tpu_custom_call" | custom-call | flops 8800000000 | tf_op jit(solution)/shard_map/weight/pallas_call | solution.py:289
  85.7 2.1 %collective-permute-done.10.refs_2_ = bf16[16,24,384]{2,1,0:T(8,128)(2,1)S(1)} collective-permute-done((bf16[16,24,384]{2,1,0:T(8,128)(2,1)S(1)}, bf16[16,24,384]{2,1,0:T(8,128)(2,1)S(1)}, u32[]{:S(2)}, u32[]{:S(2)}) %collective-permute-start.10) | collective-permute-done | bytes 294944 | tf_op jit(solution)/shard_map/ppermute | solution.py:654
  89.6 2.1 %collective-permute-start.12 = (bf16[8,24,768]{2,1,0:T(8,128)(2,1)S(1)}, bf16[8,24,768]{2,1,0:T(8,128)(2,1)S(1)}, u32[]{:S(2)}, u32[]{:S(2)}) collective-permute-start(bf16[8,24,768]{2,1,0:T(8,128)(2,1)S(1)} %get-tuple-element.131.refs_1_), channel_id=1, source_target_pairs={{0,2},{1,3},{2,0},{3,1},{4,6},{5,7},{6,4},{7,5},{8,10},{9,11},{10,... | collective-permute-start | bytes 884744 | tf_op jit(solution)/shard_map/ppermute | solution.py:654
  91.7 4.0 %weight.9.refs_0_ = bf16[5,384,768]{2,1,0:T(8,128)(2,1)S(1)} custom-call(s32[1]{0:T(128)} %bitcast.2.side, bf16[5,384,768]{2,1,0:T(8,128)(2,1)S(1)} %weight.8.refs_0_, bf16[8,24,768]{2,1,0:T(8,128)(2,1)S(1)} %get-tuple-element.131.refs_1_, bf16[768,768]{1,0:T(8,128)(2,1)S(1)} %copy-done.19, bf16[768,3072]{1,0:T(8,128)(2,1)S(1)} %copy-done.8, ...), custom_call_target="tpu_custom_call" | custom-call | flops 65999998976 | tf_op jit(solution)/shard_map/weight/pallas_call | solution.py:289
  95.7 1.6 collective-permute-done.12.refs_2_
  97.9 2.1 %collective-permute-start.20 = (bf16[4,24,768]{2,1,0:T(8,128)(2,1)S(1)}, bf16[4,24,768]{2,1,0:T(8,128)(2,1)S(1)}, u32[]{:S(2)}, u32[]{:S(2)}) collective-permute-start(bf16[4,24,768]{2,1,0:T(8,128)(2,1)S(1)} %get-tuple-element.133.refs_0_), channel_id=1, source_target_pairs={{0,4},{1,5},{2,6},{3,7},{4,0},{5,1},{6,2},{7,3},{8,12},{9,13},{10,... | collective-permute-start | bytes 442376 | tf_op jit(solution)/shard_map/ppermute | solution.py:654
  102.0 1.7 collective-permute-start.16
  103.8 5.7 %unattend.2 = (bf16[768,2304]{1,0:T(8,128)(2,1)}, f32[2,768]{1,0:T(2,128)S(1)}) custom-call(bf16[4,24,768]{2,1,0:T(8,128)(2,1)S(1)} %get-tuple-element.133.refs_0_, bf16[40,24,256]{2,1,0:T(8,128)(2,1)S(1)} %get-tuple-element.134.refs_1_, bf16[40,24,256]{2,1,0:T(8,128)(2,1)S(1)} %get-tuple-element.135.refs_2_, ...), custom_call_target="tpu_custom_call" | custom-call | flops 8800000000 | tf_op jit(solution)/shard_map/unattend/pallas_call | solution.py:427
  109.5 5.7 %unattend.3 = (bf16[768,2304]{1,0:T(8,128)(2,1)}, f32[12,768]{1,0:T(8,128)S(1)}) custom-call(bf16[768,2304]{1,0:T(8,128)(2,1)} %get-tuple-element.142.refs_0_, bf16[768,768]{1,0:T(8,128)(2,1)S(1)} %copy-done.12, bf16[768,768]{1,0:T(8,128)(2,1)S(1)} %copy-done.13, bf16[768,768]{1,0:T(8,128)(2,1)S(1)} %copy-done.14, ...), custom_call_target="tpu_custom_call", output_to_operand_aliasing={{0}: (0, {})} | custom-call | flops 8800000000 | tf_op jit(solution)/shard_map/unattend/pallas_call | solution.py:427
  119.3 2.4 %weight.10.refs_0_ = bf16[3,384,768]{2,1,0:T(8,128)(2,1)S(1)} custom-call(s32[1]{0:T(128)} %bitcast.7.side, bf16[20,24,256]{2,1,0:T(8,128)(2,1)S(1)} %get-tuple-element.149.refs_0_, bf16[20,24,256]{2,1,0:T(8,128)(2,1)S(1)} %get-tuple-element.150.refs_1_, bf16[20,24,256]{2,1,0:T(8,128)(2,1)S(1)} %get-tuple-element.151.refs_2_, ...), custom_call_target="tpu_custom_call" | custom-call | flops 8800000000 | tf_op jit(solution)/shard_map/weight/pallas_call | solution.py:289
  121.8 2.4 %weight.11 = bf16[3,384,768]{2,1,0:T(8,128)(2,1)S(1)} custom-call(s32[1]{0:T(128)} %bitcast.2.side, bf16[3,384,768]{2,1,0:T(8,128)(2,1)S(1)} %weight.10.refs_0_, bf16[768,768]{1,0:T(8,128)(2,1)S(1)} %copy-done.4, bf16[768,2304]{1,0:T(8,128)(2,1)S(1)} %copy-done.9), custom_call_target="tpu_custom_call" | custom-call | flops 65999998976 | tf_op jit(solution)/shard_map/weight/pallas_call | solution.py:289
  130.3 4.3 %input.1.refs_0_ = f32[768,768]{1,0:T(8,128)} custom-call(bf16[26,24,256]{2,1,0:T(8,128)(2,1)S(1)} %get-tuple-element.153.refs_0_, bf16[24,24,256]{2,1,0:T(8,128)(2,1)S(1)} %get-tuple-element.154.refs_1_, bf16[24,24,256]{2,1,0:T(8,128)(2,1)S(1)} %get-tuple-element.155.refs_2_, f32[768,768]{1,0:T(8,128)S(1)} %copy-done.10, bf16[768,2304]{1,0:T(8,128)(2,1)S(1)} %copy-done.9, ...), custom_call_target="tpu_custom_call" | custom-call | flops 8800000000 | tf_op jit(solution)/shard_map/input/pallas_call | solution.py:458
  145.1 1.8 collective-permute-done.30.refs_2_
  148.9 2.0 %collective-permute-start.35 = (bf16[6,24,256]{2,1,0:T(8,128)(2,1)S(1)}, bf16[6,24,256]{2,1,0:T(8,128)(2,1)S(1)}, u32[]{:S(2)}, u32[]{:S(2)}) collective-permute-start(bf16[6,24,256]{2,1,0:T(8,128)(2,1)S(1)} %get-tuple-element.184), channel_id=1, source_target_pairs={{0,1},{1,0},{2,3},{3,2},{4,5},{5,4},{6,7},{7,6},{8,9},{9,8},{10,11... | collective-permute-start | bytes 221192 | tf_op jit(solution)/shard_map/ppermute | solution.py:654
  154.8 6.2 %ready.3.refs_0_.refs_11_ = bf16[6,768,768]{2,1,0:T(8,128)(2,1)} custom-call(bf16[6,768,768]{2,1,0:T(8,128)(2,1)} %ready.2.refs_0_, bf16[4,24,768]{2,1,0:T(8,128)(2,1)S(1)} %get-tuple-element.186.refs_1_, f32[6,768,768]{2,1,0:T(8,128)} %refs_2_.1), custom_call_target="tpu_custom_call", output_to_operand_aliasing={{}: (0, {})} | custom-call | flops 6600000000 | tf_op jit(solution)/shard_map/ready/pallas_call | solution.py:588
  162.6 1.6 collective-permute-start.40
  164.2 2.4 %collective-permute-start.41 = (bf16[72,384]{1,0:T(8,128)(2,1)S(1)}, bf16[72,384]{1,0:T(8,128)(2,1)S(1)}, u32[]{:S(2)}, u32[]{:S(2)}) collective-permute-start(bf16[72,384]{1,0:T(8,128)(2,1)S(1)} %get-tuple-element.196), channel_id=1, source_target_pairs={{0,5},{1,4},{2,7},{3,6},{4,1},{5,0},{6,3},{7,2},{8,13},{9,12},{10,... | collective-permute-start | bytes 165896 | tf_op jit(solution)/shard_map/ppermute | solution.py:887
  168.1 2.2 %collective-permute-start.43 = (bf16[72,384]{1,0:T(8,128)(2,1)S(1)}, bf16[72,384]{1,0:T(8,128)(2,1)S(1)}, u32[]{:S(2)}, u32[]{:S(2)}) collective-permute-start(bf16[72,384]{1,0:T(8,128)(2,1)S(1)} %get-tuple-element.198), channel_id=1, source_target_pairs={{0,7},{1,6},{2,5},{3,4},{4,3},{5,2},{6,1},{7,0},{8,15},{9,14},{10,... | collective-permute-start | bytes 165896 | tf_op jit(solution)/shard_map/ppermute | solution.py:887
  171.9 1.9 collective-permute-start.39
  178.2 3.0 %collective-permute-done.45.refs_3_ = bf16[4,72,384]{2,1,0:T(8,128)(2,1)S(1)} collective-permute-done((bf16[4,72,384]{2,1,0:T(8,128)(2,1)S(1)}, bf16[4,72,384]{2,1,0:T(8,128)(2,1)S(1)}, u32[]{:S(2)}, u32[]{:S(2)}) %collective-permute-start.45) | collective-permute-done | bytes 221216 | tf_op jit(solution)/shard_map/ppermute | solution.py:654
  181.1 2.4 %collective-permute-done.44.refs_2_ = bf16[4,72,384]{2,1,0:T(8,128)(2,1)S(1)} collective-permute-done((bf16[4,72,384]{2,1,0:T(8,128)(2,1)S(1)}, bf16[4,72,384]{2,1,0:T(8,128)(2,1)S(1)}, u32[]{:S(2)}, u32[]{:S(2)}) %collective-permute-start.44) | collective-permute-done | bytes 221216 | tf_op jit(solution)/shard_map/ppermute | solution.py:654
  185.0 14.3 %adam.1 = (f32[6,192,768]{2,1,0:T(8,128)}, f32[6,192,768]{2,1,0:T(8,128)}, f32[6,192,768]{2,1,0:T(8,128)}, bf16[6,192,768]{2,1,0:T(8,128)(2,1)}) custom-call(s32[1]{0:T(128)} %bitcast.18.position, bf16[4,72,384]{2,1,0:T(8,128)(2,1)S(1)} %merge.4.refs_0_, bf16[4,72,384]{2,1,0:T(8,128)(2,1)S(1)} %merge.5.refs_1_, ...), custom_call_target="tpu_custom_call" | custom-call | flops 22000001024 | tf_op jit(solution)/shard_map/adam/pallas_call | solution.py:625
  (167 shorter events, 56.3 us)
Async XLA Ops:
  30.1 9.4 %collective-permute-start.2 = (bf16[8,768]{1,0:T(8,128)(2,1)S(1)}, bf16[8,768]{1,0:T(8,128)(2,1)S(1)}, u32[]{:S(2)}, u32[]{:S(2)}) collective-permute-start(bf16[8,768]{1,0:T(8,128)(2,1)S(1)} %get-tuple-element.110.refs_0_.refs_1_), channel_id=1, source_target_pairs={{0,6},{1,7},{2,4},{3,5},{4,2},{5,3},{6,0},{7,1},{8,14},{9,15},{10,... | collective-permute-start | bytes 36872 | tf_op jit(solution)/shard_map/ppermute | solution.py:671
  60.7 17.6 %collective-permute-start.8 = (bf16[32,24,384]{2,1,0:T(8,128)(2,1)S(1)}, bf16[32,24,384]{2,1,0:T(8,128)(2,1)S(1)}, u32[]{:S(2)}, u32[]{:S(2)}) collective-permute-start(bf16[32,24,384]{2,1,0:T(8,128)(2,1)S(1)} %get-tuple-element.115.refs_0_), channel_id=1, source_target_pairs={{0,16},{8,24},{16,0},{24,8},{1,17},{9,25},{17,1},{25,9},{2,18},{10... | collective-permute-start | bytes 1769480 | tf_op jit(solution)/shard_map/ppermute | solution.py:654
  62.2 16.1 %collective-permute-start.9 = (bf16[32,24,384]{2,1,0:T(8,128)(2,1)S(1)}, bf16[32,24,384]{2,1,0:T(8,128)(2,1)S(1)}, u32[]{:S(2)}, u32[]{:S(2)}) collective-permute-start(bf16[32,24,384]{2,1,0:T(8,128)(2,1)S(1)} %get-tuple-element.116.refs_1_), channel_id=1, source_target_pairs={{0,1},{1,0},{2,3},{3,2},{4,5},{5,4},{6,7},{7,6},{8,9},{9,8},{10,11... | collective-permute-start | bytes 1769480 | tf_op jit(solution)/shard_map/ppermute | solution.py:654
  79.3 8.5 %collective-permute-start.10 = (bf16[16,24,384]{2,1,0:T(8,128)(2,1)S(1)}, bf16[16,24,384]{2,1,0:T(8,128)(2,1)S(1)}, u32[]{:S(2)}, u32[]{:S(2)}) collective-permute-start(bf16[16,24,384]{2,1,0:T(8,128)(2,1)S(1)} %get-tuple-element.124.refs_0_), channel_id=1, source_target_pairs={{0,1},{1,0},{2,3},{3,2},{4,5},{5,4},{6,7},{7,6},{8,9},{9,8},{10,11... | collective-permute-start | bytes 884744 | tf_op jit(solution)/shard_map/ppermute | solution.py:654
  80.8 8.2 %collective-permute-start.11 = (bf16[16,24,384]{2,1,0:T(8,128)(2,1)S(1)}, bf16[16,24,384]{2,1,0:T(8,128)(2,1)S(1)}, u32[]{:S(2)}, u32[]{:S(2)}) collective-permute-start(bf16[16,24,384]{2,1,0:T(8,128)(2,1)S(1)} %get-tuple-element.125.refs_1_), channel_id=1, source_target_pairs={{0,16},{8,24},{16,0},{24,8},{1,17},{9,25},{17,1},{25,9},{2,18},{10... | collective-permute-start | bytes 884744 | tf_op jit(solution)/shard_map/ppermute | solution.py:654
  85.6 14.3 %collective-permute-start.13 = (bf16[5,384,768]{2,1,0:T(8,128)(2,1)S(1)}, bf16[5,384,768]{2,1,0:T(8,128)(2,1)S(1)}, u32[]{:S(2)}, u32[]{:S(2)}) collective-permute-start(bf16[5,384,768]{2,1,0:T(8,128)(2,1)S(1)} %weight.8.refs_0_), channel_id=1, source_target_pairs={{0,8},{8,0},{16,24},{24,16},{1,9},{9,1},{17,25},{25,17},{2,10},{10... | collective-permute-start | bytes 8847368 | tf_op jit(solution)/shard_map/ppermute | solution.py:654
  89.6 7.6 %collective-permute-start.12 = (bf16[8,24,768]{2,1,0:T(8,128)(2,1)S(1)}, bf16[8,24,768]{2,1,0:T(8,128)(2,1)S(1)}, u32[]{:S(2)}, u32[]{:S(2)}) collective-permute-start(bf16[8,24,768]{2,1,0:T(8,128)(2,1)S(1)} %get-tuple-element.131.refs_1_), channel_id=1, source_target_pairs={{0,2},{1,3},{2,0},{3,1},{4,6},{5,7},{6,4},{7,5},{8,10},{9,11},{10,... | collective-permute-start | bytes 884744 | tf_op jit(solution)/shard_map/ppermute | solution.py:654
  97.9 21.5 %collective-permute-start.20 = (bf16[4,24,768]{2,1,0:T(8,128)(2,1)S(1)}, bf16[4,24,768]{2,1,0:T(8,128)(2,1)S(1)}, u32[]{:S(2)}, u32[]{:S(2)}) collective-permute-start(bf16[4,24,768]{2,1,0:T(8,128)(2,1)S(1)} %get-tuple-element.133.refs_0_), channel_id=1, source_target_pairs={{0,4},{1,5},{2,6},{3,7},{4,0},{5,1},{6,2},{7,3},{8,12},{9,13},{10,... | collective-permute-start | bytes 442376 | tf_op jit(solution)/shard_map/ppermute | solution.py:654
  100.8 14.4 %collective-permute-start.14 = (bf16[40,24,256]{2,1,0:T(8,128)(2,1)S(1)}, bf16[40,24,256]{2,1,0:T(8,128)(2,1)S(1)}, u32[]{:S(2)}, u32[]{:S(2)}) collective-permute-start(bf16[40,24,256]{2,1,0:T(8,128)(2,1)S(1)} %get-tuple-element.134.refs_1_), channel_id=1, source_target_pairs={{0,16},{8,24},{16,0},{24,8},{1,17},{9,25},{17,1},{25,9},{2,18},{10... | collective-permute-start | bytes 1474568 | tf_op jit(solution)/shard_map/ppermute | solution.py:654
  101.4 13.8 %collective-permute-start.15 = (bf16[40,24,256]{2,1,0:T(8,128)(2,1)S(1)}, bf16[40,24,256]{2,1,0:T(8,128)(2,1)S(1)}, u32[]{:S(2)}, u32[]{:S(2)}) collective-permute-start(bf16[40,24,256]{2,1,0:T(8,128)(2,1)S(1)} %get-tuple-element.135.refs_2_), channel_id=1, source_target_pairs={{0,1},{1,0},{2,3},{3,2},{4,5},{5,4},{6,7},{7,6},{8,9},{9,8},{10,11... | collective-permute-start | bytes 1474568 | tf_op jit(solution)/shard_map/ppermute | solution.py:654
  102.0 13.3 %collective-permute-start.16 = (bf16[40,24,256]{2,1,0:T(8,128)(2,1)S(1)}, bf16[40,24,256]{2,1,0:T(8,128)(2,1)S(1)}, u32[]{:S(2)}, u32[]{:S(2)}) collective-permute-start(bf16[40,24,256]{2,1,0:T(8,128)(2,1)S(1)} %get-tuple-element.136.refs_3_), channel_id=1, source_target_pairs={{0,2},{1,3},{2,0},{3,1},{4,6},{5,7},{6,4},{7,5},{8,10},{9,11},{10,... | collective-permute-start | bytes 1474568 | tf_op jit(solution)/shard_map/ppermute | solution.py:654
  115.2 9.0 %collective-permute-start.22 = (f32[12,768]{1,0:T(8,128)S(1)}, f32[12,768]{1,0:T(8,128)S(1)}, u32[]{:S(2)}, u32[]{:S(2)}) collective-permute-start(f32[12,768]{1,0:T(8,128)S(1)} %get-tuple-element.145.refs_0_.refs_5_), channel_id=1, source_target_pairs={{0,8},{8,0},{16,24},{24,16},{1,9},{9,1},{17,25},{25,17},{2,10},{10... | collective-permute-start | bytes 110600 | tf_op jit(solution)/shard_map/ppermute | solution.py:654
  116.0 8.4 %collective-permute-start.17 = (bf16[20,24,256]{2,1,0:T(8,128)(2,1)S(1)}, bf16[20,24,256]{2,1,0:T(8,128)(2,1)S(1)}, u32[]{:S(2)}, u32[]{:S(2)}) collective-permute-start(bf16[20,24,256]{2,1,0:T(8,128)(2,1)S(1)} %get-tuple-element.149.refs_0_), channel_id=1, source_target_pairs={{0,1},{1,0},{2,3},{3,2},{4,5},{5,4},{6,7},{7,6},{8,9},{9,8},{10,11... | collective-permute-start | bytes 737288 | tf_op jit(solution)/shard_map/ppermute | solution.py:654
  117.6 8.1 %collective-permute-start.18 = (bf16[20,24,256]{2,1,0:T(8,128)(2,1)S(1)}, bf16[20,24,256]{2,1,0:T(8,128)(2,1)S(1)}, u32[]{:S(2)}, u32[]{:S(2)}) collective-permute-start(bf16[20,24,256]{2,1,0:T(8,128)(2,1)S(1)} %get-tuple-element.150.refs_1_), channel_id=1, source_target_pairs={{0,2},{1,3},{2,0},{3,1},{4,6},{5,7},{6,4},{7,5},{8,10},{9,11},{10,... | collective-permute-start | bytes 737288 | tf_op jit(solution)/shard_map/ppermute | solution.py:654
  117.8 7.8 %collective-permute-start.19 = (bf16[20,24,256]{2,1,0:T(8,128)(2,1)S(1)}, bf16[20,24,256]{2,1,0:T(8,128)(2,1)S(1)}, u32[]{:S(2)}, u32[]{:S(2)}) collective-permute-start(bf16[20,24,256]{2,1,0:T(8,128)(2,1)S(1)} %get-tuple-element.151.refs_2_), channel_id=1, source_target_pairs={{0,16},{8,24},{16,0},{24,8},{1,17},{9,25},{17,1},{25,9},{2,18},{10... | collective-permute-start | bytes 737288 | tf_op jit(solution)/shard_map/ppermute | solution.py:654
  126.4 10.3 %collective-permute-start.28 = (bf16[24,24,256]{2,1,0:T(8,128)(2,1)S(1)}, bf16[24,24,256]{2,1,0:T(8,128)(2,1)S(1)}, u32[]{:S(2)}, u32[]{:S(2)}) collective-permute-start(bf16[24,24,256]{2,1,0:T(8,128)(2,1)S(1)} %get-tuple-element.154.refs_1_), channel_id=1, source_target_pairs={{0,1},{1,0},{2,3},{3,2},{4,5},{5,4},{6,7},{7,6},{8,9},{9,8},{10,11... | collective-permute-start | bytes 884744 | tf_op jit(solution)/shard_map/ppermute | solution.py:654
  127.6 9.9 %collective-permute-start.29 = (bf16[24,24,256]{2,1,0:T(8,128)(2,1)S(1)}, bf16[24,24,256]{2,1,0:T(8,128)(2,1)S(1)}, u32[]{:S(2)}, u32[]{:S(2)}) collective-permute-start(bf16[24,24,256]{2,1,0:T(8,128)(2,1)S(1)} %get-tuple-element.155.refs_2_), channel_id=1, source_target_pairs={{0,2},{1,3},{2,0},{3,1},{4,6},{5,7},{6,4},{7,5},{8,10},{9,11},{10,... | collective-permute-start | bytes 884744 | tf_op jit(solution)/shard_map/ppermute | solution.py:654
  128.8 9.0 %collective-permute-start.27 = (bf16[26,24,256]{2,1,0:T(8,128)(2,1)S(1)}, bf16[26,24,256]{2,1,0:T(8,128)(2,1)S(1)}, u32[]{:S(2)}, u32[]{:S(2)}) collective-permute-start(bf16[26,24,256]{2,1,0:T(8,128)(2,1)S(1)} %get-tuple-element.153.refs_0_), channel_id=1, source_target_pairs={{0,16},{8,24},{16,0},{24,8},{1,17},{9,25},{17,1},{25,9},{2,18},{10... | collective-permute-start | bytes 958472 | tf_op jit(solution)/shard_map/ppermute | solution.py:654
  135.2 6.3 %collective-permute-start.23 = (bf16[10,24,256]{2,1,0:T(8,128)(2,1)S(1)}, bf16[10,24,256]{2,1,0:T(8,128)(2,1)S(1)}, u32[]{:S(2)}, u32[]{:S(2)}) collective-permute-start(bf16[10,24,256]{2,1,0:T(8,128)(2,1)S(1)} %get-tuple-element.162), channel_id=1, source_target_pairs={{0,2},{1,3},{2,0},{3,1},{4,6},{5,7},{6,4},{7,5},{8,10},{9,11},{10,... | collective-permute-start | bytes 368648 | tf_op jit(solution)/shard_map/ppermute | solution.py:654
  135.6 6.7 %collective-permute-start.24 = (bf16[10,24,256]{2,1,0:T(8,128)(2,1)S(1)}, bf16[10,24,256]{2,1,0:T(8,128)(2,1)S(1)}, u32[]{:S(2)}, u32[]{:S(2)}) collective-permute-start(bf16[10,24,256]{2,1,0:T(8,128)(2,1)S(1)} %get-tuple-element.164), channel_id=1, source_target_pairs={{0,16},{8,24},{16,0},{24,8},{1,17},{9,25},{17,1},{25,9},{2,18},{10... | collective-permute-start | bytes 368648 | tf_op jit(solution)/shard_map/ppermute | solution.py:654
  138.4 6.0 %collective-permute-start.31 = (bf16[12,24,256]{2,1,0:T(8,128)(2,1)S(1)}, bf16[12,24,256]{2,1,0:T(8,128)(2,1)S(1)}, u32[]{:S(2)}, u32[]{:S(2)}) collective-permute-start(bf16[12,24,256]{2,1,0:T(8,128)(2,1)S(1)} %get-tuple-element.175), channel_id=1, source_target_pairs={{0,2},{1,3},{2,0},{3,1},{4,6},{5,7},{6,4},{7,5},{8,10},{9,11},{10,... | collective-permute-start | bytes 442376 | tf_op jit(solution)/shard_map/ppermute | solution.py:654
  142.9 8.5 %collective-permute-start.26 = (bf16[5,24,768]{2,1,0:T(8,128)(2,1)S(1)}, bf16[5,24,768]{2,1,0:T(8,128)(2,1)S(1)}, u32[]{:S(2)}, u32[]{:S(2)}) collective-permute-start(bf16[5,24,768]{2,1,0:T(8,128)(2,1)S(1)} %get-tuple-element.167.refs_0_), channel_id=1, source_target_pairs={{0,4},{1,5},{2,6},{3,7},{4,0},{5,1},{6,2},{7,3},{8,12},{9,13},{10,... | collective-permute-start | bytes 552968 | tf_op jit(solution)/shard_map/ppermute | solution.py:654
  153.9 7.7 %collective-permute-start.36 = (bf16[4,24,768]{2,1,0:T(8,128)(2,1)S(1)}, bf16[4,24,768]{2,1,0:T(8,128)(2,1)S(1)}, u32[]{:S(2)}, u32[]{:S(2)}) collective-permute-start(bf16[4,24,768]{2,1,0:T(8,128)(2,1)S(1)} %get-tuple-element.186.refs_1_), channel_id=1, source_target_pairs={{0,4},{1,5},{2,6},{3,7},{4,0},{5,1},{6,2},{7,3},{8,12},{9,13},{10,... | collective-permute-start | bytes 442376 | tf_op jit(solution)/shard_map/ppermute | solution.py:654
  162.6 9.3 %collective-permute-start.40 = (bf16[72,384]{1,0:T(8,128)(2,1)S(1)}, bf16[72,384]{1,0:T(8,128)(2,1)S(1)}, u32[]{:S(2)}, u32[]{:S(2)}) collective-permute-start(bf16[72,384]{1,0:T(8,128)(2,1)S(1)} %get-tuple-element.195), channel_id=1, source_target_pairs={{0,4},{1,5},{2,6},{3,7},{4,0},{5,1},{6,2},{7,3},{8,12},{9,13},{10,... | collective-permute-start | bytes 165896 | tf_op jit(solution)/shard_map/ppermute | solution.py:887
  164.2 7.7 %collective-permute-start.41 = (bf16[72,384]{1,0:T(8,128)(2,1)S(1)}, bf16[72,384]{1,0:T(8,128)(2,1)S(1)}, u32[]{:S(2)}, u32[]{:S(2)}) collective-permute-start(bf16[72,384]{1,0:T(8,128)(2,1)S(1)} %get-tuple-element.196), channel_id=1, source_target_pairs={{0,5},{1,4},{2,7},{3,6},{4,1},{5,0},{6,3},{7,2},{8,13},{9,12},{10,... | collective-permute-start | bytes 165896 | tf_op jit(solution)/shard_map/ppermute | solution.py:887
  166.6 7.2 %collective-permute-start.42 = (bf16[72,384]{1,0:T(8,128)(2,1)S(1)}, bf16[72,384]{1,0:T(8,128)(2,1)S(1)}, u32[]{:S(2)}, u32[]{:S(2)}) collective-permute-start(bf16[72,384]{1,0:T(8,128)(2,1)S(1)} %get-tuple-element.197), channel_id=1, source_target_pairs={{0,6},{1,7},{2,4},{3,5},{4,2},{5,3},{6,0},{7,1},{8,14},{9,15},{10,... | collective-permute-start | bytes 165896 | tf_op jit(solution)/shard_map/ppermute | solution.py:887
  168.1 7.0 %collective-permute-start.43 = (bf16[72,384]{1,0:T(8,128)(2,1)S(1)}, bf16[72,384]{1,0:T(8,128)(2,1)S(1)}, u32[]{:S(2)}, u32[]{:S(2)}) collective-permute-start(bf16[72,384]{1,0:T(8,128)(2,1)S(1)} %get-tuple-element.198), channel_id=1, source_target_pairs={{0,7},{1,6},{2,5},{3,4},{4,3},{5,2},{6,1},{7,0},{8,15},{9,14},{10,... | collective-permute-start | bytes 165896 | tf_op jit(solution)/shard_map/ppermute | solution.py:887
  170.3 6.1 %collective-permute-start.37 = (bf16[72,384]{1,0:T(8,128)(2,1)S(1)}, bf16[72,384]{1,0:T(8,128)(2,1)S(1)}, u32[]{:S(2)}, u32[]{:S(2)}) collective-permute-start(bf16[72,384]{1,0:T(8,128)(2,1)S(1)} %get-tuple-element.192), channel_id=1, source_target_pairs={{0,1},{1,0},{2,3},{3,2},{4,5},{5,4},{6,7},{7,6},{8,9},{9,8},{10,11... | collective-permute-start | bytes 165896 | tf_op jit(solution)/shard_map/ppermute | solution.py:887
  175.1 6.0 %collective-permute-start.45 = (bf16[4,72,384]{2,1,0:T(8,128)(2,1)S(1)}, bf16[4,72,384]{2,1,0:T(8,128)(2,1)S(1)}, u32[]{:S(2)}, u32[]{:S(2)}) collective-permute-start(bf16[4,72,384]{2,1,0:T(8,128)(2,1)S(1)} %merge.5.refs_1_), channel_id=1, source_target_pairs={{0,16},{8,24},{16,0},{24,8},{1,17},{9,25},{17,1},{25,9},{2,18},{10... | collective-permute-start | bytes 663560 | tf_op jit(solution)/shard_map/ppermute | solution.py:654
  177.0 6.5 %collective-permute-start.44 = (bf16[4,72,384]{2,1,0:T(8,128)(2,1)S(1)}, bf16[4,72,384]{2,1,0:T(8,128)(2,1)S(1)}, u32[]{:S(2)}, u32[]{:S(2)}) collective-permute-start(bf16[4,72,384]{2,1,0:T(8,128)(2,1)S(1)} %merge.4.refs_0_), channel_id=1, source_target_pairs={{0,16},{8,24},{16,0},{24,8},{1,17},{9,25},{17,1},{25,9},{2,18},{10... | collective-permute-start | bytes 663560 | tf_op jit(solution)/shard_map/ppermute | solution.py:654
  177.6 6.5 %collective-permute-start.47 = (bf16[4,72,384]{2,1,0:T(8,128)(2,1)S(1)}, bf16[4,72,384]{2,1,0:T(8,128)(2,1)S(1)}, u32[]{:S(2)}, u32[]{:S(2)}) collective-permute-start(bf16[4,72,384]{2,1,0:T(8,128)(2,1)S(1)} %merge.5.refs_1_), channel_id=1, source_target_pairs={{0,8},{8,0},{16,24},{24,16},{1,9},{9,1},{17,25},{25,17},{2,10},{10... | collective-permute-start | bytes 663560 | tf_op jit(solution)/shard_map/ppermute | solution.py:654
  177.6 6.5 %collective-permute-start.46 = (bf16[4,72,384]{2,1,0:T(8,128)(2,1)S(1)}, bf16[4,72,384]{2,1,0:T(8,128)(2,1)S(1)}, u32[]{:S(2)}, u32[]{:S(2)}) collective-permute-start(bf16[4,72,384]{2,1,0:T(8,128)(2,1)S(1)} %merge.4.refs_0_), channel_id=1, source_target_pairs={{0,8},{8,0},{16,24},{24,16},{1,9},{9,1},{17,25},{25,17},{2,10},{10... | collective-permute-start | bytes 663560 | tf_op jit(solution)/shard_map/ppermute | solution.py:654
  (45 other events, 212.6 us)
